TPU v7x, 32 devices: a whole 2x2x4 slice. The times are simulated.
32 devices in a mesh: dp: 4 (over x, core), fsdp: 8 (over z, y).
Axes of the slice: x: 2, y: 2, z: 4, core: 2. Of those that a mesh axis runs over, the one named last changes fastest.
Arguments:
- block_input: bfloat16 [16384, 1024], P(('dp', 'fsdp')), may hold values from -6 to 6
- in_weight: float32 [1024, 3072], P(('dp', 'fsdp')), may hold values from -0.1875 to 0.1875
- out_weight: float32 [1024, 1024], P(('dp', 'fsdp')), may hold values from -0.1875 to 0.1875
- gate_weight: float32 [1024, 4608], P(('dp', 'fsdp')), may hold values from -0.1875 to 0.1875
- up_weight: float32 [1024, 4608], P(('dp', 'fsdp')), may hold values from -0.1875 to 0.1875
- down_weight: float32 [4608, 1024], P(('dp', 'fsdp')), may hold values from -0.09375 to 0.09375
- norm_gain: float32 [1024], P(('dp', 'fsdp')), may hold values from 0.5 to 1.5
- ffn_gain: float32 [1024], P(('dp', 'fsdp')), may hold values from 0.5 to 1.5
- conv_weight: float32 [1024, 3], P(('dp', 'fsdp')), may hold values from -3 to 3
- seq_starts: int32 [4, 4], P('dp'), may hold values from 0 to 3072, as said below
- cotangent: bfloat16 [16384, 1024], P(('dp', 'fsdp')), may hold values from -6 to 6
Outputs:
- block_output: bfloat16 [16384, 1024], P(('dp', 'fsdp'))
- grad_input: bfloat16 [16384, 1024], P(('dp', 'fsdp'))
- grad_in_weight: float32 [1024, 3072], P(('dp', 'fsdp'))
- grad_out_weight: float32 [1024, 1024], P(('dp', 'fsdp'))
- grad_gate_weight: float32 [1024, 4608], P(('dp', 'fsdp'))
- grad_up_weight: float32 [1024, 4608], P(('dp', 'fsdp'))
- grad_down_weight: float32 [4608, 1024], P(('dp', 'fsdp'))
- grad_norm_gain: float32 [1024], P(('dp', 'fsdp'))
- grad_ffn_gain: float32 [1024], P(('dp', 'fsdp'))
- grad_conv_weight: float32 [1024, 3], P(('dp', 'fsdp'))
Inputs may be any that keep to these rules, and one draw needn't show every extreme that they name: `seq_starts`: row g holds the offsets within group g of the sequences packed there, in rising order, each sequence 1024, 2048 or 4096 tokens long, the first at 0; a row with fewer than 4 sequences repeats its last start. Some row holds four sequences.
All inputs are finite; a program needn't handle non-finite values.
Results may differ from a plain program's by a relative error of at most 0.012.
The roundings to bfloat16 on the way count: a program that leaves them out, or rounds other values in their place, can miss the bound.
Values may be sent and summed in bfloat16 or wider, within the bound.
No kernel may reach another device: no remote copies, remote signals or barrier semaphores. Data moves between devices by JAX's collectives and lax.ppermute only.
A program may use at most 320 MiB of HBM per device.

v0:
```python
import functools
import itertools
import math

import jax
import jax.numpy as jnp
from jax import lax
from jax.experimental import pallas as pl
from jax.experimental.pallas import tpu as pltpu
from jax.sharding import Mesh
from jax.sharding import PartitionSpec as P

EPS = 1e-05
AXES = ("far", "x", "core", "z", "y")
SPREAD = ("far", "z", "y")
BF = jnp.bfloat16
F32 = jnp.float32


class Axis:
    def __init__(self, name):
        self.name, self.size = name, lax.axis_size(name)
        self.here = lax.axis_index(name)
        near = sorted(range(1, self.size), key=lambda by: (min(by, self.size - by), by))
        self.steps = tuple(near)

    def shift(self, value, by=1):
        return lax.ppermute(value, self.name, [(i, (i + by) % self.size) for i in range(self.size)])

    def at(self, by):
        return lax.rem(self.here + by, self.size)


def passed_along(shard, by):
    peers = lax.axis_size(("z", "y"))
    pairs = [(i, i + by) for i in range(peers) if 0 <= i + by < peers]
    return lax.ppermute(shard, ("z", "y"), pairs)


def fence(*values):
    return lax.optimization_barrier(values)


def contract_rows(left, right):
    return lax.dot_general(
        left, right, (((0,), (0,)), ((), ())), preferred_element_type=F32
    )


def contract_cols(left, right):
    return lax.dot_general(
        left, right, (((1,), (1,)), ((), ())), preferred_element_type=F32
    )


def times(left, right):
    return jnp.dot(left, right, preferred_element_type=F32)


def pick(value, at, dim):
    return lax.dynamic_index_in_dim(value, at, dim, keepdims=False)


def ordered(mine, other, here, dim):
    low = jnp.where(here == 0, mine, other)
    high = jnp.where(here == 0, other, mine)
    return jnp.stack([low, high], dim)


def cut(value, axis, dim):
    return pick(value, axis.here, dim), [pick(value, axis.at(by), dim) for by in axis.steps]


def shifted(parts, axis):
    return [axis.shift(part, by) for part, by in zip(parts, axis.steps, strict=True)]


def summed(own, others):
    total = own.astype(F32)
    for other in others:
        total = total + other.astype(F32)
    return total


def place_body(moves, here_ref, *refs):
    sems = refs[-1]
    copies = []
    for i, (source, target) in enumerate(moves(here_ref, refs[:-1])):
        copy = pltpu.make_async_copy(source, target, sems.at[i])
        copy.start()
        copies.append(copy)
    for copy in copies:
        copy.wait()


def out_array(shape, kind):
    return pltpu.HBM(shape, kind) if math.prod(shape) >= 2**18 else jax.ShapeDtypeStruct(shape, kind)


def pinned(*arrays):
    return [
        pltpu.with_memory_space_constraint(a, pltpu.HBM) if a.size >= 2**18 else a for a in arrays
    ]


def kept(array):
    return pltpu.with_memory_space_constraint(array, pltpu.VMEM)


def place(moves, count, here, sources, shapes):
    return pl.pallas_call(
        functools.partial(place_body, moves),
        out_shape=[pltpu.VMEM(shape, BF) for shape in shapes],
        in_specs=[pl.BlockSpec(memory_space=pltpu.SMEM)]
        + [pl.BlockSpec(memory_space=pl.ANY)] * len(sources),
        out_specs=[pl.BlockSpec(memory_space=pltpu.VMEM)] * len(shapes),
        scratch_shapes=[pltpu.SemaphoreType.DMA((count,))],
        compiler_params=params(20),
        cost_estimate=pl.CostEstimate(flops=0, bytes_accessed=2**20, transcendentals=0),
    )(here, *pinned(*sources))


def back(at, by, size):
    return lax.rem(at + size - by, size)


def place_mix(pieces, here, ax, ay, az, columns, width):
    nx, ny, nz = ax.size, ay.size, az.size
    rows, half = pieces[0][3].shape[-2], width // 2

    def moves(at, refs):
        wide, small, narrow = refs[-3:]
        for (dx, dy, backs, _), source in zip(pieces, refs[:-3], strict=True):
            x, y = back(at[0], dx, nx), back(at[1], dy, ny)
            for n, dz in enumerate(backs):
                z = back(at[2], dz, nz)
                block = source.at[n]
                yield block.at[:, :, pl.ds(0, columns)], wide.at[x, :, z, y]
                yield block.at[:, :, pl.ds(columns, 128)], small.at[x, :, z, y]
                for k in range(2):
                    yield (
                        block.at[k, :, pl.ds(columns + 128, half)],
                        narrow.at[x, z, y, :, pl.ds(k * half, half)],
                    )

    lead = (nx, 2, nz, ny, rows)
    shapes = [lead + (columns,), lead + (128,), (nx, nz, ny, rows, width)]
    arrays = [piece[3] for piece in pieces]
    wide, small, narrow = place(moves, 4 * nx * ny * nz, here, arrays, shapes)
    return wide.reshape(-1, columns), small.reshape(-1, 128), narrow.reshape(-1, width)


def cost():
    return pl.CostEstimate(flops=0, bytes_accessed=2**16, transcendentals=0)


def params(mib):
    return pltpu.CompilerParams(vmem_limit_bytes=mib * 1024 * 1024)


def whole(array):
    return pl.BlockSpec(
        array.shape, lambda i: (0,) * array.ndim, pipeline_mode=pl.Buffered(1)
    )


def tiles(rows, columns):
    return pl.BlockSpec((rows, columns), lambda i: (i, 0))


def chunks(columns):
    step = 384 if columns % 384 == 0 else 128 if columns % 128 == 0 else columns
    return [(a, step) for a in range(0, columns, step)]


def logistic(v):
    return 0.5 * jnp.tanh(0.5 * v) + 0.5


def piece_specs(pieces, tile):
    specs = []
    for p, piece in enumerate(pieces):
        first, last = p * piece.shape[0] // tile, (p + 1) * piece.shape[0] // tile - 1

        def at(i, first=first, last=last):
            return jnp.clip(i - first, 0, last - first), 0

        specs.append(pl.BlockSpec((tile, piece.shape[1]), at))
    return specs


def piece_tile(refs):
    steps = pl.num_programs(0) // len(refs)
    value = refs[0][...]
    for p, ref in enumerate(refs[1:], 1):
        value = jnp.where(pl.program_id(0) >= p * steps, ref[...], value)
    return value


def forward_body(count, *refs):
    w_ref, ev_ref, s_ref = refs[count:]
    hidden = s_ref.shape[1]
    x = piece_tile(refs[:count])
    for a, n in chunks(hidden):
        gate = times(x, w_ref[:, a : a + n])
        rise = times(x, w_ref[:, hidden + a : hidden + a + n])
        ev_ref[:, a : a + n] = gate.astype(BF)
        ev_ref[:, hidden + a : hidden + a + n] = rise.astype(BF)
        s_ref[:, a : a + n] = (gate * logistic(gate) * rise).astype(BF)


def ffn_forward(pieces, w, tile):
    count, both = sum(piece.shape[0] for piece in pieces), w.shape[1]
    return pl.pallas_call(
        functools.partial(forward_body, len(pieces)),
        grid=(count // tile,),
        in_specs=piece_specs(pieces, tile) + [whole(w)],
        out_specs=[tiles(tile, both), tiles(tile, both // 2)],
        out_shape=[out_array((count, both), BF), out_array((count, both // 2), BF)],
        compiler_params=params(24),
        cost_estimate=cost(),
    )(*pinned(*pieces, w))


def back_body(count, half, *refs):
    ev_ref, down_ref, w_ref, dev_ref, keep_ref, *sends = refs[count:]
    hidden = down_ref.shape[0]
    dy = piece_tile(refs[:count])
    for a, n in chunks(hidden):
        back = contract_cols(dy, down_ref[a : a + n, :])
        gate = ev_ref[:, a : a + n].astype(F32)
        rise = ev_ref[:, hidden + a : hidden + a + n].astype(F32)
        sigma = logistic(gate)
        back = back * sigma
        dev_ref[:, a : a + n] = (back * rise * (1.0 + gate * (1.0 - sigma))).astype(BF)
        dev_ref[:, hidden + a : hidden + a + n] = (back * gate).astype(BF)
    split_pieces(half, contract_cols(dev_ref[...], w_ref[...]), keep_ref, sends)


def split_rows(half, value, keep_ref, send_ref):
    @pl.when(pl.program_id(0) < half)
    def _():
        keep_ref[...] = value

    @pl.when(pl.program_id(0) >= half)
    def _():
        send_ref[...] = value.astype(send_ref.dtype)


def split_specs(tile, columns, half):
    return [
        pl.BlockSpec((tile, columns), lambda i: (jnp.minimum(i, half - 1), 0)),
        pl.BlockSpec((tile, columns), lambda i: (jnp.maximum(i - half, 0), 0)),
    ]


def split_pieces(half, value, keep_ref, sends):
    cuts = len(sends) // half
    size = value.shape[0] // cuts

    @pl.when(pl.program_id(0) < half)
    def _():
        keep_ref[...] = value

    for n, ref in enumerate(sends):

        @pl.when(pl.program_id(0) == half + n // cuts)
        def _(n=n, ref=ref):
            at = n % cuts * size
            ref[...] = value[at : at + size].astype(ref.dtype)


def piece_outputs(count, width, tile, cuts):
    half, size = count // (2 * tile), tile // cuts
    specs = split_specs(tile, width, half)[:1]
    specs += [pl.BlockSpec((size, width), lambda i: (0, 0))] * (half * cuts)
    shapes = [out_array((count // 2, width), F32)]
    return specs, shapes + [out_array((size, width), BF)] * (half * cuts)


def ffn_back(pieces, ev, down, w, tile):
    count, both = ev.shape
    width, half = down.shape[1], count // (2 * tile)
    specs, shapes = piece_outputs(count, width, tile, 1)
    out = pl.pallas_call(
        functools.partial(back_body, len(pieces), half),
        grid=(2 * half,),
        in_specs=piece_specs(pieces, tile) + [tiles(tile, both), whole(down), whole(w)],
        out_specs=[tiles(tile, both)] + specs,
        out_shape=[pltpu.VMEM((count, both), BF)] + shapes,
        compiler_params=params(32),
        cost_estimate=cost(),
    )(*pinned(*pieces, ev, down, w))
    return out[0], out[1], out[2:]


def rows_body(function, half, left_ref, weight_ref, keep_ref, *sends):
    split_pieces(half, function(left_ref[...], weight_ref[...]), keep_ref, sends)


def row_halves(function, left, weight, width, tile):
    count = left.shape[0]
    half = count // (2 * tile)
    specs, shapes = piece_outputs(count, width, tile, 2)
    out = pl.pallas_call(
        functools.partial(rows_body, function, half),
        grid=(2 * half,),
        in_specs=[tiles(tile, left.shape[1]), whole(weight)],
        out_specs=specs,
        out_shape=shapes,
        compiler_params=params(20),
        cost_estimate=cost(),
    )(*pinned(left, weight))
    return out[0], out[1:]


def input_grad_body(half, dp_ref, win_ref, x_ref, keep_ref, *refs):
    sends, gain_ref = refs[:-1], refs[-1]
    value = contract_cols(dp_ref[...], win_ref[...])
    split_pieces(half, value, keep_ref, sends)
    x = x_ref[...].astype(F32)
    scale = lax.rsqrt(jnp.mean(x * x, axis=1, keepdims=True) + EPS)

    @pl.when(pl.program_id(0) == 0)
    def _():
        gain_ref[...] = jnp.zeros_like(gain_ref)

    gain_ref[...] += jnp.sum(value * (x * scale), axis=0, keepdims=True)


def input_grad(dp, win, x, tile):
    count, width = x.shape
    half = count // (2 * tile)
    specs, shapes = piece_outputs(count, width, tile, 2)
    out = pl.pallas_call(
        functools.partial(input_grad_body, half),
        grid=(2 * half,),
        in_specs=[tiles(tile, dp.shape[1]), whole(win), tiles(tile, width)],
        out_specs=specs + [pl.BlockSpec((1, width), lambda i: (0, 0))],
        out_shape=shapes + [jax.ShapeDtypeStruct((1, width), F32)],
        compiler_params=params(24),
        cost_estimate=cost(),
    )(*pinned(dp, win, x))
    return out[0], out[1:-1], out[-1][0]


def grad_body(lefts, rights, *refs):
    rest = refs[len(lefts) + len(rights) :]
    total = None
    for i, (first, end) in enumerate(lefts):
        for j, (start, stop) in enumerate(rights):
            low, high = max(first, start), min(end, stop)
            if low < high:
                left = refs[i][low - first : high - first, :]
                right = refs[len(lefts) + j][low - start : high - start, :]
                term = contract_rows(left, right)
                total = term if total is None else total + term
    for ref in rest[:-1]:
        total = total + ref[...]
    rest[-1][...] = total.astype(rest[-1].dtype).reshape(rest[-1].shape)


def token_spans(pieces):
    ends = list(itertools.accumulate(piece.shape[0] for piece in pieces))
    return list(zip([0] + ends[:-1], ends, strict=True))


def weight_grad(lefts, rights, tile, out_spec, shape, kind=BF, extra=(), stay=False):
    rows = lefts[0].shape[1]
    return pl.pallas_call(
        functools.partial(grad_body, token_spans(lefts), token_spans(rights)),
        grid=(rows // tile,),
        in_specs=[pl.BlockSpec((left.shape[0], tile), lambda i: (0, i)) for left in lefts]
        + [whole(right) for right in rights]
        + [out_spec] * len(extra),
        out_specs=out_spec,
        out_shape=out_array(shape, kind),
        compiler_params=params(34),
        cost_estimate=cost(),
    )(*pinned(*lefts), *(kept(right) if stay else pinned(right)[0] for right in rights), *pinned(*extra))


def gate_up_grad(lefts, rights, far, nz, rows):
    columns, width = rights[0].shape[1], lefts[0].shape[1]
    tile = 2 * nz * rows
    if tile % 128 == 0 and rows % 16 == 0:
        block = (1, 2 * nz, 1, rows, columns)
        spec = pl.BlockSpec(block, lambda i: (i // 4, 0, i % 4, 0, 0))
        out = weight_grad(lefts, rights, tile, spec, (far, 2 * nz, 4, rows, columns), stay=True)
    else:
        out = weight_grad(lefts, rights, 256, tiles(256, columns), (width, columns), stay=True)
        out = out.reshape(far, 4, 2 * nz, rows, columns).transpose(0, 2, 1, 3, 4)
    return out.reshape(width, columns)


def mixer_body(
    per_group, x_ref, gain_ref, win_ref, halo_ref, masks_ref, taps_ref, wout_ref, *refs
):
    normed_ref, projected_ref, mixed_ref, gated_ref, keep_ref, send_ref, rows, carry = refs
    count, feats = mixed_ref.shape
    x = x_ref[...].astype(F32)
    scale = lax.rsqrt(jnp.mean(x * x, axis=1, keepdims=True) + EPS)
    normed = (x * scale * gain_ref[...]).astype(BF)
    normed_ref[...] = normed
    projected = times(normed, win_ref[...])
    projected_ref[...] = projected
    product = projected[:, :feats] * projected[:, 2 * feats :]
    opens = lax.rem(pl.program_id(0), per_group) == 0
    rows[6:8, :] = jnp.where(opens, halo_ref[0], carry[...])
    rows[8 : 8 + count, :] = product
    mixed = taps_ref[2:3, :] * product
    mixed = mixed + masks_ref[:, 0:1] * (taps_ref[1:2, :] * rows[7 : 7 + count, :])
    mixed = mixed + masks_ref[:, 1:2] * (taps_ref[0:1, :] * rows[6 : 6 + count, :])
    carry[...] = product[count - 2 :]
    mixed_ref[...] = mixed
    gated = (projected[:, feats : 2 * feats] * mixed).astype(BF)
    gated_ref[...] = gated
    half = pl.num_programs(0) // 2
    split_rows(half, times(gated, wout_ref[...]), keep_ref, send_ref)


def mixer_forward(x, gain, win, halo, masks, taps, wout, tile):
    count, width = x.shape
    wide, feats = win.shape[1], wout.shape[0]
    per_group = count // (2 * tile)
    row = pl.BlockSpec((1, width), lambda i: (0, 0))
    return pl.pallas_call(
        functools.partial(mixer_body, per_group),
        grid=(2 * per_group,),
        in_specs=[
            tiles(tile, width),
            row,
            whole(win),
            pl.BlockSpec((1, 2, feats), lambda i: (i // per_group, 0, 0)),
            tiles(tile, masks.shape[1]),
            whole(taps),
            whole(wout),
        ],
        out_specs=[tiles(tile, width), tiles(tile, wide), tiles(tile, feats), tiles(tile, feats)]
        + split_specs(tile, width, per_group),
        out_shape=[
            out_array((count, width), BF),
            out_array((count, wide), F32),
            out_array((count, feats), F32),
            out_array((count, feats), BF),
        ]
        + [out_array((count // 2, width), kind) for kind in (F32, BF)],
        scratch_shapes=[pltpu.VMEM((tile + 8, feats), F32), pltpu.VMEM((2, feats), F32)],
        compiler_params=params(28),
        cost_estimate=cost(),
    )(*pinned(x, gain[None]), kept(win), *pinned(halo, masks, taps), kept(wout))


def mixer_back_body(
    per_group, dh_ref, dh2_ref, wout_ref, projected_ref, mixed_ref, halo_ref, masks_ref, *refs
):
    taps_ref, *refs = refs
    out_ref, grad_ref, rows, carry = refs
    count, feats = mixed_ref.shape
    projected = projected_ref[...]
    dh = jnp.where(pl.program_id(0) < per_group, dh_ref[...], dh2_ref[...])
    back = contract_cols(dh, wout_ref[...])
    grad_c = back * mixed_ref[...]
    grad_mixed = back * projected[:, feats : 2 * feats]
    closes = lax.rem(pl.program_id(0), per_group) == 0
    rows[0:count, :] = grad_mixed
    rows[count : count + 2, :] = jnp.where(closes, halo_ref[0], carry[...])
    carry[...] = grad_mixed[:2]
    ahead = (
        grad_mixed,
        masks_ref[:, 2:3] * rows[1 : 1 + count, :],
        masks_ref[:, 3:4] * rows[2 : 2 + count, :],
    )
    grad_product = sum(taps_ref[2 - lag : 3 - lag, :] * ahead[lag] for lag in range(3))
    b_branch, x_branch = projected[:, :feats], projected[:, 2 * feats :]
    out_ref[:, :feats] = (grad_product * x_branch).astype(BF)
    out_ref[:, feats : 2 * feats] = grad_c.astype(BF)
    out_ref[:, 2 * feats :] = (grad_product * b_branch).astype(BF)

    @pl.when(pl.program_id(0) == 0)
    def _():
        grad_ref[...] = jnp.zeros_like(grad_ref)

    product = b_branch * x_branch
    for lag in range(3):
        grad_ref[2 - lag : 3 - lag, :] += jnp.sum(product * ahead[lag], axis=0, keepdims=True)


def mixer_back(dh, wout, projected, mixed, halo, masks, taps, tile):
    count, wide = projected.shape
    width, feats = dh[0].shape[1], wout.shape[0]
    per_group = count // (2 * tile)

    def at(i):
        return (i // per_group) * per_group + per_group - 1 - lax.rem(i, per_group)

    def turned(columns):
        return pl.BlockSpec((tile, columns), lambda i: (at(i), 0))

    return pl.pallas_call(
        functools.partial(mixer_back_body, per_group),
        grid=(2 * per_group,),
        in_specs=[
            pl.BlockSpec((tile, width), lambda i: (jnp.maximum(per_group - 1 - i, 0), 0)),
            pl.BlockSpec(
                (tile, width), lambda i: (jnp.minimum(2 * per_group - 1 - i, per_group - 1), 0)
            ),
            whole(wout),
            turned(wide),
            turned(feats),
            pl.BlockSpec((1, 2, feats), lambda i: (i // per_group, 0, 0)),
            turned(masks.shape[1]),
            whole(taps),
        ],
        out_specs=[turned(wide), pl.BlockSpec((8, feats), lambda i: (0, 0))],
        out_shape=[
            out_array((count, wide), BF),
            out_array((8, feats), F32),
        ],
        scratch_shapes=[pltpu.VMEM((tile + 8, feats), F32), pltpu.VMEM((2, feats), F32)],
        compiler_params=params(24),
        cost_estimate=cost(),
    )(*pinned(*dh, wout, projected, mixed, halo, masks, taps))


def mixer_grads_body(per_group, lower, here_ref, normed_ref, gated_ref, *refs):
    ins, out_ref, grad_ref = refs[:8], refs[8], refs[9]
    blocks, (rows, carry, in_sum, out_sum) = refs[10:18], refs[18:]
    mixer_back_body(per_group, *ins, out_ref, grad_ref, rows, carry)
    width, wide = in_sum.shape
    tile = width // 4

    @pl.when(pl.program_id(0) == 0)
    def _():
        in_sum[...] = jnp.zeros_like(in_sum)
        out_sum[...] = jnp.zeros_like(out_sum)

    grad = out_ref[...]
    dh = jnp.where(pl.program_id(0) < per_group, ins[0][...], ins[1][...])
    for q in range(4):
        part = slice(q * tile, (q + 1) * tile)
        in_sum[part, :] += contract_rows(normed_ref[:, part], grad)
    for x in range(2):
        part = slice(x * tile, (x + 1) * tile)
        out_sum[part, :] += contract_rows(gated_ref[:, part], dh)

    @pl.when(pl.program_id(0) == pl.num_programs(0) - 1)
    def _():
        own_y = here_ref[1] == 0
        half = width // 2
        for dx in range(2):
            x = lax.rem(here_ref[0] + dx, 2)
            for k in range(2):
                q = pl.multiple_of((2 * x + k) * tile, tile)
                parts = (
                    (in_sum[pl.ds(q, tile), :], slice(0, wide)),
                    (
                        out_sum[pl.ds(pl.multiple_of(x * tile, tile), tile), k * half : (k + 1) * half],
                        slice(wide, wide + half),
                    ),
                )
                for value, where in parts:
                    value = value.astype(BF).reshape(-1, 2, blocks[0].shape[2], value.shape[1])
                    low, high = value[:, 0], value[:, 1]
                    own, other = jnp.where(own_y, low, high), jnp.where(own_y, high, low)
                    cuts = (own[:lower], other[:lower], own[lower:], other[lower:])
                    for cut_, target in zip(cuts, blocks[4 * dx : 4 * dx + 4], strict=True):
                        target[k, :, :, where] = cut_


def mixer_grads(dh, wout, projected, mixed, halo, masks, taps, normed, gated, here, nz, rows, lower, tile):
    count, wide = projected.shape
    width, feats = dh[0].shape[1], wout.shape[0]
    per_group = count // (2 * tile)

    def at(i):
        return (i // per_group) * per_group + per_group - 1 - lax.rem(i, per_group)

    def turned(columns):
        return pl.BlockSpec((tile, columns), lambda i: (at(i), 0))

    def fixed(shape):
        return pl.BlockSpec(shape, lambda i: (0,) * len(shape))

    columns = wide + width // 2
    shapes = [(2, n, rows, columns) for n in (lower, lower, nz - lower, nz - lower)] * 2
    out = pl.pallas_call(
        functools.partial(mixer_grads_body, per_group, lower),
        grid=(2 * per_group,),
        in_specs=[
            pl.BlockSpec(memory_space=pltpu.SMEM),
            turned(width),
            turned(feats),
            pl.BlockSpec((tile, width), lambda i: (jnp.maximum(per_group - 1 - i, 0), 0)),
            pl.BlockSpec(
                (tile, width), lambda i: (jnp.minimum(2 * per_group - 1 - i, per_group - 1), 0)
            ),
            whole(wout),
            turned(wide),
            turned(feats),
            pl.BlockSpec((1, 2, feats), lambda i: (i // per_group, 0, 0)),
            turned(masks.shape[1]),
            whole(taps),
        ],
        out_specs=[turned(wide), fixed((8, feats))] + [fixed(shape) for shape in shapes],
        out_shape=[out_array((count, wide), BF), out_array((8, feats), F32)]
        + [out_array(shape, BF) for shape in shapes],
        scratch_shapes=[
            pltpu.VMEM((tile + 8, feats), F32),
            pltpu.VMEM((2, feats), F32),
            pltpu.VMEM((width, wide), F32),
            pltpu.VMEM((feats, width), F32),
        ],
        compiler_params=params(46),
        cost_estimate=cost(),
    )(here, *pinned(normed, gated, *dh, wout, projected, mixed, halo, masks, taps))
    return out[0], out[1], [out[2:6], out[6:]]


def norm_back_body(counts, *refs):
    grad, refs = 0.0, list(refs)
    for count in counts:
        grad = grad + piece_tile(refs[:count]).astype(F32)
        refs = refs[count:]
    x_ref, gain_ref, up_ref, *outs = refs
    x = x_ref[...].astype(F32)
    scale = lax.rsqrt(jnp.mean(x * x, axis=1, keepdims=True) + EPS)
    scaled = x * scale
    weighted = grad * gain_ref[...]
    mean = jnp.mean(weighted * scaled, axis=1, keepdims=True)
    out = up_ref[...].astype(F32) + scale * (weighted - scaled * mean)
    for ref in outs[:-1]:
        ref[...] = out.astype(ref.dtype)

    @pl.when(pl.program_id(0) == 0)
    def _():
        outs[-1][...] = jnp.zeros_like(outs[-1])

    outs[-1][...] += jnp.sum(grad * scaled, axis=0, keepdims=True)


def norm_back(grads, x, gain, upstream, kinds, tile):
    count, width = x.shape
    line = pl.BlockSpec((1, width), lambda i: (0, 0))
    specs = [spec for pieces in grads for spec in piece_specs(pieces, tile)]
    out = pl.pallas_call(
        functools.partial(norm_back_body, [len(pieces) for pieces in grads]),
        grid=(count // tile,),
        in_specs=specs + [tiles(tile, width), line, tiles(tile, width)],
        out_specs=[tiles(tile, width)] * len(kinds) + [line],
        out_shape=[out_array((count, width), kind) for kind in kinds]
        + [jax.ShapeDtypeStruct((1, width), F32)],
        compiler_params=params(16),
        cost_estimate=cost(),
    )(*pinned(*[piece for pieces in grads for piece in pieces], x, gain[None], upstream))
    return out[:-1], out[-1][0]


def per_device(
    block_input,
    in_weight,
    out_weight,
    gate_weight,
    up_weight,
    down_weight,
    norm_gain,
    ffn_gain,
    conv_weight,
    seq_starts,
    cotangent,
):
    ax, ac, az, ay = Axis(("far", "x")), Axis("core"), Axis("z"), Axis("y")
    ap = Axis("x")
    nx, nz, far = ax.size, az.size, lax.axis_size("far")
    core = ac.here
    here = jnp.stack([ax.here, ay.here, az.here]).astype(jnp.int32)
    tokens, width = block_input.shape
    rows = in_weight.shape[0]
    hidden = gate_weight.shape[1] // 4
    feats = width // 2
    wide_cols = 3 * feats
    lower = nz // 2
    few = max(1, nz // 4)
    z_back = (0,) + az.steps
    first_back, second_back = z_back[:lower], z_back[lower:]

    small = jnp.concatenate(
        [norm_gain[:, None], ffn_gain[:, None], conv_weight, jnp.zeros((rows, 123), F32)], 1
    ).astype(BF)
    in_sets = in_weight.astype(BF).reshape(rows, 3 * nx, 2, feats // nx)

    def in_part(which):
        return jnp.concatenate([pick(in_sets, which, 2).reshape(rows, wide_cols), small], 1)

    in_mine, in_got = in_part(core), ac.shift(in_part(1 - core))
    starts_core = ac.shift(seq_starts)

    def split_hidden(weight):
        cut = weight.astype(BF).reshape(rows, far, 2, 2, hidden // far)
        return jnp.transpose(cut, (2, 3, 0, 1, 4)).reshape(2, 2, rows, hidden)

    in_mine, in_got, gate_weight, up_weight = fence(in_mine, in_got, gate_weight, up_weight)
    out_low = out_weight.astype(BF).reshape(rows, 2, feats).transpose(1, 0, 2)
    mix = jnp.concatenate([ordered(in_mine, in_got, core, 0), out_low], 2)
    mix_z = {by: az.shift(mix, by) for by in first_back[1:]}
    gate_up = jnp.concatenate([split_hidden(gate_weight), split_hidden(up_weight)], 3)
    pair_mine = pick(gate_up, core, 1)
    pair_send = jnp.split(pick(gate_up, 1 - core, 1), 2, 2)
    pair_got = jnp.concatenate([ac.shift(part) for part in pair_send], 2)

    pair_mine, pair_got, mix, mix_z, cotangent, down_low = fence(
        pair_mine, pair_got, mix, mix_z, cotangent, down_weight.astype(BF)
    )
    first = jnp.stack([mix] + [mix_z[by] for by in first_back[1:]])
    first_y = ay.shift(first)
    second = [az.shift(mix, by) for by in second_back]
    pair = ordered(pair_mine, pair_got, core, 1)
    quad_mine, quad_got = pick(pair, ap.here, 0), ap.shift(pick(pair, 1 - ap.here, 0))
    quad = ordered(quad_mine, quad_got, ap.here, 0)
    first_x = [ax.shift(first, by) for by in ax.steps]
    second, first, first_y, first_x, quad, down_low = fence(
        second, first, first_y, first_x, quad, down_low
    )

    gathered = lax.all_gather(quad.reshape(4 * rows, 2 * hidden), SPREAD, axis=0, tiled=True)
    second = jnp.stack(second)
    second_x = [ax.shift(second, by) for by in ax.steps]
    second_y = ay.shift(second)
    second_x, second_y, second, first_y, block_input, cotangent, down_low = fence(
        second_x, second_y, second, first_y, block_input, cotangent, down_low
    )

    ffn_down = lax.all_gather(down_low, SPREAD, axis=0, tiled=True)
    first_yx = [ax.shift(first_y, by) for by in ax.steps]
    second_xy = [ay.shift(part) for part in second_x]
    x_core = ac.shift(block_input)
    dy_core = ac.shift(cotangent)
    x_all = jnp.concatenate([block_input, x_core], 0)
    starts = jnp.concatenate([seq_starts, starts_core], 0)
    position = lax.axis_index(("z", "y")) * tokens + jnp.arange(tokens + 2, dtype=jnp.int32)
    reached = starts[:, None, :] <= position[None, :, None]
    offset = position[None, :] - jnp.max(jnp.where(reached, starts[:, None, :], 0), axis=2)
    masks = [offset[:, :tokens] >= 1, offset[:, :tokens] >= 2]
    masks += [offset[:, 1 : 1 + tokens] >= 1, offset[:, 2:] >= 2]
    masks = jnp.stack(masks, 2).astype(F32).reshape(2 * tokens, 4)
    first_yx, second_xy, first, second, x_all, dy_core, masks, cotangent = fence(
        first_yx, second_xy, first, second, x_all, dy_core, masks, cotangent
    )

    dy_x = ap.shift(cotangent)
    pieces = [(0, 0, first_back, first), (0, 1, first_back, first_y)]
    pieces += [(0, 0, second_back, second), (0, 1, second_back, second_y)]
    for n, dx in enumerate(ax.steps):
        pieces += [(dx, 0, first_back, first_x[n]), (dx, 1, first_back, first_yx[n])]
        pieces += [(dx, 0, second_back, second_x[n]), (dx, 1, second_back, second_xy[n])]
    mix_in, tiny, mix_out = place_mix(pieces, here, ax, ay, az, wide_cols, width)
    tiny = tiny[:, :8].astype(F32)
    gain_mix, gain_ffn = tiny[:, 0], tiny[:, 1]
    taps = pick(tiny[:, 2:5].reshape(nx, 2, feats // nx, 3), core, 1).reshape(feats, 3)

    taps = jnp.concatenate([taps.T, jnp.zeros((5, feats), F32)], 0)

    last = x_all.reshape(2, tokens, width)[:, tokens - 2 :].reshape(4, width).astype(F32)
    scale = lax.rsqrt(jnp.mean(last * last, axis=1, keepdims=True) + EPS)
    last = times((last * scale * gain_mix[None, :]).astype(BF), mix_in)
    halo = passed_along((last[:, :feats] * last[:, 2 * feats :]).reshape(2, 2, feats), 1)
    normed_mix, projected, mixed, gated, mixer_keep, mixer_send = mixer_forward(
        x_all, gain_mix, mix_in, halo, masks, taps, mix_out, tokens // 2
    )
    mixer_send, mixer_keep, dy_x = fence(mixer_send, mixer_keep, dy_x)

    mixer_got = ac.shift(mixer_send)
    dy_far = [dy_x, ac.shift(dy_x)]
    own_inputs = block_input.astype(F32)
    h = own_inputs + (mixer_keep + mixer_got)
    scale_ffn = lax.rsqrt(jnp.mean(h * h, axis=1, keepdims=True) + EPS)
    normed_own = (h * scale_ffn * gain_ffn[None, :]).astype(BF)
    normed_core = ac.shift(normed_own)

    normed_core, normed_own, h, scale_ffn = fence(normed_core, normed_own, h, scale_ffn)
    normed_x = ap.shift(normed_own)
    gathered = gathered.reshape(far, 2 * nz, 4, rows, 2 * hidden)
    gate_up = gathered.transpose(0, 2, 1, 3, 4).reshape(width, 2 * hidden)
    near = [normed_own, normed_core]
    dy_near = [cotangent, dy_core]
    near_ev, near_s = ffn_forward(near, gate_up, tokens // 2)
    tile = 384 if hidden % 384 == 0 else hidden
    spec = pl.BlockSpec((tile, width), lambda i: (i, 0))
    near_down = weight_grad([near_s], dy_near, tile, spec, (hidden, width), F32)
    normed_x, near_ev, near_s, near_down = fence(normed_x, near_ev, near_s, near_down)

    far_tokens = [normed_x, ac.shift(normed_x)]
    far_ev, far_s = ffn_forward(far_tokens, gate_up, tokens // 2)

    grad_down = weight_grad([far_s], dy_far, tile, spec, (hidden, width), BF, [near_down])
    far_ev, far_s, grad_down = fence(far_ev, far_s, grad_down)

    down_own, down_send = cut(grad_down.reshape(far, nz, 2, -1, width), ay, 2)
    down_got = shifted(down_send, ay)
    far_dev, far_keep, far_send = ffn_back(dy_far, far_ev, ffn_down, gate_up, tokens // 2)
    far_got = [ac.shift(part) for part in far_send]
    far_fed, far_fed_send = row_halves(times, far_s, ffn_down, width, tokens // 2)
    down_own, down_got, far_dev, far_keep, far_got, far_fed, far_fed_send, near_ev, dy_near = fence(
        down_own, down_got, far_dev, far_keep, far_got, far_fed, far_fed_send, near_ev, dy_near
    )

    down_own, down_send = cut(summed(down_own, down_got).astype(BF), az, 1)
    down_got = shifted(down_send, az)
    normed_x_got = ap.shift((far_keep + jnp.concatenate(far_got, 0)).astype(BF))
    near_dev, near_keep, near_send = ffn_back(dy_near, near_ev, ffn_down, gate_up, tokens // 2)
    grad_gate_up = gate_up_grad(near + far_tokens, [near_dev, far_dev], far, nz, rows)
    normed_x_got, near_keep, near_send, grad_gate_up, down_own, down_got = fence(
        normed_x_got, near_keep, near_send, grad_gate_up, down_own, down_got
    )

    quad = lax.psum_scatter(grad_gate_up, SPREAD, scatter_dimension=0, tiled=True)
    near_got = [ac.shift(part) for part in near_send]
    near_got, near_keep, far_fed_send, far_fed = fence(near_got, near_keep, far_fed_send, far_fed)
    far_fed_got = [ac.shift(part) for part in far_fed_send]
    (grad_hidden, hidden_own), grad_gain_ffn = norm_back(
        [[near_keep], near_got, [normed_x_got]], h, gain_ffn, cotangent, (F32, BF), tokens // 2
    )
    hidden_got = ac.shift(hidden_own)

    hidden_got, hidden_own, grad_hidden, far_fed, far_fed_got = fence(
        hidden_got, hidden_own, grad_hidden, far_fed, far_fed_got
    )
    fed_x = ap.shift((far_fed + jnp.concatenate(far_fed_got, 0)).astype(BF))
    hidden_low = [hidden_own, hidden_got]
    opening = jnp.concatenate([part[:2] for part in hidden_low], 0)
    branch = projected.reshape(2, tokens, wide_cols)[:, :2, feats : 2 * feats].reshape(4, feats)
    opening = contract_cols(opening, mix_out) * branch
    later = passed_along(opening.reshape(2, 2, feats), -1)
    back_args = (hidden_low, mix_out, projected, mixed, later, masks, taps)
    if nx == 2 and rows % 16 == 0 and 2 * nz * rows % 128 == 0:
        grad_projected, tap_grads, blocks = mixer_grads(
            *back_args, normed_mix, gated, here, nz, rows, few, tokens // 2
        )
    else:
        grad_projected, tap_grads = mixer_back(*back_args, tokens // 2)
        back_in = contract_rows(normed_mix, grad_projected).astype(BF)
        back_out = contract_rows(gated, jnp.concatenate(hidden_low, 0)).astype(BF)
        back_out = back_out.reshape(nx, nz, 2, rows, 2, feats).transpose(0, 4, 1, 2, 3, 5)
        back_mix = jnp.concatenate(
            [back_in.reshape(nx, 2, nz, 2, rows, wide_cols), back_out], 5
        )
        blocks = []
        for dx in (0,) + ax.steps:
            ys = [pick(pick(back_mix, ax.at(dx), 0), ay.at(dy), 2) for dy in range(2)]
            blocks.append([y[:, part] for part in (slice(few), slice(few, None)) for y in ys])
    blocks, grad_projected, near_s, fed_x = fence(blocks, grad_projected, near_s, fed_x)

    first_hop = [ay.shift(block[1]) for block in blocks[1:]]
    first_got = [ay.shift(blocks[0][1])]
    second_hop = [ax.shift(block[3], by) for block, by in zip(blocks[1:], ax.steps, strict=True)]
    mix_keep, mix_send, grad_gain_mix = input_grad(grad_projected, mix_in, x_all, tokens // 2)
    near_fed, near_fed_send = row_halves(times, near_s, ffn_down, width, tokens // 2)
    tap_rows = tap_grads[:3].reshape(3, nx, 1, feats // nx)
    on_core = (jnp.arange(2) == core).astype(F32)[None, None, :, None]
    tap_rows = (tap_rows * on_core).reshape(3, width)
    own_gain = jnp.concatenate([grad_gain_mix[None], grad_gain_ffn[None]], 0)
    terms = jnp.concatenate([own_gain, tap_rows], 0)
    first_hop, first_got, second_hop, blocks, mix_keep, mix_send, near_fed_send, terms = fence(
        first_hop, first_got, second_hop, blocks, mix_keep, mix_send, near_fed_send, terms
    )

    second_got = [ay.shift(summed(blocks[0][3], second_hop).astype(BF))]
    for n, by in enumerate(ax.steps):
        block = blocks[n + 1]
        first_got.append(ax.shift(summed(block[0], [first_hop[n]]).astype(BF), by))
        second_got.append(ax.shift(block[2], by))
    mix_got = [ac.shift(part) for part in mix_send]
    near_fed_got = [ac.shift(part) for part in near_fed_send]
    (grad_inputs,), _ = norm_back(
        [[mix_keep], mix_got], block_input, gain_mix, grad_hidden, (BF,), tokens // 4
    )
    for axis in (ac, ax):
        terms = summed(terms, [axis.shift(terms, by) for by in axis.steps])
    terms = terms.reshape(5, 2 * nx, nz, 2 * rows).transpose(2, 0, 1, 3).reshape(nz, -1)
    high = lax.reduce_precision(terms, 8, 7)
    terms = jnp.concatenate([high, terms - high], 1).astype(BF)
    extra = -(-terms.shape[1] // (2 * rows * 128)) * 128
    terms = jnp.pad(terms, ((0, 0), (0, 2 * rows * extra - terms.shape[1])))
    terms = terms.reshape(nz, 2, rows, extra).transpose(1, 0, 2, 3)
    first_got, second_got, blocks, grad_inputs, terms, near_fed_got = fence(
        first_got, second_got, blocks, grad_inputs, terms, near_fed_got
    )

    own_z = jnp.concatenate(
        [summed(blocks[0][0], first_got).astype(BF), summed(blocks[0][2], second_got).astype(BF)], 1
    )
    own_z = jnp.concatenate([own_z, terms], 3)
    mix_own, mix_send = cut(own_z, az, 1)
    mix_parts = shifted(mix_send, az)
    quad = quad.reshape(4, rows, 2 * hidden)
    quad = [pick(quad, (2 * ap.here + core) ^ step, 0) for step in range(4)]
    quad[1:] = [
        lax.ppermute(part, ("x", "core"), [(i, i ^ step) for i in range(4)])
        for step, part in enumerate(quad[1:], 1)
    ]
    mix_parts, mix_own, quad = fence(mix_parts, mix_own, quad)
    mix_sum = summed(mix_own, mix_parts)
    terms = mix_sum[..., wide_cols + feats :].reshape(-1)
    count = 5 * 4 * nx * rows
    terms = (terms[:count] + terms[count : 2 * count]).reshape(5, 4 * nx * rows)

    terms = terms + ay.shift(terms)
    at = ((ax.here * 2 + core) * 2 + ay.here) * rows
    sides = [ordered(quad[n], quad[n + 1], core, 0) for n in (0, 2)]
    part_down = summed(down_own, down_got)
    if far > 1:
        part_down = lax.psum_scatter(part_down, "far", scatter_dimension=0, tiled=True)
    part_down = part_down[0]
    block_output = (h + (near_fed + jnp.concatenate(near_fed_got, 0) + fed_x.astype(F32))).astype(BF)
    part_out = mix_sum[..., wide_cols : wide_cols + feats].transpose(1, 0, 2).reshape(rows, width)
    in_mine, in_send = cut(mix_sum[..., :wide_cols], ac, 0)
    in_got = shifted(in_send, ac)[0]
    blocks = (rows, 3 * nx, feats // nx)
    part_in = ordered(in_mine.reshape(blocks), in_got.reshape(blocks), core, 2)
    quads = ordered(*sides, ap.here, 0).astype(F32)

    def join_hidden(sets):
        sets = sets.reshape(2, 2, rows, far, hidden // far)
        return jnp.transpose(sets, (2, 3, 0, 1, 4)).reshape(rows, 4 * hidden)

    part_gate, part_rise = join_hidden(quads[..., :hidden]), join_hidden(quads[..., hidden:])
    own_terms = lax.dynamic_slice_in_dim(terms, at, rows, 1)
    return (
        block_output,
        grad_inputs,
        part_in.reshape(rows, 3 * width),
        part_out,
        part_gate,
        part_rise,
        part_down,
        own_terms[0],
        own_terms[1],
        own_terms[2:].T,
    )


def solution(mesh):
    nd, nf = mesh.shape["dp"], mesh.shape["fsdp"]
    rows, line = P(AXES, None), P(AXES)
    return jax.shard_map(
        per_device,
        mesh=Mesh(mesh.devices.reshape(nd // 4, 2, 2, nf // 2, 2), AXES),
        in_specs=(rows,) * 6 + (line, line, rows, P(AXES[:3], None), rows),
        out_specs=(rows,) * 7 + (line, line, rows),
        check_vma=False,
    )
```

profile of v0, /device:TPU:0, one launch (start us, length us, event | category | flops | bytes accessed | tf_op | source)
XLA Modules:
  0.0 389.6 jit_solution(6574904684446516942)
XLA Ops:
  16.3 3.0 collective-permute-start.3
  19.3 9.0 %collective-permute-done.3 = bf16[2,32,2176]{2,1,0:T(8,128)(2,1)S(1)} collective-permute-done((bf16[2,32,2176]{2,1,0:T(8,128)(2,1)S(1)}, bf16[2,32,2176]{2,1,0:T(8,128)(2,1)S(1)}, u32[]{:S(2)}, u32[]{:S(2)}) %collective-permute-start.3) | collective-permute-done | bytes 278560 | tf_op jit(solution)/shard_map/ppermute | solution.py:28
  33.9 6.2 %collective-permute-done.8 = bf16[2,32,2304]{2,1,0:T(8,128)(2,1)S(1)} collective-permute-done((bf16[2,32,2304]{2,1,0:T(8,128)(2,1)S(1)}, bf16[2,32,2304]{2,1,0:T(8,128)(2,1)S(1)}, u32[]{:S(2)}, u32[]{:S(2)}) %collective-permute-start.8) | collective-permute-done | bytes 294944 | tf_op jit(solution)/shard_map/ppermute | solution.py:28
  41.1 6.2 %collective-permute-done.5 = bf16[2,32,2176]{2,1,0:T(8,128)(2,1)S(1)} collective-permute-done((bf16[2,32,2176]{2,1,0:T(8,128)(2,1)S(1)}, bf16[2,32,2176]{2,1,0:T(8,128)(2,1)S(1)}, u32[]{:S(2)}, u32[]{:S(2)}) %collective-permute-start.5) | collective-permute-done | bytes 278560 | tf_op jit(solution)/shard_map/ppermute | solution.py:28
  47.3 2.8 collective-permute-done.7.refs_4_
  54.1 9.6 %collective-permute-done.9.refs_6_ = bf16[2,2,32,2176]{3,2,1,0:T(8,128)(2,1)S(1)} collective-permute-done((bf16[2,2,32,2176]{3,2,1,0:T(8,128)(2,1)S(1)}, bf16[2,2,32,2176]{3,2,1,0:T(8,128)(2,1)S(1)}, u32[]{:S(2)}, u32[]{:S(2)}) %collective-permute-start.9) | collective-permute-done | bytes 557088 | tf_op jit(solution)/shard_map/ppermute | solution.py:28
  63.8 6.7 %collective-permute-done.10.refs_3_ = bf16[2,2,32,2176]{3,2,1,0:T(8,128)(2,1)S(1)} collective-permute-done((bf16[2,2,32,2176]{3,2,1,0:T(8,128)(2,1)S(1)}, bf16[2,2,32,2176]{3,2,1,0:T(8,128)(2,1)S(1)}, u32[]{:S(2)}, u32[]{:S(2)}) %collective-permute-start.10) | collective-permute-done | bytes 557088 | tf_op jit(solution)/shard_map/ppermute | solution.py:28
  73.4 2.4 collective-permute-start.12
  78.7 9.7 %collective-permute-done.11.refs_5_ = bf16[2,2,32,2176]{3,2,1,0:T(8,128)(2,1)} collective-permute-done((bf16[2,2,32,2176]{3,2,1,0:T(8,128)(2,1)}, bf16[2,2,32,2176]{3,2,1,0:T(8,128)(2,1)}, u32[]{:S(2)}, u32[]{:S(2)}) %collective-permute-start.11) | collective-permute-done | bytes 557088 | tf_op jit(solution)/shard_map/ppermute | solution.py:28
  88.3 1.8 collective-permute-done.12.refs_7_
  90.1 3.5 shard_map.186
  94.7 1.9 collective-permute-start.17
  98.9 4.4 %collective-permute-start.16 = (f32[2,2,512]{2,1,0:T(2,128)S(1)}, f32[2,2,512]{2,1,0:T(2,128)S(1)}, u32[]{:S(2)}, u32[]{:S(2)}) collective-permute-start(f32[2,2,512]{2,1,0:T(2,128)S(1)} %reshape.359), channel_id=1, source_target_pairs={{0,1},{1,2},{2,3},{3,4},{4,5},{5,6},{6,7},{8,9},{9,10},{10,11},{11... | collective-permute-start | bytes 24584 | tf_op jit(solution)/shard_map/ppermute | solution.py:37
  106.9 10.3 %shard_map.187 = (bf16[1024,1024]{1,0:T(8,128)(2,1)}, f32[1024,1536]{1,0:T(8,128)}, f32[1024,512]{1,0:T(8,128)}, bf16[1024,512]{1,0:T(8,128)(2,1)}, f32[512,1024]{1,0:T(8,128)}, /*index=5*/bf16[512,1024]{1,0:T(8,128)(2,1)}) custom-call(bf16[1024,1024]{1,0:T(8,128)(2,1)} %pad_maximum_fusion.x_ref, f32[1,1024]{1,0:T(1,128)S(1)} %get-tuple-element.419.gain_ref.refs_6_, ...), custom_call_target="tpu_custom_call" | custom-call | bytes 65536 | tf_op jit(solution)/shard_map/pallas_call | solution.py:427
  119.3 2.3 collective-permute-done.18
  121.6 2.4 multiply_reduce_fusion
  124.4 2.5 collective-permute-done.19.refs_1_
  129.3 2.1 all-gather.3.cloned.1.call-done
  131.4 4.8 %copy.102 = bf16[1,4,8,32,2304]{4,3,2,1,0:T(8,128)(2,1)} copy(bf16[1,4,8,32,2304]{4,3,1,2,0:T(8,128)(2,1)} %bitcast.196) | data formatting | bytes 9437184 | tf_op jit(solution)/shard_map/transpose | solution.py:783
  136.3 11.3 %shard_map.188 = (bf16[1024,2304]{1,0:T(8,128)(2,1)}, bf16[1024,1152]{1,0:T(8,128)(2,1)}) custom-call(bf16[512,1024]{1,0:T(8,128)(2,1)} %copy-done.9, bf16[512,1024]{1,0:T(8,128)(2,1)} %copy-done.12, bf16[1024,2304]{1,0:T(8,128)(2,1)} %bitcast.187), custom_call_target="tpu_custom_call" | custom-call | bytes 65536 | tf_op jit(solution)/shard_map/pallas_call | solution.py:214
  147.6 6.7 %shard_map.189.refs_3_ = f32[1152,1024]{1,0:T(8,128)} custom-call(bf16[1024,1152]{1,0:T(8,128)(2,1)} %get-tuple-element.309.refs_0_.left_ref, bf16[512,1024]{1,0:T(8,128)(2,1)} %refs_6_, bf16[512,1024]{1,0:T(8,128)(2,1)} %collective-permute-done.14.refs_2_.refs_1_), custom_call_target="tpu_custom_call" | custom-call | bytes 65536 | tf_op jit(solution)/shard_map/pallas_call | solution.py:370
  154.8 2.4 collective-permute-done.21.refs_1_.refs_3_
  158.1 11.6 %shard_map.190 = (bf16[1024,2304]{1,0:T(8,128)(2,1)}, bf16[1024,1152]{1,0:T(8,128)(2,1)}) custom-call(bf16[512,1024]{1,0:T(8,128)(2,1)} %collective-permute-done.20.refs_0_.refs_2_, bf16[512,1024]{1,0:T(8,128)(2,1)} %copy-done.13, bf16[1024,2304]{1,0:T(8,128)(2,1)} %bitcast.188), custom_call_target="tpu_custom_call" | custom-call | bytes 65536 | tf_op jit(solution)/shard_map/pallas_call | solution.py:214
  170.7 7.1 %shard_map.191 = bf16[1152,1024]{1,0:T(8,128)(2,1)} custom-call(bf16[1024,1152]{1,0:T(8,128)(2,1)} %get-tuple-element.251.refs_0_.left_ref, bf16[512,1024]{1,0:T(8,128)(2,1)} %collective-permute-done.17.refs_1_.refs_0_, bf16[512,1024]{1,0:T(8,128)(2,1)} %copy-done.14, f32[1152,1024]{1,0:T(8,128)} %shard_map.189.refs_3_), custom_call_target="tpu_custom_call" | custom-call | bytes 65536 | tf_op jit(solution)/shard_map/pallas_call | solution.py:370
  177.8 3.0 dynamic-slice_bitcast_fusion
  182.2 2.4 all-gather.5.cloned.1.call-done.refs_3_.weight_ref
  184.6 14.8 %shard_map.192 = (bf16[1024,2304]{1,0:T(8,128)(2,1)S(1)}, f32[512,1024]{1,0:T(8,128)}, bf16[256,1024]{1,0:T(8,128)(2,1)}, bf16[256,1024]{1,0:T(8,128)(2,1)}) custom-call(bf16[512,1024]{1,0:T(8,128)(2,1)} %collective-permute-done.17.refs_1_.refs_0_, bf16[512,1024]{1,0:T(8,128)(2,1)} %copy-done.14, bf16[1024,2304]{1,0:T(8,128)(2,1)} %get-tuple-element.245.refs_2_, ...), custom_call_target="tpu_custom_call" | custom-call | bytes 65536 | tf_op jit(solution)/shard_map/pallas_call | solution.py:285
  200.0 8.7 %shard_map.193 = (f32[512,1024]{1,0:T(8,128)}, bf16[128,1024]{1,0:T(8,128)(2,1)S(1)}, bf16[128,1024]{1,0:T(8,128)(2,1)S(1)}, bf16[128,1024]{1,0:T(8,128)(2,1)S(1)}, bf16[128,1024]{1,0:T(8,128)(2,1)S(1)}) custom-call(bf16[1024,1152]{1,0:T(8,128)(2,1)} %get-tuple-element.251.refs_0_.left_ref, bf16[1152,1024]{1,0:T(8,128)(2,1)} %all-gather.5.cloned.1.call-done.refs_3_.weight_ref), custom_call_target="tpu_custom_call" | custom-call | bytes 65536 | tf_op jit(solution)/shard_map/pallas_call | solution.py:305
  213.8 2.6 collective-permute-start.28
  216.5 14.9 %shard_map.194 = (bf16[1024,2304]{1,0:T(8,128)(2,1)S(1)}, f32[512,1024]{1,0:T(8,128)}, bf16[256,1024]{1,0:T(8,128)(2,1)}, bf16[256,1024]{1,0:T(8,128)(2,1)}) custom-call(bf16[512,1024]{1,0:T(8,128)(2,1)} %refs_6_, bf16[512,1024]{1,0:T(8,128)(2,1)} %collective-permute-done.14.refs_2_.refs_1_, bf16[1024,2304]{1,0:T(8,128)(2,1)} %get-tuple-element.263.refs_2_, ...), custom_call_target="tpu_custom_call" | custom-call | bytes 65536 | tf_op jit(solution)/shard_map/pallas_call | solution.py:285
  231.4 13.0 %shard_map.195 = bf16[1,8,4,32,2304]{4,3,2,1,0:T(8,128)(2,1)} custom-call(bf16[512,1024]{1,0:T(8,128)(2,1)} %copy-done.9, bf16[512,1024]{1,0:T(8,128)(2,1)} %copy-done.12, bf16[512,1024]{1,0:T(8,128)(2,1)} %collective-permute-done.20.refs_0_.refs_2_, bf16[512,1024]{1,0:T(8,128)(2,1)} %copy-done.13, bf16[1024,2304]{1,0:T(8,128)(2,1)S(1)} %get-tuple-element.267.refs_4_, ...), custom_call_target="tpu_custom_call" | custom-call | bytes 65536 | tf_op jit(solution)/shard_map/pallas_call | solution.py:370
  248.7 5.0 %shard_map.196 = (f32[512,1024]{1,0:T(8,128)}, bf16[512,1024]{1,0:T(8,128)(2,1)}, f32[1,1024]{1,0:T(1,128)S(1)}) custom-call(f32[512,1024]{1,0:T(8,128)} %get-tuple-element.279.refs_0_, bf16[256,1024]{1,0:T(8,128)(2,1)} %copy-done.29, bf16[256,1024]{1,0:T(8,128)(2,1)} %copy-done.30, bf16[512,1024]{1,0:T(8,128)(2,1)} %collective-permute-done.26.refs_3_, ...), custom_call_target="tpu_custom_call" | custom-call | bytes 65536 | tf_op jit(solution)/shard_map/pallas_call | solution.py:646
  254.9 1.9 collective-permute-done.33
  264.4 4.0 %collective-permute-done.37.refs_5_ = f32[2,2,512]{2,1,0:T(2,128)S(1)} collective-permute-done((f32[2,2,512]{2,1,0:T(2,128)S(1)}, f32[2,2,512]{2,1,0:T(2,128)S(1)}, u32[]{:S(2)}, u32[]{:S(2)}) %collective-permute-start.37) | collective-permute-done | bytes 8224 | tf_op jit(solution)/shard_map/ppermute | solution.py:37
  268.4 14.8 %shard_map.197 = (bf16[1024,1536]{1,0:T(8,128)(2,1)}, f32[8,512]{1,0:T(8,128)S(1)}, bf16[2,1,32,2048]{3,2,1,0:T(8,128)(2,1)S(1)}, bf16[2,1,32,2048]{3,2,1,0:T(8,...) custom-call(s32[3]{0:T(128)S(1)} %pad_add_fusion.2.here_ref, ...), custom_call_target="tpu_custom_call" | custom-call | bytes 65536 | tf_op jit(solution)/shard_map/pallas_call | solution.py:587
  283.2 2.6 collective-permute-done.38
  286.6 1.9 collective-permute-start.39
  288.7 9.3 %shard_map.199 = (f32[512,1024]{1,0:T(8,128)}, bf16[128,1024]{1,0:T(8,128)(2,1)S(1)}, bf16[128,1024]{1,0:T(8,128)(2,1)S(1)}, bf16[128,1024]{1,0:T(8,128)(2,1)S(1...) custom-call(bf16[1024,1536]{1,0:T(8,128)(2,1)} %get-tuple-element.319.dp_ref, bf16[1024,1536]{1,0:T(8,128)(2,1)} %bitcast.180, ...), custom_call_target="tpu_custom_call" | custom-call | bytes 65536 | tf_op jit(solution)/shard_map/pallas_call | solution.py:335
  298.0 7.1 %shard_map.198 = (f32[512,1024]{1,0:T(8,128)}, bf16[128,1024]{1,0:T(8,128)(2,1)S(1)}, bf16[128,1024]{1,0:T(8,128)(2,1)S(1)}, bf16[128,1024]{1,0:T(8,128)(2,1)S(1)}, bf16[128,1024]{1,0:T(8,128)(2,1)S(1)}) custom-call(bf16[1024,1152]{1,0:T(8,128)(2,1)} %get-tuple-element.309.refs_0_.left_ref, bf16[1152,1024]{1,0:T(8,128)(2,1)} %all-gather.5.cloned.1.call-done.refs_3_.weight_ref), custom_call_target="tpu_custom_call" | custom-call | bytes 65536 | tf_op jit(solution)/shard_map/pallas_call | solution.py:305
  308.6 2.3 add_convert_fusion.5
  312.5 2.9 collective-permute-done.50
  320.0 4.8 %shard_map.200 = (bf16[512,1024]{1,0:T(8,128)(2,1)}, f32[1,1024]{1,0:T(1,128)}) custom-call(f32[512,1024]{1,0:T(8,128)} %get-tuple-element.340.refs_0_, bf16[128,1024]{1,0:T(8,128)(2,1)S(1)} %collective-permute-done.45.refs_1_, bf16[128,1024]{1,0:T(8,128)(2,1)S(1)} %collective-permute-done.46.refs_2_, bf16[128,1024]{1,0:T(8,128)(2,1)S(1)} %collective-permute-done.47.refs_3_, ...), custom_call_target="tpu_custom_call" | custom-call | bytes 65536 | tf_op jit(solution)/shard_map/pallas_call | solution.py:646
  324.8 8.5 %collective-permute-done.43 = bf16[2,3,32,2048]{3,2,1,0:T(8,128)(2,1)} collective-permute-done((bf16[2,3,32,2048]{3,2,1,0:T(8,128)(2,1)}, bf16[2,3,32,2048]{3,2,1,0:T(8,128)(2,1)}, u32[]{:S(2)}, u32[]{:S(2)}) %collective-permute-start.43) | collective-permute-done | bytes 786464 | tf_op jit(solution)/shard_map/ppermute | solution.py:28
  335.1 1.8 add_convert_fusion.4
  338.5 3.5 collective-permute-start.56
  343.0 16.6 %reduce-scatter.2.cloned.1.call-done = bf16[128,2304]{1,0:T(8,128)(2,1)} async-done(((bf16[1024,2304]{1,0:T(8,128)(2,1)}), bf16[128,2304]{1,0:T(8,128)(2,1)}) %reduce-scatter.2.cloned.1.call-update) | async-done | bytes 589840 | tf_op jit(solution)/shard_map/reduce_scatter | solution.py:816
  362.7 3.8 add_convert_fusion.1
  366.5 6.5 %collective-permute-done.57 = bf16[2,32,2176]{2,1,0:T(8,128)(2,1)S(1)} collective-permute-done((bf16[2,32,2176]{2,1,0:T(8,128)(2,1)S(1)}, bf16[2,32,2176]{2,1,0:T(8,128)(2,1)S(1)}, u32[]{:S(2)}, u32[]{:S(2)}) %collective-permute-start.57) | collective-permute-done | bytes 278560 | tf_op jit(solution)/shard_map/ppermute | solution.py:28
  (327 shorter events, 87.2 us)
Async XLA Ops:
  7.2 124.2 %all-gather.3.cloned.1.call-start = ((), (), s32[]{:S(2)}) async-start(), calls=%async_computation.1 | async-start | bytes 5308416 | tf_op jit(solution)/shard_map/all_gather | solution.py:725
  16.3 12.0 %collective-permute-start.3 = (bf16[2,32,2176]{2,1,0:T(8,128)(2,1)S(1)}, bf16[2,32,2176]{2,1,0:T(8,128)(2,1)S(1)}, u32[]{:S(2)}, u32[]{:S(2)}) collective-permute-start(bf16[2,32,2176]{2,1,0:T(8,128)(2,1)S(1)} %pad_maximum_fusion.9), channel_id=1, source_target_pairs={{0,2},{2,4},{4,6},{6,0},{1,3},{3,5},{5,7},{7,1},{8,10},{10,12},{12... | collective-permute-start | bytes 835592 | tf_op jit(solution)/shard_map/ppermute | solution.py:28
  28.3 12.8 %collective-permute-start.4 = (bf16[2,32,2176]{2,1,0:T(8,128)(2,1)S(1)}, bf16[2,32,2176]{2,1,0:T(8,128)(2,1)S(1)}, u32[]{:S(2)}, u32[]{:S(2)}) collective-permute-start(bf16[2,32,2176]{2,1,0:T(8,128)(2,1)S(1)} %pad_maximum_fusion.9), channel_id=1, source_target_pairs={{0,6},{2,0},{4,2},{6,4},{1,7},{3,1},{5,3},{7,5},{8,14},{10,8},{12,... | collective-permute-start | bytes 835592 | tf_op jit(solution)/shard_map/ppermute | solution.py:28
  30.0 17.2 %collective-permute-start.5 = (bf16[2,32,2176]{2,1,0:T(8,128)(2,1)S(1)}, bf16[2,32,2176]{2,1,0:T(8,128)(2,1)S(1)}, u32[]{:S(2)}, u32[]{:S(2)}) collective-permute-start(bf16[2,32,2176]{2,1,0:T(8,128)(2,1)S(1)} %pad_maximum_fusion.9), channel_id=1, source_target_pairs={{0,4},{2,6},{4,0},{6,2},{1,5},{3,7},{5,1},{7,3},{8,12},{10,14},{12... | collective-permute-start | bytes 835592 | tf_op jit(solution)/shard_map/ppermute | solution.py:28
  30.1 10.0 %collective-permute-start.8 = (bf16[2,32,2304]{2,1,0:T(8,128)(2,1)S(1)}, bf16[2,32,2304]{2,1,0:T(8,128)(2,1)S(1)}, u32[]{:S(2)}, u32[]{:S(2)}) collective-permute-start(bf16[2,32,2304]{2,1,0:T(8,128)(2,1)S(1)} %fusion.1), channel_id=1, source_target_pairs={{0,16},{16,0},{1,17},{17,1},{2,18},{18,2},{3,19},{19,3},{4,20},{20... | collective-permute-start | bytes 884744 | tf_op jit(solution)/shard_map/ppermute | solution.py:28
  31.8 15.5 %collective-permute-start.6 = (bf16[2,2,32,2176]{3,2,1,0:T(8,128)(2,1)S(1)}, bf16[2,2,32,2176]{3,2,1,0:T(8,128)(2,1)S(1)}, u32[]{:S(2)}, u32[]{:S(2)}) collective-permute-start(bf16[2,2,32,2176]{3,2,1,0:T(8,128)(2,1)S(1)} %pad_maximum_fusion.3.refs_0_), channel_id=1, source_target_pairs={{0,1},{1,0},{2,3},{3,2},{4,5},{5,4},{6,7},{7,6},{8,9},{9,8},{10,11... | collective-permute-start | bytes 1671176 | tf_op jit(solution)/shard_map/ppermute | solution.py:28
  33.4 16.7 %collective-permute-start.7 = (bf16[2,2,32,2176]{3,2,1,0:T(8,128)(2,1)S(1)}, bf16[2,2,32,2176]{3,2,1,0:T(8,128)(2,1)S(1)}, u32[]{:S(2)}, u32[]{:S(2)}) collective-permute-start(bf16[2,2,32,2176]{3,2,1,0:T(8,128)(2,1)S(1)} %pad_maximum_fusion.3.refs_0_), channel_id=1, source_target_pairs={{0,16},{16,0},{1,17},{17,1},{2,18},{18,2},{3,19},{19,3},{4,20},{20... | collective-permute-start | bytes 1671176 | tf_op jit(solution)/shard_map/ppermute | solution.py:28
  50.9 133.7 %all-gather.5.cloned.1.call-start = ((), (), s32[]{:S(2)}) async-start(), calls=%async_computation.2 | async-start | bytes 2654208 | tf_op jit(solution)/shard_map/all_gather | solution.py:733
  51.1 12.7 %collective-permute-start.9 = (bf16[2,2,32,2176]{3,2,1,0:T(8,128)(2,1)S(1)}, bf16[2,2,32,2176]{3,2,1,0:T(8,128)(2,1)S(1)}, u32[]{:S(2)}, u32[]{:S(2)}) collective-permute-start(bf16[2,2,32,2176]{3,2,1,0:T(8,128)(2,1)S(1)} %pad_maximum_fusion.4.refs_2_), channel_id=1, source_target_pairs={{0,16},{16,0},{1,17},{17,1},{2,18},{18,2},{3,19},{19,3},{4,20},{20... | collective-permute-start | bytes 1671176 | tf_op jit(solution)/shard_map/ppermute | solution.py:28
  52.6 17.8 %collective-permute-start.10 = (bf16[2,2,32,2176]{3,2,1,0:T(8,128)(2,1)S(1)}, bf16[2,2,32,2176]{3,2,1,0:T(8,128)(2,1)S(1)}, u32[]{:S(2)}, u32[]{:S(2)}) collective-permute-start(bf16[2,2,32,2176]{3,2,1,0:T(8,128)(2,1)S(1)} %pad_maximum_fusion.4.refs_2_), channel_id=1, source_target_pairs={{0,1},{1,0},{2,3},{3,2},{4,5},{5,4},{6,7},{7,6},{8,9},{9,8},{10,11... | collective-permute-start | bytes 1671176 | tf_op jit(solution)/shard_map/ppermute | solution.py:28
  70.5 6.7 %collective-permute-start.13 = (bf16[512,1024]{1,0:T(8,128)(2,1)S(1)}, bf16[512,1024]{1,0:T(8,128)(2,1)S(1)}, u32[]{:S(2)}, u32[]{:S(2)}) collective-permute-start(bf16[512,1024]{1,0:T(8,128)(2,1)S(1)} %copy-done.11), channel_id=1, source_target_pairs={{0,8},{8,0},{1,9},{9,1},{2,10},{10,2},{3,11},{11,3},{4,12},{12,4},... | collective-permute-start | bytes 3145736 | tf_op jit(solution)/shard_map/ppermute | solution.py:28
  71.3 18.8 %collective-permute-start.14 = (bf16[512,1024]{1,0:T(8,128)(2,1)S(1)}, bf16[512,1024]{1,0:T(8,128)(2,1)}, u32[]{:S(2)}, u32[]{:S(2)}) collective-permute-start(bf16[512,1024]{1,0:T(8,128)(2,1)S(1)} %copy-done.10), channel_id=1, source_target_pairs={{0,8},{8,0},{1,9},{9,1},{2,10},{10,2},{3,11},{11,3},{4,12},{12,4},... | collective-permute-start | bytes 3145736 | tf_op jit(solution)/shard_map/ppermute | solution.py:28
  73.3 15.0 %collective-permute-start.11 = (bf16[2,2,32,2176]{3,2,1,0:T(8,128)(2,1)}, bf16[2,2,32,2176]{3,2,1,0:T(8,128)(2,1)}, u32[]{:S(2)}, u32[]{:S(2)}) collective-permute-start(bf16[2,2,32,2176]{3,2,1,0:T(8,128)(2,1)} %copy-done.25), channel_id=1, source_target_pairs={{0,16},{16,0},{1,17},{17,1},{2,18},{18,2},{3,19},{19,3},{4,20},{20... | collective-permute-start | bytes 1671176 | tf_op jit(solution)/shard_map/ppermute | solution.py:28
  73.4 16.7 %collective-permute-start.12 = (bf16[2,2,32,2176]{3,2,1,0:T(8,128)(2,1)}, bf16[2,2,32,2176]{3,2,1,0:T(8,128)(2,1)}, u32[]{:S(2)}, u32[]{:S(2)}) collective-permute-start(bf16[2,2,32,2176]{3,2,1,0:T(8,128)(2,1)} %copy-done.27), channel_id=1, source_target_pairs={{0,1},{1,0},{2,3},{3,2},{4,5},{5,4},{6,7},{7,6},{8,9},{9,8},{10,11... | collective-permute-start | bytes 1671176 | tf_op jit(solution)/shard_map/ppermute | solution.py:28
  94.7 24.0 %collective-permute-start.17 = (bf16[512,1024]{1,0:T(8,128)(2,1)}, bf16[512,1024]{1,0:T(8,128)(2,1)}, u32[]{:S(2)}, u32[]{:S(2)}) collective-permute-start(bf16[512,1024]{1,0:T(8,128)(2,1)} %refs_6_), channel_id=1, source_target_pairs={{0,16},{16,0},{1,17},{17,1},{2,18},{18,2},{3,19},{19,3},{4,20},{20... | collective-permute-start | bytes 3145736 | tf_op jit(solution)/shard_map/ppermute | solution.py:28
  98.9 5.8 %collective-permute-start.16 = (f32[2,2,512]{2,1,0:T(2,128)S(1)}, f32[2,2,512]{2,1,0:T(2,128)S(1)}, u32[]{:S(2)}, u32[]{:S(2)}) collective-permute-start(f32[2,2,512]{2,1,0:T(2,128)S(1)} %reshape.359), channel_id=1, source_target_pairs={{0,1},{1,2},{2,3},{3,4},{4,5},{5,6},{6,7},{8,9},{9,10},{10,11},{11... | collective-permute-start | bytes 24584 | tf_op jit(solution)/shard_map/ppermute | solution.py:37
  118.8 240.9 %reduce-scatter.2.cloned.1.call-start = ((), (), s32[]{:S(2)}) async-start(), calls=%async_computation.3 | async-start | bytes 5308416 | tf_op jit(solution)/shard_map/reduce_scatter | solution.py:816
  128.0 26.3 %collective-permute-start.20 = (bf16[512,1024]{1,0:T(8,128)(2,1)S(1)}, bf16[512,1024]{1,0:T(8,128)(2,1)}, u32[]{:S(2)}, u32[]{:S(2)}) collective-permute-start(bf16[512,1024]{1,0:T(8,128)(2,1)S(1)} %multiply_convert_fusion.refs_0_), channel_id=1, source_target_pairs={{0,16},{16,0},{1,17},{17,1},{2,18},{18,2},{3,19},{19,3},{4,20},{20... | collective-permute-start | bytes 3145736 | tf_op jit(solution)/shard_map/ppermute | solution.py:28
  154.3 15.4 %collective-permute-start.22 = (bf16[512,1024]{1,0:T(8,128)(2,1)}, bf16[512,1024]{1,0:T(8,128)(2,1)S(1)}, u32[]{:S(2)}, u32[]{:S(2)}) collective-permute-start(bf16[512,1024]{1,0:T(8,128)(2,1)} %collective-permute-done.17.refs_1_.refs_0_), channel_id=1, source_target_pairs={{0,8},{8,0},{1,9},{9,1},{2,10},{10,2},{3,11},{11,3},{4,12},{12,4},... | collective-permute-start | bytes 3145736 | tf_op jit(solution)/shard_map/ppermute | solution.py:28
  180.8 28.3 %collective-permute-start.23 = (bf16[1,4,144,1024]{3,2,1,0:T(8,128)(2,1)}, bf16[1,4,144,1024]{3,2,1,0:T(8,128)(2,1)S(1)}, u32[]{:S(2)}, u32[]{:S(2)}) collective-permute-start(bf16[1,4,144,1024]{3,2,1,0:T(8,128)(2,1)} %get-tuple-element.382), channel_id=1, source_target_pairs={{0,1},{1,0},{2,3},{3,2},{4,5},{5,4},{6,7},{7,6},{8,9},{9,8},{10,11... | collective-permute-start | bytes 3538952 | tf_op jit(solution)/shard_map/ppermute | solution.py:28
  199.4 9.3 %collective-permute-start.24 = (bf16[256,1024]{1,0:T(8,128)(2,1)}, bf16[256,1024]{1,0:T(8,128)(2,1)S(1)}, u32[]{:S(2)}, u32[]{:S(2)}) collective-permute-start(bf16[256,1024]{1,0:T(8,128)(2,1)} %get-tuple-element.249), channel_id=1, source_target_pairs={{0,8},{8,0},{1,9},{9,1},{2,10},{10,2},{3,11},{11,3},{4,12},{12,4},... | collective-permute-start | bytes 1572872 | tf_op jit(solution)/shard_map/ppermute | solution.py:28
  199.5 9.2 %collective-permute-start.25 = (bf16[256,1024]{1,0:T(8,128)(2,1)}, bf16[256,1024]{1,0:T(8,128)(2,1)S(1)}, u32[]{:S(2)}, u32[]{:S(2)}) collective-permute-start(bf16[256,1024]{1,0:T(8,128)(2,1)} %get-tuple-element.250), channel_id=1, source_target_pairs={{0,8},{8,0},{1,9},{9,1},{2,10},{10,2},{3,11},{11,3},{4,12},{12,4},... | collective-permute-start | bytes 1572872 | tf_op jit(solution)/shard_map/ppermute | solution.py:28
  210.5 33.9 %collective-permute-start.26 = (bf16[512,1024]{1,0:T(8,128)(2,1)}, bf16[512,1024]{1,0:T(8,128)(2,1)}, u32[]{:S(2)}, u32[]{:S(2)}) collective-permute-start(bf16[512,1024]{1,0:T(8,128)(2,1)} %add_convert_fusion.3), channel_id=1, source_target_pairs={{0,16},{16,0},{1,17},{17,1},{2,18},{18,2},{3,19},{19,3},{4,20},{20... | collective-permute-start | bytes 3145736 | tf_op jit(solution)/shard_map/ppermute | solution.py:28
  212.5 31.9 %collective-permute-start.27 = (bf16[1,144,1024]{2,1,0:T(8,128)(2,1)S(1)}, bf16[1,144,1024]{2,1,0:T(8,128)(2,1)S(1)}, u32[]{:S(2)}, u32[]{:S(2)}) collective-permute-start(bf16[1,144,1024]{2,1,0:T(8,128)(2,1)S(1)} %get-tuple-element.388), channel_id=1, source_target_pairs={{0,2},{2,4},{4,6},{6,0},{1,3},{3,5},{5,7},{7,1},{8,10},{10,12},{12... | collective-permute-start | bytes 884744 | tf_op jit(solution)/shard_map/ppermute | solution.py:28
  213.8 30.5 %collective-permute-start.28 = (bf16[1,144,1024]{2,1,0:T(8,128)(2,1)S(1)}, bf16[1,144,1024]{2,1,0:T(8,128)(2,1)S(1)}, u32[]{:S(2)}, u32[]{:S(2)}) collective-permute-start(bf16[1,144,1024]{2,1,0:T(8,128)(2,1)S(1)} %get-tuple-element.387), channel_id=1, source_target_pairs={{0,6},{2,0},{4,2},{6,4},{1,7},{3,1},{5,3},{7,5},{8,14},{10,8},{12,... | collective-permute-start | bytes 884744 | tf_op jit(solution)/shard_map/ppermute | solution.py:28
  216.5 27.9 %collective-permute-start.29 = (bf16[1,144,1024]{2,1,0:T(8,128)(2,1)S(1)}, bf16[1,144,1024]{2,1,0:T(8,128)(2,1)S(1)}, u32[]{:S(2)}, u32[]{:S(2)}) collective-permute-start(bf16[1,144,1024]{2,1,0:T(8,128)(2,1)S(1)} %get-tuple-element.386), channel_id=1, source_target_pairs={{0,4},{2,6},{4,0},{6,2},{1,5},{3,7},{5,1},{7,3},{8,12},{10,14},{12... | collective-permute-start | bytes 884744 | tf_op jit(solution)/shard_map/ppermute | solution.py:28
  260.3 25.5 %collective-permute-start.38 = (bf16[512,1024]{1,0:T(8,128)(2,1)}, bf16[512,1024]{1,0:T(8,128)(2,1)}, u32[]{:S(2)}, u32[]{:S(2)}) collective-permute-start(bf16[512,1024]{1,0:T(8,128)(2,1)} %add_convert_fusion.2), channel_id=1, source_target_pairs={{0,16},{16,0},{1,17},{17,1},{2,18},{18,2},{3,19},{19,3},{4,20},{20... | collective-permute-start | bytes 3145736 | tf_op jit(solution)/shard_map/ppermute | solution.py:28
  262.9 5.5 %collective-permute-start.37 = (f32[2,2,512]{2,1,0:T(2,128)S(1)}, f32[2,2,512]{2,1,0:T(2,128)S(1)}, u32[]{:S(2)}, u32[]{:S(2)}) collective-permute-start(f32[2,2,512]{2,1,0:T(2,128)S(1)} %reshape.370), channel_id=1, source_target_pairs={{1,0},{2,1},{3,2},{4,3},{5,4},{6,5},{7,6},{9,8},{10,9},{11,10},{12... | collective-permute-start | bytes 24584 | tf_op jit(solution)/shard_map/ppermute | solution.py:37
  285.8 20.1 %collective-permute-start.41 = (bf16[2,3,32,2048]{3,2,1,0:T(8,128)(2,1)}, bf16[2,3,32,2048]{3,2,1,0:T(8,128)(2,1)}, u32[]{:S(2)}, u32[]{:S(2)}) collective-permute-start(bf16[2,3,32,2048]{3,2,1,0:T(8,128)(2,1)} %get-tuple-element.313), channel_id=1, source_target_pairs={{0,16},{16,0},{1,17},{17,1},{2,18},{18,2},{3,19},{19,3},{4,20},{20... | collective-permute-start | bytes 2359304 | tf_op jit(solution)/shard_map/ppermute | solution.py:28
  286.6 18.5 %collective-permute-start.39 = (bf16[2,1,32,2048]{3,2,1,0:T(8,128)(2,1)S(1)}, bf16[2,1,32,2048]{3,2,1,0:T(8,128)(2,1)S(1)}, u32[]{:S(2)}, u32[]{:S(2)}) collective-permute-start(bf16[2,1,32,2048]{3,2,1,0:T(8,128)(2,1)S(1)} %get-tuple-element.311), channel_id=1, source_target_pairs={{0,1},{1,0},{2,3},{3,2},{4,5},{5,4},{6,7},{7,6},{8,9},{9,8},{10,11... | collective-permute-start | bytes 786440 | tf_op jit(solution)/shard_map/ppermute | solution.py:28
  288.5 17.3 %collective-permute-start.40 = (bf16[2,1,32,2048]{3,2,1,0:T(8,128)(2,1)S(1)}, bf16[2,1,32,2048]{3,2,1,0:T(8,128)(2,1)S(1)}, u32[]{:S(2)}, u32[]{:S(2)}) collective-permute-start(bf16[2,1,32,2048]{3,2,1,0:T(8,128)(2,1)S(1)} %get-tuple-element.312), channel_id=1, source_target_pairs={{0,1},{1,0},{2,3},{3,2},{4,5},{5,4},{6,7},{7,6},{8,9},{9,8},{10,11... | collective-permute-start | bytes 786440 | tf_op jit(solution)/shard_map/ppermute | solution.py:28
  305.9 10.8 %collective-permute-start.42 = (bf16[2,1,32,2048]{3,2,1,0:T(8,128)(2,1)S(1)}, bf16[2,1,32,2048]{3,2,1,0:T(8,128)(2,1)S(1)}, u32[]{:S(2)}, u32[]{:S(2)}) collective-permute-start(bf16[2,1,32,2048]{3,2,1,0:T(8,128)(2,1)S(1)} %add_convert_fusion.7), channel_id=1, source_target_pairs={{0,16},{16,0},{1,17},{17,1},{2,18},{18,2},{3,19},{19,3},{4,20},{20... | collective-permute-start | bytes 786440 | tf_op jit(solution)/shard_map/ppermute | solution.py:28
  307.3 10.1 %collective-permute-start.45 = (bf16[128,1024]{1,0:T(8,128)(2,1)S(1)}, bf16[128,1024]{1,0:T(8,128)(2,1)S(1)}, u32[]{:S(2)}, u32[]{:S(2)}) collective-permute-start(bf16[128,1024]{1,0:T(8,128)(2,1)S(1)} %get-tuple-element.341), channel_id=1, source_target_pairs={{0,8},{8,0},{1,9},{9,1},{2,10},{10,2},{3,11},{11,3},{4,12},{12,4},... | collective-permute-start | bytes 786440 | tf_op jit(solution)/shard_map/ppermute | solution.py:28
  307.6 9.9 %collective-permute-start.46 = (bf16[128,1024]{1,0:T(8,128)(2,1)S(1)}, bf16[128,1024]{1,0:T(8,128)(2,1)S(1)}, u32[]{:S(2)}, u32[]{:S(2)}) collective-permute-start(bf16[128,1024]{1,0:T(8,128)(2,1)S(1)} %get-tuple-element.342), channel_id=1, source_target_pairs={{0,8},{8,0},{1,9},{9,1},{2,10},{10,2},{3,11},{11,3},{4,12},{12,4},... | collective-permute-start | bytes 786440 | tf_op jit(solution)/shard_map/ppermute | solution.py:28
  307.9 7.5 %collective-permute-start.50 = (f32[5,1024]{1,0:T(8,128)S(1)}, f32[5,1024]{1,0:T(8,128)S(1)}, u32[]{:S(2)}, u32[]{:S(2)}) collective-permute-start(f32[5,1024]{1,0:T(8,128)S(1)} %add.238), channel_id=1, source_target_pairs={{0,16},{16,0},{1,17},{17,1},{2,18},{18,2},{3,19},{19,3},{4,20},{20... | collective-permute-start | bytes 61448 | tf_op jit(solution)/shard_map/ppermute | solution.py:28
  310.9 22.4 %collective-permute-start.43 = (bf16[2,3,32,2048]{3,2,1,0:T(8,128)(2,1)}, bf16[2,3,32,2048]{3,2,1,0:T(8,128)(2,1)}, u32[]{:S(2)}, u32[]{:S(2)}) collective-permute-start(bf16[2,3,32,2048]{3,2,1,0:T(8,128)(2,1)} %add_convert_fusion.5), channel_id=1, source_target_pairs={{0,1},{1,0},{2,3},{3,2},{4,5},{5,4},{6,7},{7,6},{8,9},{9,8},{10,11... | collective-permute-start | bytes 2359304 | tf_op jit(solution)/shard_map/ppermute | solution.py:28
  315.4 19.6 %collective-permute-start.44 = (bf16[2,3,32,2048]{3,2,1,0:T(8,128)(2,1)}, bf16[2,3,32,2048]{3,2,1,0:T(8,128)(2,1)}, u32[]{:S(2)}, u32[]{:S(2)}) collective-permute-start(bf16[2,3,32,2048]{3,2,1,0:T(8,128)(2,1)} %get-tuple-element.337), channel_id=1, source_target_pairs={{0,16},{16,0},{1,17},{17,1},{2,18},{18,2},{3,19},{19,3},{4,20},{20... | collective-permute-start | bytes 2359304 | tf_op jit(solution)/shard_map/ppermute | solution.py:28
  319.2 5.6 %collective-permute-start.52 = (bf16[128,1024]{1,0:T(8,128)(2,1)S(1)}, bf16[128,1024]{1,0:T(8,128)(2,1)S(1)}, u32[]{:S(2)}, u32[]{:S(2)}) collective-permute-start(bf16[128,1024]{1,0:T(8,128)(2,1)S(1)} %get-tuple-element.349), channel_id=1, source_target_pairs={{0,8},{8,0},{1,9},{9,1},{2,10},{10,2},{3,11},{11,3},{4,12},{12,4},... | collective-permute-start | bytes 786440 | tf_op jit(solution)/shard_map/ppermute | solution.py:28
  319.3 5.4 %collective-permute-start.53 = (bf16[128,1024]{1,0:T(8,128)(2,1)S(1)}, bf16[128,1024]{1,0:T(8,128)(2,1)S(1)}, u32[]{:S(2)}, u32[]{:S(2)}) collective-permute-start(bf16[128,1024]{1,0:T(8,128)(2,1)S(1)} %get-tuple-element.350), channel_id=1, source_target_pairs={{0,8},{8,0},{1,9},{9,1},{2,10},{10,2},{3,11},{11,3},{4,12},{12,4},... | collective-permute-start | bytes 786440 | tf_op jit(solution)/shard_map/ppermute | solution.py:28
  319.8 5.0 %collective-permute-start.54 = (bf16[128,1024]{1,0:T(8,128)(2,1)S(1)}, bf16[128,1024]{1,0:T(8,128)(2,1)S(1)}, u32[]{:S(2)}, u32[]{:S(2)}) collective-permute-start(bf16[128,1024]{1,0:T(8,128)(2,1)S(1)} %get-tuple-element.351), channel_id=1, source_target_pairs={{0,8},{8,0},{1,9},{9,1},{2,10},{10,2},{3,11},{11,3},{4,12},{12,4},... | collective-permute-start | bytes 786440 | tf_op jit(solution)/shard_map/ppermute | solution.py:28
  337.9 24.4 %collective-permute-start.55 = (bf16[2,32,2176]{2,1,0:T(8,128)(2,1)}, bf16[2,32,2176]{2,1,0:T(8,128)(2,1)S(1)}, u32[]{:S(2)}, u32[]{:S(2)}) collective-permute-start(bf16[2,32,2176]{2,1,0:T(8,128)(2,1)} %get-tuple-element.393), channel_id=1, source_target_pairs={{0,2},{2,4},{4,6},{6,0},{1,3},{3,5},{5,7},{7,1},{8,10},{10,12},{12... | collective-permute-start | bytes 835592 | tf_op jit(solution)/shard_map/ppermute | solution.py:28
  338.5 28.0 %collective-permute-start.56 = (bf16[2,32,2176]{2,1,0:T(8,128)(2,1)}, bf16[2,32,2176]{2,1,0:T(8,128)(2,1)S(1)}, u32[]{:S(2)}, u32[]{:S(2)}) collective-permute-start(bf16[2,32,2176]{2,1,0:T(8,128)(2,1)} %get-tuple-element.392), channel_id=1, source_target_pairs={{0,6},{2,0},{4,2},{6,4},{1,7},{3,1},{5,3},{7,5},{8,14},{10,8},{12,... | collective-permute-start | bytes 835592 | tf_op jit(solution)/shard_map/ppermute | solution.py:28
  342.0 31.1 %collective-permute-start.57 = (bf16[2,32,2176]{2,1,0:T(8,128)(2,1)S(1)}, bf16[2,32,2176]{2,1,0:T(8,128)(2,1)S(1)}, u32[]{:S(2)}, u32[]{:S(2)}) collective-permute-start(bf16[2,32,2176]{2,1,0:T(8,128)(2,1)S(1)} %get-tuple-element.391), channel_id=1, source_target_pairs={{0,4},{2,6},{4,0},{6,2},{1,5},{3,7},{5,1},{7,3},{8,12},{10,14},{12... | collective-permute-start | bytes 835592 | tf_op jit(solution)/shard_map/ppermute | solution.py:28
  360.8 12.2 %collective-permute-start.58 = (bf16[32,2304]{1,0:T(8,128)(2,1)S(1)}, bf16[32,2304]{1,0:T(8,128)(2,1)S(1)}, u32[]{:S(2)}, u32[]{:S(2)}) collective-permute-start(bf16[32,2304]{1,0:T(8,128)(2,1)S(1)} %get-tuple-element.400), channel_id=1, source_target_pairs={{0,8},{8,0},{16,24},{24,16},{1,9},{9,1},{17,25},{25,17},{2,10},{10... | collective-permute-start | bytes 442376 | tf_op jit(solution)/shard_map/ppermute | solution.py:898
  360.9 12.2 %collective-permute-start.59 = (bf16[32,2304]{1,0:T(8,128)(2,1)S(1)}, bf16[32,2304]{1,0:T(8,128)(2,1)S(1)}, u32[]{:S(2)}, u32[]{:S(2)}) collective-permute-start(bf16[32,2304]{1,0:T(8,128)(2,1)S(1)} %get-tuple-element.399), channel_id=1, source_target_pairs={{0,16},{8,24},{16,0},{24,8},{1,17},{9,25},{17,1},{25,9},{2,18},{10... | collective-permute-start | bytes 442376 | tf_op jit(solution)/shard_map/ppermute | solution.py:898
  362.3 10.8 %collective-permute-start.60 = (bf16[32,2304]{1,0:T(8,128)(2,1)S(1)}, bf16[32,2304]{1,0:T(8,128)(2,1)S(1)}, u32[]{:S(2)}, u32[]{:S(2)}) collective-permute-start(bf16[32,2304]{1,0:T(8,128)(2,1)S(1)} %get-tuple-element.398), channel_id=1, source_target_pairs={{0,24},{8,16},{16,8},{24,0},{1,25},{9,17},{17,9},{25,1},{2,26},{10... | collective-permute-start | bytes 442376 | tf_op jit(solution)/shard_map/ppermute | solution.py:898
  373.6 6.1 %collective-permute-start.62 = (f32[5,256]{1,0:T(8,128)S(1)}, f32[5,256]{1,0:T(8,128)S(1)}, u32[]{:S(2)}, u32[]{:S(2)}) collective-permute-start(f32[5,256]{1,0:T(8,128)S(1)} %slice_add_fusion), channel_id=1, source_target_pairs={{0,1},{1,0},{2,3},{3,2},{4,5},{5,4},{6,7},{7,6},{8,9},{9,8},{10,11... | collective-permute-start | bytes 15368 | tf_op jit(solution)/shard_map/ppermute | solution.py:28
  375.4 5.4 %collective-permute-start.61 = (f32[32,1536]{1,0:T(8,128)S(1)}, f32[32,1536]{1,0:T(8,128)S(1)}, u32[]{:S(2)}, u32[]{:S(2)}) collective-permute-start(f32[32,1536]{1,0:T(8,128)S(1)} %get-tuple-element.409), channel_id=1, source_target_pairs={{0,8},{8,0},{1,9},{9,1},{2,10},{10,2},{3,11},{11,3},{4,12},{12,4},... | collective-permute-start | bytes 589832 | tf_op jit(solution)/shard_map/ppermute | solution.py:28
  (66 other events, 508.4 us)
Sparse Core Ops, SparseCore 0:
  51.1 80.3 all-gather.2
  134.2 50.3 all-gather.4
  245.3 114.2 reduce-scatter.1
where the time goes:
time: 397 us; the launch traced here: 390 us
  Pallas kernels  143 us (36%)
  waiting for transfers between devices  117 us (29%)
  starting transfers between devices  53.8 us (14%)
  local copies, waits for them, and re-layouts  33.6 us (8%)
  other arithmetic  26.6 us (7%)
  between operations  15 us (4%)
    ppermute x58, waiting for transfers between devices, shift(): lax.ppermute(value, self.name, [(i, (i + by) % self.size) for i in range(...  90.4 us
    ppermute x58, starting transfers between devices, shift(): lax.ppermute(value, self.name, [(i, (i + by) % self.size) for i in range(...  45.3 us
    pallas_call x2, Pallas kernels, ffn_back(): pl.pallas_call(functools.partial(back_body, len(pieces), half), grid=(2 *...  29.7 us
    pallas_call x3, Pallas kernels, weight_grad(): pl.pallas_call(functools.partial(grad_body, token_spans(lefts), token_spa...  26.7 us
    pallas_call x2, Pallas kernels, ffn_forward(): pl.pallas_call(functools.partial(forward_body, len(pieces)), grid=(count...  22.9 us
    reduce_scatter x1, waiting for transfers between devices, per_device(): lax.psum_scatter(grad_gate_up, SPREAD, scatter_dimension=0, tiled=True)  16.6 us
    pallas_call x2, Pallas kernels, row_halves(): pl.pallas_call(functools.partial(rows_body, function, half), grid=(2 * ha...  15.8 us
    pallas_call x1, Pallas kernels, mixer_grads(): pl.pallas_call(functools.partial(mixer_grads_body, per_group, lower), gri...  14.8 us
  transfers between devices with their start and end apart: 66, of which 31 were waited for; matrix products, arithmetic and copies ran while one was open for 10% of the time, Pallas kernels for 37%

commit v1 on v0

--- a/solution.py
+++ b/solution.py
@@ -656,6 +656,31 @@
     return out[:-1], out[-1][0]
 
 
+def join_body(here_ref, *refs):
+    sets, outs = refs[:4], refs[4:]
+    own, hidden = here_ref[3], outs[0].shape[1] // 4
+    for half, out_ref in enumerate(outs):
+        for block in range(4):
+            value = sets[block][:, half * hidden : (half + 1) * hidden]
+            for at in range(1, 4):
+                other = sets[block ^ at][:, half * hidden : (half + 1) * hidden]
+                value = jnp.where(own == at, other, value)
+            out_ref[:, block * hidden : (block + 1) * hidden] = value.astype(F32)
+
+
+def join_columns(sets, here):
+    rows, both = sets[0].shape
+    return pl.pallas_call(
+        join_body,
+        in_specs=[pl.BlockSpec(memory_space=pltpu.SMEM)]
+        + [pl.BlockSpec(memory_space=pltpu.VMEM)] * 4,
+        out_specs=[pl.BlockSpec(memory_space=pltpu.VMEM)] * 2,
+        out_shape=[jax.ShapeDtypeStruct((rows, 2 * both), F32)] * 2,
+        compiler_params=params(12),
+        cost_estimate=cost(),
+    )(here, *sets)
+
+
 def per_device(
     block_input,
     in_weight,
@@ -673,7 +698,7 @@
     ap = Axis("x")
     nx, nz, far = ax.size, az.size, lax.axis_size("far")
     core = ac.here
-    here = jnp.stack([ax.here, ay.here, az.here]).astype(jnp.int32)
+    here = jnp.stack([ax.here, ay.here, az.here, 2 * ap.here + core]).astype(jnp.int32)
     tokens, width = block_input.shape
     rows = in_weight.shape[0]
     hidden = gate_weight.shape[1] // 4
@@ -899,6 +924,16 @@
         for step, part in enumerate(quad[1:], 1)
     ]
     mix_parts, mix_own, quad = fence(mix_parts, mix_own, quad)
+    if far == 1 and hidden % 128 == 0 and rows % 16 == 0:
+        joined = join_columns(quad, here)
+    else:
+        sides = [ordered(quad[n], quad[n + 1], core, 0) for n in (0, 2)]
+        quads = ordered(*sides, ap.here, 0).astype(F32)
+        joined = []
+        for part in (quads[..., :hidden], quads[..., hidden:]):
+            part = part.reshape(2, 2, rows, far, hidden // far)
+            joined.append(jnp.transpose(part, (2, 3, 0, 1, 4)).reshape(rows, 4 * hidden))
+    part_gate, part_rise = joined
     mix_sum = summed(mix_own, mix_parts)
     terms = mix_sum[..., wide_cols + feats :].reshape(-1)
     count = 5 * 4 * nx * rows
@@ -906,7 +941,6 @@
 
     terms = terms + ay.shift(terms)
     at = ((ax.here * 2 + core) * 2 + ay.here) * rows
-    sides = [ordered(quad[n], quad[n + 1], core, 0) for n in (0, 2)]
     part_down = summed(down_own, down_got)
     if far > 1:
         part_down = lax.psum_scatter(part_down, "far", scatter_dimension=0, tiled=True)
@@ -917,13 +951,6 @@
     in_got = shifted(in_send, ac)[0]
     blocks = (rows, 3 * nx, feats // nx)
     part_in = ordered(in_mine.reshape(blocks), in_got.reshape(blocks), core, 2)
-    quads = ordered(*sides, ap.here, 0).astype(F32)
-
-    def join_hidden(sets):
-        sets = sets.reshape(2, 2, rows, far, hidden // far)
-        return jnp.transpose(sets, (2, 3, 0, 1, 4)).reshape(rows, 4 * hidden)
-
-    part_gate, part_rise = join_hidden(quads[..., :hidden]), join_hidden(quads[..., hidden:])
     own_terms = lax.dynamic_slice_in_dim(terms, at, rows, 1)
     return (
         block_output,

time: 397 us -> 396 us (level)
  local copies, waits for them, and re-layouts: 33.6 us -> 29 us
  transfers between devices with their start and end apart: 66 -> 66, of which waited for: 31 -> 31; matrix products, arithmetic and copies ran while one was open for 10% -> 9% of each run, Pallas kernels for 37% -> 37%
where the time goes in v1:
time: 396 us; the launch traced here: 389 us
  Pallas kernels  145 us (37%)
  waiting for transfers between devices  118 us (30%)
  starting transfers between devices  53.2 us (13%)
  local copies, waits for them, and re-layouts  29 us (7%)
  other arithmetic  27.4 us (7%)
  between operations  15.2 us (4%)
    ppermute x58, waiting for transfers between devices, shift(): lax.ppermute(value, self.name, [(i, (i + by) % self.size) for i in range(...  90.4 us
    ppermute x58, starting transfers between devices, shift(): lax.ppermute(value, self.name, [(i, (i + by) % self.size) for i in range(...  45 us
    pallas_call x2, Pallas kernels, ffn_back(): pl.pallas_call(functools.partial(back_body, len(pieces), half), grid=(2 *...  29.8 us
    pallas_call x3, Pallas kernels, weight_grad(): pl.pallas_call(functools.partial(grad_body, token_spans(lefts), token_spa...  27 us
    pallas_call x2, Pallas kernels, ffn_forward(): pl.pallas_call(functools.partial(forward_body, len(pieces)), grid=(count...  22.9 us
    reduce_scatter x1, waiting for transfers between devices, per_device(): lax.psum_scatter(grad_gate_up, SPREAD, scatter_dimension=0, tiled=True)  18.1 us
    pallas_call x2, Pallas kernels, row_halves(): pl.pallas_call(functools.partial(rows_body, function, half), grid=(2 * ha...  15.8 us
    pallas_call x1, Pallas kernels, mixer_grads(): pl.pallas_call(functools.partial(mixer_grads_body, per_group, lower), gri...  14.8 us
  transfers between devices with their start and end apart: 66, of which 31 were waited for; matrix products, arithmetic and copies ran while one was open for 9% of the time, Pallas kernels for 37%

profile of v1, /device:TPU:0, one launch (start us, length us, event | category | flops | bytes accessed | tf_op | source)
XLA Modules:
  0.0 388.8 jit_solution(6679918845867849481)
XLA Ops:
  13.8 1.7 dynamic-slice_maximum_fusion
  16.3 3.0 collective-permute-start.3
  19.3 9.0 %collective-permute-done.3 = bf16[2,32,2176]{2,1,0:T(8,128)(2,1)S(1)} collective-permute-done((bf16[2,32,2176]{2,1,0:T(8,128)(2,1)S(1)}, bf16[2,32,2176]{2,1,0:T(8,128)(2,1)S(1)}, u32[]{:S(2)}, u32[]{:S(2)}) %collective-permute-start.3) | collective-permute-done | bytes 278560 | tf_op jit(solution)/shard_map/ppermute | solution.py:28
  28.3 1.7 collective-permute-start.4
  33.9 6.2 %collective-permute-done.8 = bf16[2,32,2304]{2,1,0:T(8,128)(2,1)S(1)} collective-permute-done((bf16[2,32,2304]{2,1,0:T(8,128)(2,1)S(1)}, bf16[2,32,2304]{2,1,0:T(8,128)(2,1)S(1)}, u32[]{:S(2)}, u32[]{:S(2)}) %collective-permute-start.8) | collective-permute-done | bytes 294944 | tf_op jit(solution)/shard_map/ppermute | solution.py:28
  41.1 6.2 %collective-permute-done.5 = bf16[2,32,2176]{2,1,0:T(8,128)(2,1)S(1)} collective-permute-done((bf16[2,32,2176]{2,1,0:T(8,128)(2,1)S(1)}, bf16[2,32,2176]{2,1,0:T(8,128)(2,1)S(1)}, u32[]{:S(2)}, u32[]{:S(2)}) %collective-permute-start.5) | collective-permute-done | bytes 278560 | tf_op jit(solution)/shard_map/ppermute | solution.py:28
  47.3 2.8 collective-permute-done.7.refs_4_
  54.1 9.6 %collective-permute-done.9.refs_6_ = bf16[2,2,32,2176]{3,2,1,0:T(8,128)(2,1)S(1)} collective-permute-done((bf16[2,2,32,2176]{3,2,1,0:T(8,128)(2,1)S(1)}, bf16[2,2,32,2176]{3,2,1,0:T(8,128)(2,1)S(1)}, u32[]{:S(2)}, u32[]{:S(2)}) %collective-permute-start.9) | collective-permute-done | bytes 557088 | tf_op jit(solution)/shard_map/ppermute | solution.py:28
  63.8 6.7 %collective-permute-done.10.refs_3_ = bf16[2,2,32,2176]{3,2,1,0:T(8,128)(2,1)S(1)} collective-permute-done((bf16[2,2,32,2176]{3,2,1,0:T(8,128)(2,1)S(1)}, bf16[2,2,32,2176]{3,2,1,0:T(8,128)(2,1)S(1)}, u32[]{:S(2)}, u32[]{:S(2)}) %collective-permute-start.10) | collective-permute-done | bytes 557088 | tf_op jit(solution)/shard_map/ppermute | solution.py:28
  73.4 2.4 collective-permute-start.12
  78.6 9.7 %collective-permute-done.11.refs_5_ = bf16[2,2,32,2176]{3,2,1,0:T(8,128)(2,1)} collective-permute-done((bf16[2,2,32,2176]{3,2,1,0:T(8,128)(2,1)}, bf16[2,2,32,2176]{3,2,1,0:T(8,128)(2,1)}, u32[]{:S(2)}, u32[]{:S(2)}) %collective-permute-start.11) | collective-permute-done | bytes 557088 | tf_op jit(solution)/shard_map/ppermute | solution.py:28
  88.3 1.8 collective-permute-done.12.refs_7_
  90.1 3.5 shard_map.186
  94.7 1.9 collective-permute-start.17
  98.9 4.4 %collective-permute-start.16 = (f32[2,2,512]{2,1,0:T(2,128)S(1)}, f32[2,2,512]{2,1,0:T(2,128)S(1)}, u32[]{:S(2)}, u32[]{:S(2)}) collective-permute-start(f32[2,2,512]{2,1,0:T(2,128)S(1)} %reshape.229), channel_id=1, source_target_pairs={{0,1},{1,2},{2,3},{3,4},{4,5},{5,6},{6,7},{8,9},{9,10},{10,11},{11... | collective-permute-start | bytes 24584 | tf_op jit(solution)/shard_map/ppermute | solution.py:37
  106.9 10.3 %shard_map.187 = (bf16[1024,1024]{1,0:T(8,128)(2,1)}, f32[1024,1536]{1,0:T(8,128)}, f32[1024,512]{1,0:T(8,128)}, bf16[1024,512]{1,0:T(8,128)(2,1)}, f32[512,1024]{1,0:T(8,128)}, /*index=5*/bf16[512,1024]{1,0:T(8,128)(2,1)}) custom-call(bf16[1024,1024]{1,0:T(8,128)(2,1)} %pad_maximum_fusion.x_ref, f32[1,1024]{1,0:T(1,128)S(1)} %get-tuple-element.415.gain_ref.refs_6_, ...), custom_call_target="tpu_custom_call" | custom-call | bytes 65536 | tf_op jit(solution)/shard_map/pallas_call | solution.py:427
  119.0 2.6 collective-permute-done.18
  121.6 2.4 multiply_reduce_fusion
  124.4 2.5 collective-permute-done.19.refs_1_
  129.3 2.1 all-gather.3.cloned.1.call-done
  131.4 4.8 %copy.95 = bf16[1,4,8,32,2304]{4,3,2,1,0:T(8,128)(2,1)} copy(bf16[1,4,8,32,2304]{4,3,1,2,0:T(8,128)(2,1)} %bitcast.177) | data formatting | bytes 9437184 | tf_op jit(solution)/shard_map/transpose | solution.py:808
  136.3 11.3 %shard_map.188 = (bf16[1024,2304]{1,0:T(8,128)(2,1)}, bf16[1024,1152]{1,0:T(8,128)(2,1)}) custom-call(bf16[512,1024]{1,0:T(8,128)(2,1)} %copy-done.9, bf16[512,1024]{1,0:T(8,128)(2,1)} %copy-done.12, bf16[1024,2304]{1,0:T(8,128)(2,1)} %bitcast.168), custom_call_target="tpu_custom_call" | custom-call | bytes 65536 | tf_op jit(solution)/shard_map/pallas_call | solution.py:214
  147.5 6.7 %shard_map.189.refs_3_ = f32[1152,1024]{1,0:T(8,128)} custom-call(bf16[1024,1152]{1,0:T(8,128)(2,1)} %get-tuple-element.311.refs_0_.left_ref, bf16[512,1024]{1,0:T(8,128)(2,1)} %refs_6_, bf16[512,1024]{1,0:T(8,128)(2,1)} %collective-permute-done.14.refs_2_.refs_1_), custom_call_target="tpu_custom_call" | custom-call | bytes 65536 | tf_op jit(solution)/shard_map/pallas_call | solution.py:370
  154.7 2.4 collective-permute-done.21.refs_1_.refs_3_
  158.1 11.6 %shard_map.190 = (bf16[1024,2304]{1,0:T(8,128)(2,1)}, bf16[1024,1152]{1,0:T(8,128)(2,1)}) custom-call(bf16[512,1024]{1,0:T(8,128)(2,1)} %collective-permute-done.20.refs_0_.refs_2_, bf16[512,1024]{1,0:T(8,128)(2,1)} %copy-done.13, bf16[1024,2304]{1,0:T(8,128)(2,1)} %bitcast.169), custom_call_target="tpu_custom_call" | custom-call | bytes 65536 | tf_op jit(solution)/shard_map/pallas_call | solution.py:214
  170.7 7.1 %shard_map.191 = bf16[1152,1024]{1,0:T(8,128)(2,1)} custom-call(bf16[1024,1152]{1,0:T(8,128)(2,1)} %get-tuple-element.253.refs_0_.left_ref, bf16[512,1024]{1,0:T(8,128)(2,1)} %collective-permute-done.17.refs_1_.refs_0_, bf16[512,1024]{1,0:T(8,128)(2,1)} %copy-done.14, f32[1152,1024]{1,0:T(8,128)} %shard_map.189.refs_3_), custom_call_target="tpu_custom_call" | custom-call | bytes 65536 | tf_op jit(solution)/shard_map/pallas_call | solution.py:370
  177.8 3.0 dynamic-slice_bitcast_fusion
  182.2 2.4 all-gather.5.cloned.1.call-done.refs_3_.weight_ref
  184.6 14.8 %shard_map.192 = (bf16[1024,2304]{1,0:T(8,128)(2,1)S(1)}, f32[512,1024]{1,0:T(8,128)}, bf16[256,1024]{1,0:T(8,128)(2,1)}, bf16[256,1024]{1,0:T(8,128)(2,1)}) custom-call(bf16[512,1024]{1,0:T(8,128)(2,1)} %collective-permute-done.17.refs_1_.refs_0_, bf16[512,1024]{1,0:T(8,128)(2,1)} %copy-done.14, bf16[1024,2304]{1,0:T(8,128)(2,1)} %get-tuple-element.247.refs_2_, ...), custom_call_target="tpu_custom_call" | custom-call | bytes 65536 | tf_op jit(solution)/shard_map/pallas_call | solution.py:285
  200.0 8.7 %shard_map.193 = (f32[512,1024]{1,0:T(8,128)}, bf16[128,1024]{1,0:T(8,128)(2,1)S(1)}, bf16[128,1024]{1,0:T(8,128)(2,1)S(1)}, bf16[128,1024]{1,0:T(8,128)(2,1)S(1)}, bf16[128,1024]{1,0:T(8,128)(2,1)S(1)}) custom-call(bf16[1024,1152]{1,0:T(8,128)(2,1)} %get-tuple-element.253.refs_0_.left_ref, bf16[1152,1024]{1,0:T(8,128)(2,1)} %all-gather.5.cloned.1.call-done.refs_3_.weight_ref), custom_call_target="tpu_custom_call" | custom-call | bytes 65536 | tf_op jit(solution)/shard_map/pallas_call | solution.py:305
  213.8 2.6 collective-permute-start.28
  216.5 14.9 %shard_map.194 = (bf16[1024,2304]{1,0:T(8,128)(2,1)S(1)}, f32[512,1024]{1,0:T(8,128)}, bf16[256,1024]{1,0:T(8,128)(2,1)}, bf16[256,1024]{1,0:T(8,128)(2,1)}) custom-call(bf16[512,1024]{1,0:T(8,128)(2,1)} %refs_6_, bf16[512,1024]{1,0:T(8,128)(2,1)} %collective-permute-done.14.refs_2_.refs_1_, bf16[1024,2304]{1,0:T(8,128)(2,1)} %get-tuple-element.265.refs_2_, ...), custom_call_target="tpu_custom_call" | custom-call | bytes 65536 | tf_op jit(solution)/shard_map/pallas_call | solution.py:285
  231.4 13.2 %shard_map.195 = bf16[1,8,4,32,2304]{4,3,2,1,0:T(8,128)(2,1)} custom-call(bf16[512,1024]{1,0:T(8,128)(2,1)} %copy-done.9, bf16[512,1024]{1,0:T(8,128)(2,1)} %copy-done.12, bf16[512,1024]{1,0:T(8,128)(2,1)} %collective-permute-done.20.refs_0_.refs_2_, bf16[512,1024]{1,0:T(8,128)(2,1)} %copy-done.13, bf16[1024,2304]{1,0:T(8,128)(2,1)S(1)} %get-tuple-element.269.refs_4_, ...), custom_call_target="tpu_custom_call" | custom-call | bytes 65536 | tf_op jit(solution)/shard_map/pallas_call | solution.py:370
  249.0 5.0 %shard_map.196 = (f32[512,1024]{1,0:T(8,128)}, bf16[512,1024]{1,0:T(8,128)(2,1)}, f32[1,1024]{1,0:T(1,128)S(1)}) custom-call(f32[512,1024]{1,0:T(8,128)} %get-tuple-element.281.refs_0_, bf16[256,1024]{1,0:T(8,128)(2,1)} %copy-done.29, bf16[256,1024]{1,0:T(8,128)(2,1)} %copy-done.30, bf16[512,1024]{1,0:T(8,128)(2,1)} %collective-permute-done.26.refs_3_, ...), custom_call_target="tpu_custom_call" | custom-call | bytes 65536 | tf_op jit(solution)/shard_map/pallas_call | solution.py:646
  255.2 1.9 collective-permute-done.33
  263.7 4.0 %collective-permute-done.37.refs_5_ = f32[2,2,512]{2,1,0:T(2,128)S(1)} collective-permute-done((f32[2,2,512]{2,1,0:T(2,128)S(1)}, f32[2,2,512]{2,1,0:T(2,128)S(1)}, u32[]{:S(2)}, u32[]{:S(2)}) %collective-permute-start.37) | collective-permute-done | bytes 8224 | tf_op jit(solution)/shard_map/ppermute | solution.py:37
  267.7 14.8 %shard_map.197 = (bf16[1024,1536]{1,0:T(8,128)(2,1)}, f32[8,512]{1,0:T(8,128)S(1)}, bf16[2,1,32,2048]{3,2,1,0:T(8,128)(2,1)S(1)}, bf16[2,1,32,2048]{3,2,1,0:T(8,...) custom-call(s32[4]{0:T(128)S(1)} %pad_add_fusion.2.here_ref, ...), custom_call_target="tpu_custom_call" | custom-call | bytes 65536 | tf_op jit(solution)/shard_map/pallas_call | solution.py:587
  282.5 2.6 collective-permute-done.38
  288.0 9.2 %shard_map.199 = (f32[512,1024]{1,0:T(8,128)}, bf16[128,1024]{1,0:T(8,128)(2,1)S(1)}, bf16[128,1024]{1,0:T(8,128)(2,1)S(1)}, bf16[128,1024]{1,0:T(8,128)(2,1)S(1...) custom-call(bf16[1024,1536]{1,0:T(8,128)(2,1)} %get-tuple-element.321.dp_ref, bf16[1024,1536]{1,0:T(8,128)(2,1)} %bitcast.161, ...), custom_call_target="tpu_custom_call" | custom-call | bytes 65536 | tf_op jit(solution)/shard_map/pallas_call | solution.py:335
  297.2 7.1 %shard_map.198 = (f32[512,1024]{1,0:T(8,128)}, bf16[128,1024]{1,0:T(8,128)(2,1)S(1)}, bf16[128,1024]{1,0:T(8,128)(2,1)S(1)}, bf16[128,1024]{1,0:T(8,128)(2,1)S(1)}, bf16[128,1024]{1,0:T(8,128)(2,1)S(1)}) custom-call(bf16[1024,1152]{1,0:T(8,128)(2,1)} %get-tuple-element.311.refs_0_.left_ref, bf16[1152,1024]{1,0:T(8,128)(2,1)} %all-gather.5.cloned.1.call-done.refs_3_.weight_ref), custom_call_target="tpu_custom_call" | custom-call | bytes 65536 | tf_op jit(solution)/shard_map/pallas_call | solution.py:305
  307.9 2.3 add_convert_fusion.5
  311.7 3.0 collective-permute-done.50
  319.2 4.8 %shard_map.200 = (bf16[512,1024]{1,0:T(8,128)(2,1)}, f32[1,1024]{1,0:T(1,128)}) custom-call(f32[512,1024]{1,0:T(8,128)} %get-tuple-element.342.refs_0_, bf16[128,1024]{1,0:T(8,128)(2,1)S(1)} %collective-permute-done.45.refs_1_, bf16[128,1024]{1,0:T(8,128)(2,1)S(1)} %collective-permute-done.46.refs_2_, bf16[128,1024]{1,0:T(8,128)(2,1)S(1)} %collective-permute-done.47.refs_3_, ...), custom_call_target="tpu_custom_call" | custom-call | bytes 65536 | tf_op jit(solution)/shard_map/pallas_call | solution.py:646
  324.1 8.9 %collective-permute-done.43 = bf16[2,3,32,2048]{3,2,1,0:T(8,128)(2,1)} collective-permute-done((bf16[2,3,32,2048]{3,2,1,0:T(8,128)(2,1)}, bf16[2,3,32,2048]{3,2,1,0:T(8,128)(2,1)}, u32[]{:S(2)}, u32[]{:S(2)}) %collective-permute-start.43) | collective-permute-done | bytes 786464 | tf_op jit(solution)/shard_map/ppermute | solution.py:28
  337.7 3.2 collective-permute-start.56
  342.0 18.1 %reduce-scatter.2.cloned.1.call-done = bf16[128,2304]{1,0:T(8,128)(2,1)} async-done(((bf16[1024,2304]{1,0:T(8,128)(2,1)}), bf16[128,2304]{1,0:T(8,128)(2,1)}) %reduce-scatter.2.cloned.1.call-update) | async-done | bytes 589840 | tf_op jit(solution)/shard_map/reduce_scatter | solution.py:841
  363.2 3.9 %add_convert_fusion.1 = bf16[512,1024]{1,0:T(8,128)(2,1)} fusion(f32[512,1024]{1,0:T(8,128)S(1)} %copy-done.8, bf16[512,1024]{1,0:T(8,128)(2,1)} %collective-permute-done.38, f32[512,1024]{1,0:T(8,128)} %get-tuple-element.312, bf16[128,1024]{1,0:T(8,128)(2,1)} %copy-done.37, bf16[128,1024]{1,0:T(8,128)(2,1)} %copy-done.36, bf16[128,1024]{1,0:T(8,128)(2,1)} %copy-done.35, ...), kind=kLoop, calls=%fused_computation.2 | loop fusion | flops 6815744 | bytes 7340032 | tf_op jit(solution)/shard_map/convert_element_type | solution.py:948
  367.1 6.2 %collective-permute-done.57 = bf16[2,32,2176]{2,1,0:T(8,128)(2,1)} collective-permute-done((bf16[2,32,2176]{2,1,0:T(8,128)(2,1)}, bf16[2,32,2176]{2,1,0:T(8,128)(2,1)}, u32[]{:S(2)}, u32[]{:S(2)}) %collective-permute-start.57) | collective-permute-done | bytes 278560 | tf_op jit(solution)/shard_map/ppermute | solution.py:28
  (319 shorter events, 84.4 us)
Async XLA Ops:
  7.2 124.2 %all-gather.3.cloned.1.call-start = ((), (), s32[]{:S(2)}) async-start(), calls=%async_computation.1 | async-start | bytes 5308416 | tf_op jit(solution)/shard_map/all_gather | solution.py:750
  16.3 12.0 %collective-permute-start.3 = (bf16[2,32,2176]{2,1,0:T(8,128)(2,1)S(1)}, bf16[2,32,2176]{2,1,0:T(8,128)(2,1)S(1)}, u32[]{:S(2)}, u32[]{:S(2)}) collective-permute-start(bf16[2,32,2176]{2,1,0:T(8,128)(2,1)S(1)} %pad_maximum_fusion.7), channel_id=1, source_target_pairs={{0,2},{2,4},{4,6},{6,0},{1,3},{3,5},{5,7},{7,1},{8,10},{10,12},{12... | collective-permute-start | bytes 835592 | tf_op jit(solution)/shard_map/ppermute | solution.py:28
  28.3 12.8 %collective-permute-start.4 = (bf16[2,32,2176]{2,1,0:T(8,128)(2,1)S(1)}, bf16[2,32,2176]{2,1,0:T(8,128)(2,1)S(1)}, u32[]{:S(2)}, u32[]{:S(2)}) collective-permute-start(bf16[2,32,2176]{2,1,0:T(8,128)(2,1)S(1)} %pad_maximum_fusion.7), channel_id=1, source_target_pairs={{0,6},{2,0},{4,2},{6,4},{1,7},{3,1},{5,3},{7,5},{8,14},{10,8},{12,... | collective-permute-start | bytes 835592 | tf_op jit(solution)/shard_map/ppermute | solution.py:28
  30.0 17.2 %collective-permute-start.5 = (bf16[2,32,2176]{2,1,0:T(8,128)(2,1)S(1)}, bf16[2,32,2176]{2,1,0:T(8,128)(2,1)S(1)}, u32[]{:S(2)}, u32[]{:S(2)}) collective-permute-start(bf16[2,32,2176]{2,1,0:T(8,128)(2,1)S(1)} %pad_maximum_fusion.7), channel_id=1, source_target_pairs={{0,4},{2,6},{4,0},{6,2},{1,5},{3,7},{5,1},{7,3},{8,12},{10,14},{12... | collective-permute-start | bytes 835592 | tf_op jit(solution)/shard_map/ppermute | solution.py:28
  30.1 10.0 %collective-permute-start.8 = (bf16[2,32,2304]{2,1,0:T(8,128)(2,1)S(1)}, bf16[2,32,2304]{2,1,0:T(8,128)(2,1)S(1)}, u32[]{:S(2)}, u32[]{:S(2)}) collective-permute-start(bf16[2,32,2304]{2,1,0:T(8,128)(2,1)S(1)} %fusion.1), channel_id=1, source_target_pairs={{0,16},{16,0},{1,17},{17,1},{2,18},{18,2},{3,19},{19,3},{4,20},{20... | collective-permute-start | bytes 884744 | tf_op jit(solution)/shard_map/ppermute | solution.py:28
  31.8 15.5 %collective-permute-start.6 = (bf16[2,2,32,2176]{3,2,1,0:T(8,128)(2,1)S(1)}, bf16[2,2,32,2176]{3,2,1,0:T(8,128)(2,1)S(1)}, u32[]{:S(2)}, u32[]{:S(2)}) collective-permute-start(bf16[2,2,32,2176]{3,2,1,0:T(8,128)(2,1)S(1)} %pad_maximum_fusion.3.refs_0_), channel_id=1, source_target_pairs={{0,1},{1,0},{2,3},{3,2},{4,5},{5,4},{6,7},{7,6},{8,9},{9,8},{10,11... | collective-permute-start | bytes 1671176 | tf_op jit(solution)/shard_map/ppermute | solution.py:28
  33.4 16.7 %collective-permute-start.7 = (bf16[2,2,32,2176]{3,2,1,0:T(8,128)(2,1)S(1)}, bf16[2,2,32,2176]{3,2,1,0:T(8,128)(2,1)S(1)}, u32[]{:S(2)}, u32[]{:S(2)}) collective-permute-start(bf16[2,2,32,2176]{3,2,1,0:T(8,128)(2,1)S(1)} %pad_maximum_fusion.3.refs_0_), channel_id=1, source_target_pairs={{0,16},{16,0},{1,17},{17,1},{2,18},{18,2},{3,19},{19,3},{4,20},{20... | collective-permute-start | bytes 1671176 | tf_op jit(solution)/shard_map/ppermute | solution.py:28
  50.9 133.7 %all-gather.5.cloned.1.call-start = ((), (), s32[]{:S(2)}) async-start(), calls=%async_computation.2 | async-start | bytes 2654208 | tf_op jit(solution)/shard_map/all_gather | solution.py:758
  51.1 12.7 %collective-permute-start.9 = (bf16[2,2,32,2176]{3,2,1,0:T(8,128)(2,1)S(1)}, bf16[2,2,32,2176]{3,2,1,0:T(8,128)(2,1)S(1)}, u32[]{:S(2)}, u32[]{:S(2)}) collective-permute-start(bf16[2,2,32,2176]{3,2,1,0:T(8,128)(2,1)S(1)} %pad_maximum_fusion.4.refs_2_), channel_id=1, source_target_pairs={{0,16},{16,0},{1,17},{17,1},{2,18},{18,2},{3,19},{19,3},{4,20},{20... | collective-permute-start | bytes 1671176 | tf_op jit(solution)/shard_map/ppermute | solution.py:28
  52.6 17.8 %collective-permute-start.10 = (bf16[2,2,32,2176]{3,2,1,0:T(8,128)(2,1)S(1)}, bf16[2,2,32,2176]{3,2,1,0:T(8,128)(2,1)S(1)}, u32[]{:S(2)}, u32[]{:S(2)}) collective-permute-start(bf16[2,2,32,2176]{3,2,1,0:T(8,128)(2,1)S(1)} %pad_maximum_fusion.4.refs_2_), channel_id=1, source_target_pairs={{0,1},{1,0},{2,3},{3,2},{4,5},{5,4},{6,7},{7,6},{8,9},{9,8},{10,11... | collective-permute-start | bytes 1671176 | tf_op jit(solution)/shard_map/ppermute | solution.py:28
  70.5 6.7 %collective-permute-start.13 = (bf16[512,1024]{1,0:T(8,128)(2,1)S(1)}, bf16[512,1024]{1,0:T(8,128)(2,1)S(1)}, u32[]{:S(2)}, u32[]{:S(2)}) collective-permute-start(bf16[512,1024]{1,0:T(8,128)(2,1)S(1)} %copy-done.11), channel_id=1, source_target_pairs={{0,8},{8,0},{1,9},{9,1},{2,10},{10,2},{3,11},{11,3},{4,12},{12,4},... | collective-permute-start | bytes 3145736 | tf_op jit(solution)/shard_map/ppermute | solution.py:28
  71.3 18.8 %collective-permute-start.14 = (bf16[512,1024]{1,0:T(8,128)(2,1)S(1)}, bf16[512,1024]{1,0:T(8,128)(2,1)}, u32[]{:S(2)}, u32[]{:S(2)}) collective-permute-start(bf16[512,1024]{1,0:T(8,128)(2,1)S(1)} %copy-done.10), channel_id=1, source_target_pairs={{0,8},{8,0},{1,9},{9,1},{2,10},{10,2},{3,11},{11,3},{4,12},{12,4},... | collective-permute-start | bytes 3145736 | tf_op jit(solution)/shard_map/ppermute | solution.py:28
  73.3 15.0 %collective-permute-start.11 = (bf16[2,2,32,2176]{3,2,1,0:T(8,128)(2,1)}, bf16[2,2,32,2176]{3,2,1,0:T(8,128)(2,1)}, u32[]{:S(2)}, u32[]{:S(2)}) collective-permute-start(bf16[2,2,32,2176]{3,2,1,0:T(8,128)(2,1)} %copy-done.25), channel_id=1, source_target_pairs={{0,16},{16,0},{1,17},{17,1},{2,18},{18,2},{3,19},{19,3},{4,20},{20... | collective-permute-start | bytes 1671176 | tf_op jit(solution)/shard_map/ppermute | solution.py:28
  73.4 16.7 %collective-permute-start.12 = (bf16[2,2,32,2176]{3,2,1,0:T(8,128)(2,1)}, bf16[2,2,32,2176]{3,2,1,0:T(8,128)(2,1)}, u32[]{:S(2)}, u32[]{:S(2)}) collective-permute-start(bf16[2,2,32,2176]{3,2,1,0:T(8,128)(2,1)} %copy-done.27), channel_id=1, source_target_pairs={{0,1},{1,0},{2,3},{3,2},{4,5},{5,4},{6,7},{7,6},{8,9},{9,8},{10,11... | collective-permute-start | bytes 1671176 | tf_op jit(solution)/shard_map/ppermute | solution.py:28
  94.7 24.0 %collective-permute-start.17 = (bf16[512,1024]{1,0:T(8,128)(2,1)}, bf16[512,1024]{1,0:T(8,128)(2,1)}, u32[]{:S(2)}, u32[]{:S(2)}) collective-permute-start(bf16[512,1024]{1,0:T(8,128)(2,1)} %refs_6_), channel_id=1, source_target_pairs={{0,16},{16,0},{1,17},{17,1},{2,18},{18,2},{3,19},{19,3},{4,20},{20... | collective-permute-start | bytes 3145736 | tf_op jit(solution)/shard_map/ppermute | solution.py:28
  98.9 5.8 %collective-permute-start.16 = (f32[2,2,512]{2,1,0:T(2,128)S(1)}, f32[2,2,512]{2,1,0:T(2,128)S(1)}, u32[]{:S(2)}, u32[]{:S(2)}) collective-permute-start(f32[2,2,512]{2,1,0:T(2,128)S(1)} %reshape.229), channel_id=1, source_target_pairs={{0,1},{1,2},{2,3},{3,4},{4,5},{5,6},{6,7},{8,9},{9,10},{10,11},{11... | collective-permute-start | bytes 24584 | tf_op jit(solution)/shard_map/ppermute | solution.py:37
  118.7 241.4 %reduce-scatter.2.cloned.1.call-start = ((), (), s32[]{:S(2)}) async-start(), calls=%async_computation.3 | async-start | bytes 5308416 | tf_op jit(solution)/shard_map/reduce_scatter | solution.py:841
  128.0 26.3 %collective-permute-start.20 = (bf16[512,1024]{1,0:T(8,128)(2,1)S(1)}, bf16[512,1024]{1,0:T(8,128)(2,1)}, u32[]{:S(2)}, u32[]{:S(2)}) collective-permute-start(bf16[512,1024]{1,0:T(8,128)(2,1)S(1)} %multiply_convert_fusion.refs_0_), channel_id=1, source_target_pairs={{0,16},{16,0},{1,17},{17,1},{2,18},{18,2},{3,19},{19,3},{4,20},{20... | collective-permute-start | bytes 3145736 | tf_op jit(solution)/shard_map/ppermute | solution.py:28
  154.2 15.5 %collective-permute-start.22 = (bf16[512,1024]{1,0:T(8,128)(2,1)}, bf16[512,1024]{1,0:T(8,128)(2,1)S(1)}, u32[]{:S(2)}, u32[]{:S(2)}) collective-permute-start(bf16[512,1024]{1,0:T(8,128)(2,1)} %collective-permute-done.17.refs_1_.refs_0_), channel_id=1, source_target_pairs={{0,8},{8,0},{1,9},{9,1},{2,10},{10,2},{3,11},{11,3},{4,12},{12,4},... | collective-permute-start | bytes 3145736 | tf_op jit(solution)/shard_map/ppermute | solution.py:28
  180.7 28.3 %collective-permute-start.23 = (bf16[1,4,144,1024]{3,2,1,0:T(8,128)(2,1)}, bf16[1,4,144,1024]{3,2,1,0:T(8,128)(2,1)S(1)}, u32[]{:S(2)}, u32[]{:S(2)}) collective-permute-start(bf16[1,4,144,1024]{3,2,1,0:T(8,128)(2,1)} %get-tuple-element.386), channel_id=1, source_target_pairs={{0,1},{1,0},{2,3},{3,2},{4,5},{5,4},{6,7},{7,6},{8,9},{9,8},{10,11... | collective-permute-start | bytes 3538952 | tf_op jit(solution)/shard_map/ppermute | solution.py:28
  199.5 9.3 %collective-permute-start.24 = (bf16[256,1024]{1,0:T(8,128)(2,1)}, bf16[256,1024]{1,0:T(8,128)(2,1)S(1)}, u32[]{:S(2)}, u32[]{:S(2)}) collective-permute-start(bf16[256,1024]{1,0:T(8,128)(2,1)} %get-tuple-element.251), channel_id=1, source_target_pairs={{0,8},{8,0},{1,9},{9,1},{2,10},{10,2},{3,11},{11,3},{4,12},{12,4},... | collective-permute-start | bytes 1572872 | tf_op jit(solution)/shard_map/ppermute | solution.py:28
  199.5 9.2 %collective-permute-start.25 = (bf16[256,1024]{1,0:T(8,128)(2,1)}, bf16[256,1024]{1,0:T(8,128)(2,1)S(1)}, u32[]{:S(2)}, u32[]{:S(2)}) collective-permute-start(bf16[256,1024]{1,0:T(8,128)(2,1)} %get-tuple-element.252), channel_id=1, source_target_pairs={{0,8},{8,0},{1,9},{9,1},{2,10},{10,2},{3,11},{11,3},{4,12},{12,4},... | collective-permute-start | bytes 1572872 | tf_op jit(solution)/shard_map/ppermute | solution.py:28
  210.4 34.2 %collective-permute-start.26 = (bf16[512,1024]{1,0:T(8,128)(2,1)}, bf16[512,1024]{1,0:T(8,128)(2,1)}, u32[]{:S(2)}, u32[]{:S(2)}) collective-permute-start(bf16[512,1024]{1,0:T(8,128)(2,1)} %add_convert_fusion.3), channel_id=1, source_target_pairs={{0,16},{16,0},{1,17},{17,1},{2,18},{18,2},{3,19},{19,3},{4,20},{20... | collective-permute-start | bytes 3145736 | tf_op jit(solution)/shard_map/ppermute | solution.py:28
  212.4 32.2 %collective-permute-start.27 = (bf16[1,144,1024]{2,1,0:T(8,128)(2,1)S(1)}, bf16[1,144,1024]{2,1,0:T(8,128)(2,1)S(1)}, u32[]{:S(2)}, u32[]{:S(2)}) collective-permute-start(bf16[1,144,1024]{2,1,0:T(8,128)(2,1)S(1)} %get-tuple-element.390), channel_id=1, source_target_pairs={{0,2},{2,4},{4,6},{6,0},{1,3},{3,5},{5,7},{7,1},{8,10},{10,12},{12... | collective-permute-start | bytes 884744 | tf_op jit(solution)/shard_map/ppermute | solution.py:28
  213.8 30.8 %collective-permute-start.28 = (bf16[1,144,1024]{2,1,0:T(8,128)(2,1)S(1)}, bf16[1,144,1024]{2,1,0:T(8,128)(2,1)S(1)}, u32[]{:S(2)}, u32[]{:S(2)}) collective-permute-start(bf16[1,144,1024]{2,1,0:T(8,128)(2,1)S(1)} %get-tuple-element.389), channel_id=1, source_target_pairs={{0,6},{2,0},{4,2},{6,4},{1,7},{3,1},{5,3},{7,5},{8,14},{10,8},{12,... | collective-permute-start | bytes 884744 | tf_op jit(solution)/shard_map/ppermute | solution.py:28
  216.4 28.2 %collective-permute-start.29 = (bf16[1,144,1024]{2,1,0:T(8,128)(2,1)S(1)}, bf16[1,144,1024]{2,1,0:T(8,128)(2,1)S(1)}, u32[]{:S(2)}, u32[]{:S(2)}) collective-permute-start(bf16[1,144,1024]{2,1,0:T(8,128)(2,1)S(1)} %get-tuple-element.388), channel_id=1, source_target_pairs={{0,4},{2,6},{4,0},{6,2},{1,5},{3,7},{5,1},{7,3},{8,12},{10,14},{12... | collective-permute-start | bytes 884744 | tf_op jit(solution)/shard_map/ppermute | solution.py:28
  254.0 4.2 %collective-permute-start.32 = (bf16[512,1024]{1,0:T(8,128)(2,1)}, bf16[512,1024]{1,0:T(8,128)(2,1)S(1)}, u32[]{:S(2)}, u32[]{:S(2)}) collective-permute-start(bf16[512,1024]{1,0:T(8,128)(2,1)} %get-tuple-element.292.refs_0_), channel_id=1, source_target_pairs={{0,8},{8,0},{1,9},{9,1},{2,10},{10,2},{3,11},{11,3},{4,12},{12,4},... | collective-permute-start | bytes 3145736 | tf_op jit(solution)/shard_map/ppermute | solution.py:28
  259.5 25.5 %collective-permute-start.38 = (bf16[512,1024]{1,0:T(8,128)(2,1)}, bf16[512,1024]{1,0:T(8,128)(2,1)}, u32[]{:S(2)}, u32[]{:S(2)}) collective-permute-start(bf16[512,1024]{1,0:T(8,128)(2,1)} %add_convert_fusion.2), channel_id=1, source_target_pairs={{0,16},{16,0},{1,17},{17,1},{2,18},{18,2},{3,19},{19,3},{4,20},{20... | collective-permute-start | bytes 3145736 | tf_op jit(solution)/shard_map/ppermute | solution.py:28
  262.1 5.5 %collective-permute-start.37 = (f32[2,2,512]{2,1,0:T(2,128)S(1)}, f32[2,2,512]{2,1,0:T(2,128)S(1)}, u32[]{:S(2)}, u32[]{:S(2)}) collective-permute-start(f32[2,2,512]{2,1,0:T(2,128)S(1)} %reshape.240), channel_id=1, source_target_pairs={{1,0},{2,1},{3,2},{4,3},{5,4},{6,5},{7,6},{9,8},{10,9},{11,10},{12... | collective-permute-start | bytes 24584 | tf_op jit(solution)/shard_map/ppermute | solution.py:37
  285.1 20.1 %collective-permute-start.41 = (bf16[2,3,32,2048]{3,2,1,0:T(8,128)(2,1)}, bf16[2,3,32,2048]{3,2,1,0:T(8,128)(2,1)}, u32[]{:S(2)}, u32[]{:S(2)}) collective-permute-start(bf16[2,3,32,2048]{3,2,1,0:T(8,128)(2,1)} %get-tuple-element.315), channel_id=1, source_target_pairs={{0,16},{16,0},{1,17},{17,1},{2,18},{18,2},{3,19},{19,3},{4,20},{20... | collective-permute-start | bytes 2359304 | tf_op jit(solution)/shard_map/ppermute | solution.py:28
  285.9 18.4 %collective-permute-start.39 = (bf16[2,1,32,2048]{3,2,1,0:T(8,128)(2,1)S(1)}, bf16[2,1,32,2048]{3,2,1,0:T(8,128)(2,1)S(1)}, u32[]{:S(2)}, u32[]{:S(2)}) collective-permute-start(bf16[2,1,32,2048]{3,2,1,0:T(8,128)(2,1)S(1)} %get-tuple-element.313), channel_id=1, source_target_pairs={{0,1},{1,0},{2,3},{3,2},{4,5},{5,4},{6,7},{7,6},{8,9},{9,8},{10,11... | collective-permute-start | bytes 786440 | tf_op jit(solution)/shard_map/ppermute | solution.py:28
  287.5 17.6 %collective-permute-start.40 = (bf16[2,1,32,2048]{3,2,1,0:T(8,128)(2,1)S(1)}, bf16[2,1,32,2048]{3,2,1,0:T(8,128)(2,1)S(1)}, u32[]{:S(2)}, u32[]{:S(2)}) collective-permute-start(bf16[2,1,32,2048]{3,2,1,0:T(8,128)(2,1)S(1)} %get-tuple-element.314), channel_id=1, source_target_pairs={{0,1},{1,0},{2,3},{3,2},{4,5},{5,4},{6,7},{7,6},{8,9},{9,8},{10,11... | collective-permute-start | bytes 786440 | tf_op jit(solution)/shard_map/ppermute | solution.py:28
  305.2 10.8 %collective-permute-start.42 = (bf16[2,1,32,2048]{3,2,1,0:T(8,128)(2,1)S(1)}, bf16[2,1,32,2048]{3,2,1,0:T(8,128)(2,1)S(1)}, u32[]{:S(2)}, u32[]{:S(2)}) collective-permute-start(bf16[2,1,32,2048]{3,2,1,0:T(8,128)(2,1)S(1)} %add_convert_fusion.7), channel_id=1, source_target_pairs={{0,16},{16,0},{1,17},{17,1},{2,18},{18,2},{3,19},{19,3},{4,20},{20... | collective-permute-start | bytes 786440 | tf_op jit(solution)/shard_map/ppermute | solution.py:28
  306.6 10.1 %collective-permute-start.45 = (bf16[128,1024]{1,0:T(8,128)(2,1)S(1)}, bf16[128,1024]{1,0:T(8,128)(2,1)S(1)}, u32[]{:S(2)}, u32[]{:S(2)}) collective-permute-start(bf16[128,1024]{1,0:T(8,128)(2,1)S(1)} %get-tuple-element.343), channel_id=1, source_target_pairs={{0,8},{8,0},{1,9},{9,1},{2,10},{10,2},{3,11},{11,3},{4,12},{12,4},... | collective-permute-start | bytes 786440 | tf_op jit(solution)/shard_map/ppermute | solution.py:28
  306.8 9.9 %collective-permute-start.46 = (bf16[128,1024]{1,0:T(8,128)(2,1)S(1)}, bf16[128,1024]{1,0:T(8,128)(2,1)S(1)}, u32[]{:S(2)}, u32[]{:S(2)}) collective-permute-start(bf16[128,1024]{1,0:T(8,128)(2,1)S(1)} %get-tuple-element.344), channel_id=1, source_target_pairs={{0,8},{8,0},{1,9},{9,1},{2,10},{10,2},{3,11},{11,3},{4,12},{12,4},... | collective-permute-start | bytes 786440 | tf_op jit(solution)/shard_map/ppermute | solution.py:28
  307.1 7.5 %collective-permute-start.50 = (f32[5,1024]{1,0:T(8,128)S(1)}, f32[5,1024]{1,0:T(8,128)S(1)}, u32[]{:S(2)}, u32[]{:S(2)}) collective-permute-start(f32[5,1024]{1,0:T(8,128)S(1)} %add.240), channel_id=1, source_target_pairs={{0,16},{16,0},{1,17},{17,1},{2,18},{18,2},{3,19},{19,3},{4,20},{20... | collective-permute-start | bytes 61448 | tf_op jit(solution)/shard_map/ppermute | solution.py:28
  310.2 22.8 %collective-permute-start.43 = (bf16[2,3,32,2048]{3,2,1,0:T(8,128)(2,1)}, bf16[2,3,32,2048]{3,2,1,0:T(8,128)(2,1)}, u32[]{:S(2)}, u32[]{:S(2)}) collective-permute-start(bf16[2,3,32,2048]{3,2,1,0:T(8,128)(2,1)} %add_convert_fusion.5), channel_id=1, source_target_pairs={{0,1},{1,0},{2,3},{3,2},{4,5},{5,4},{6,7},{7,6},{8,9},{9,8},{10,11... | collective-permute-start | bytes 2359304 | tf_op jit(solution)/shard_map/ppermute | solution.py:28
  314.7 19.6 %collective-permute-start.44 = (bf16[2,3,32,2048]{3,2,1,0:T(8,128)(2,1)}, bf16[2,3,32,2048]{3,2,1,0:T(8,128)(2,1)}, u32[]{:S(2)}, u32[]{:S(2)}) collective-permute-start(bf16[2,3,32,2048]{3,2,1,0:T(8,128)(2,1)} %get-tuple-element.339), channel_id=1, source_target_pairs={{0,16},{16,0},{1,17},{17,1},{2,18},{18,2},{3,19},{19,3},{4,20},{20... | collective-permute-start | bytes 2359304 | tf_op jit(solution)/shard_map/ppermute | solution.py:28
  318.5 5.6 %collective-permute-start.52 = (bf16[128,1024]{1,0:T(8,128)(2,1)S(1)}, bf16[128,1024]{1,0:T(8,128)(2,1)S(1)}, u32[]{:S(2)}, u32[]{:S(2)}) collective-permute-start(bf16[128,1024]{1,0:T(8,128)(2,1)S(1)} %get-tuple-element.351), channel_id=1, source_target_pairs={{0,8},{8,0},{1,9},{9,1},{2,10},{10,2},{3,11},{11,3},{4,12},{12,4},... | collective-permute-start | bytes 786440 | tf_op jit(solution)/shard_map/ppermute | solution.py:28
  318.6 5.4 %collective-permute-start.53 = (bf16[128,1024]{1,0:T(8,128)(2,1)S(1)}, bf16[128,1024]{1,0:T(8,128)(2,1)S(1)}, u32[]{:S(2)}, u32[]{:S(2)}) collective-permute-start(bf16[128,1024]{1,0:T(8,128)(2,1)S(1)} %get-tuple-element.352), channel_id=1, source_target_pairs={{0,8},{8,0},{1,9},{9,1},{2,10},{10,2},{3,11},{11,3},{4,12},{12,4},... | collective-permute-start | bytes 786440 | tf_op jit(solution)/shard_map/ppermute | solution.py:28
  319.1 5.0 %collective-permute-start.54 = (bf16[128,1024]{1,0:T(8,128)(2,1)S(1)}, bf16[128,1024]{1,0:T(8,128)(2,1)S(1)}, u32[]{:S(2)}, u32[]{:S(2)}) collective-permute-start(bf16[128,1024]{1,0:T(8,128)(2,1)S(1)} %get-tuple-element.353), channel_id=1, source_target_pairs={{0,8},{8,0},{1,9},{9,1},{2,10},{10,2},{3,11},{11,3},{4,12},{12,4},... | collective-permute-start | bytes 786440 | tf_op jit(solution)/shard_map/ppermute | solution.py:28
  337.1 26.0 %collective-permute-start.55 = (bf16[2,32,2176]{2,1,0:T(8,128)(2,1)}, bf16[2,32,2176]{2,1,0:T(8,128)(2,1)S(1)}, u32[]{:S(2)}, u32[]{:S(2)}) collective-permute-start(bf16[2,32,2176]{2,1,0:T(8,128)(2,1)} %get-tuple-element.395), channel_id=1, source_target_pairs={{0,2},{2,4},{4,6},{6,0},{1,3},{3,5},{5,7},{7,1},{8,10},{10,12},{12... | collective-permute-start | bytes 835592 | tf_op jit(solution)/shard_map/ppermute | solution.py:28
  337.7 29.4 %collective-permute-start.56 = (bf16[2,32,2176]{2,1,0:T(8,128)(2,1)}, bf16[2,32,2176]{2,1,0:T(8,128)(2,1)S(1)}, u32[]{:S(2)}, u32[]{:S(2)}) collective-permute-start(bf16[2,32,2176]{2,1,0:T(8,128)(2,1)} %get-tuple-element.394), channel_id=1, source_target_pairs={{0,6},{2,0},{4,2},{6,4},{1,7},{3,1},{5,3},{7,5},{8,14},{10,8},{12,... | collective-permute-start | bytes 835592 | tf_op jit(solution)/shard_map/ppermute | solution.py:28
  340.9 32.4 %collective-permute-start.57 = (bf16[2,32,2176]{2,1,0:T(8,128)(2,1)}, bf16[2,32,2176]{2,1,0:T(8,128)(2,1)}, u32[]{:S(2)}, u32[]{:S(2)}) collective-permute-start(bf16[2,32,2176]{2,1,0:T(8,128)(2,1)} %get-tuple-element.393), channel_id=1, source_target_pairs={{0,4},{2,6},{4,0},{6,2},{1,5},{3,7},{5,1},{7,3},{8,12},{10,14},{12... | collective-permute-start | bytes 835592 | tf_op jit(solution)/shard_map/ppermute | solution.py:28
  361.3 12.0 %collective-permute-start.58 = (bf16[32,2304]{1,0:T(8,128)(2,1)S(1)}, bf16[32,2304]{1,0:T(8,128)(2,1)S(1)}, u32[]{:S(2)}, u32[]{:S(2)}) collective-permute-start(bf16[32,2304]{1,0:T(8,128)(2,1)S(1)} %get-tuple-element.400), channel_id=1, source_target_pairs={{0,8},{8,0},{16,24},{24,16},{1,9},{9,1},{17,25},{25,17},{2,10},{10... | collective-permute-start | bytes 442376 | tf_op jit(solution)/shard_map/ppermute | solution.py:923
  361.4 11.9 %collective-permute-start.59 = (bf16[32,2304]{1,0:T(8,128)(2,1)S(1)}, bf16[32,2304]{1,0:T(8,128)(2,1)S(1)}, u32[]{:S(2)}, u32[]{:S(2)}) collective-permute-start(bf16[32,2304]{1,0:T(8,128)(2,1)S(1)} %get-tuple-element.399), channel_id=1, source_target_pairs={{0,16},{8,24},{16,0},{24,8},{1,17},{9,25},{17,1},{25,9},{2,18},{10... | collective-permute-start | bytes 442376 | tf_op jit(solution)/shard_map/ppermute | solution.py:923
  363.1 10.2 %collective-permute-start.60 = (bf16[32,2304]{1,0:T(8,128)(2,1)S(1)}, bf16[32,2304]{1,0:T(8,128)(2,1)S(1)}, u32[]{:S(2)}, u32[]{:S(2)}) collective-permute-start(bf16[32,2304]{1,0:T(8,128)(2,1)S(1)} %get-tuple-element.398), channel_id=1, source_target_pairs={{0,24},{8,16},{16,8},{24,0},{1,25},{9,17},{17,9},{25,1},{2,26},{10... | collective-permute-start | bytes 442376 | tf_op jit(solution)/shard_map/ppermute | solution.py:923
  374.5 4.2 %collective-permute-start.62 = (f32[5,256]{1,0:T(8,128)S(1)}, f32[5,256]{1,0:T(8,128)S(1)}, u32[]{:S(2)}, u32[]{:S(2)}) collective-permute-start(f32[5,256]{1,0:T(8,128)S(1)} %slice_add_fusion), channel_id=1, source_target_pairs={{0,1},{1,0},{2,3},{3,2},{4,5},{5,4},{6,7},{7,6},{8,9},{9,8},{10,11... | collective-permute-start | bytes 15368 | tf_op jit(solution)/shard_map/ppermute | solution.py:28
  (65 other events, 506.6 us)
Sparse Core Ops, SparseCore 0:
  51.0 80.3 all-gather.2
  134.2 50.3 all-gather.4
  245.6 114.4 reduce-scatter.1

commit v2 on v1

--- a/solution.py
+++ b/solution.py
@@ -840,19 +840,19 @@
 
     quad = lax.psum_scatter(grad_gate_up, SPREAD, scatter_dimension=0, tiled=True)
     near_got = [ac.shift(part) for part in near_send]
-    near_got, near_keep, far_fed_send, far_fed = fence(near_got, near_keep, far_fed_send, far_fed)
     far_fed_got = [ac.shift(part) for part in far_fed_send]
+    near_got, near_keep, far_fed_got, far_fed = fence(near_got, near_keep, far_fed_got, far_fed)
     (grad_hidden, hidden_own), grad_gain_ffn = norm_back(
         [[near_keep], near_got, [normed_x_got]], h, gain_ffn, cotangent, (F32, BF), tokens // 2
     )
+    fed_x = ap.shift((far_fed + jnp.concatenate(far_fed_got, 0)).astype(BF))
+
+    head = hidden_own[:2]
+    head_got = ac.shift(head)
     hidden_got = ac.shift(hidden_own)
-
-    hidden_got, hidden_own, grad_hidden, far_fed, far_fed_got = fence(
-        hidden_got, hidden_own, grad_hidden, far_fed, far_fed_got
-    )
-    fed_x = ap.shift((far_fed + jnp.concatenate(far_fed_got, 0)).astype(BF))
+    head_got, head, grad_hidden = fence(head_got, head, grad_hidden)
     hidden_low = [hidden_own, hidden_got]
-    opening = jnp.concatenate([part[:2] for part in hidden_low], 0)
+    opening = jnp.concatenate([head, head_got], 0)
     branch = projected.reshape(2, tokens, wide_cols)[:, :2, feats : 2 * feats].reshape(4, feats)
     opening = contract_cols(opening, mix_out) * branch
     later = passed_along(opening.reshape(2, 2, feats), -1)

time: 396 us -> 395 us (level)
    ppermute x58 -> x59, waiting for transfers between devices: 90.4 us -> 89.2 us  [shift(): lax.ppermute(value, self.name, [(i, (i + by) % self.size) for i in range(...]
    ppermute x58 -> x59, starting transfers between devices: 45 us -> 45.5 us  [shift(): lax.ppermute(value, self.name, [(i, (i + by) % self.size) for i in range(...]
  transfers between devices with their start and end apart: 66 -> 67, of which waited for: 31 -> 30; matrix products, arithmetic and copies ran while one was open for 9% -> 10% of each run, Pallas kernels for 37% -> 37%
where the time goes in v2:
time: 395 us; the launch traced here: 388 us
  Pallas kernels  145 us (37%)
  waiting for transfers between devices  115 us (29%)
  starting transfers between devices  53.6 us (14%)
  other arithmetic  29.4 us (7%)
  local copies, waits for them, and re-layouts  28.1 us (7%)
  between operations  15.2 us (4%)
    ppermute x59, waiting for transfers between devices, shift(): lax.ppermute(value, self.name, [(i, (i + by) % self.size) for i in range(...  89.2 us
    ppermute x59, starting transfers between devices, shift(): lax.ppermute(value, self.name, [(i, (i + by) % self.size) for i in range(...  45.5 us
    pallas_call x2, Pallas kernels, ffn_back(): pl.pallas_call(functools.partial(back_body, len(pieces), half), grid=(2 *...  29.8 us
    pallas_call x3, Pallas kernels, weight_grad(): pl.pallas_call(functools.partial(grad_body, token_spans(lefts), token_spa...  27 us
    pallas_call x2, Pallas kernels, ffn_forward(): pl.pallas_call(functools.partial(forward_body, len(pieces)), grid=(count...  22.9 us
    reduce_scatter x1, waiting for transfers between devices, per_device(): lax.psum_scatter(grad_gate_up, SPREAD, scatter_dimension=0, tiled=True)  16.4 us
    pallas_call x2, Pallas kernels, row_halves(): pl.pallas_call(functools.partial(rows_body, function, half), grid=(2 * ha...  15.8 us
    pallas_call x1, Pallas kernels, mixer_grads(): pl.pallas_call(functools.partial(mixer_grads_body, per_group, lower), gri...  14.8 us
  transfers between devices with their start and end apart: 67, of which 30 were waited for; matrix products, arithmetic and copies ran while one was open for 10% of the time, Pallas kernels for 37%

profile of v2, /device:TPU:0, one launch (start us, length us, event | category | flops | bytes accessed | tf_op | source)
XLA Modules:
  0.0 387.8 jit_solution(982711354637169013)
XLA Ops:
  13.8 1.7 dynamic-slice_maximum_fusion
  16.3 3.0 collective-permute-start.3
  19.3 9.0 %collective-permute-done.3 = bf16[2,32,2176]{2,1,0:T(8,128)(2,1)S(1)} collective-permute-done((bf16[2,32,2176]{2,1,0:T(8,128)(2,1)S(1)}, bf16[2,32,2176]{2,1,0:T(8,128)(2,1)S(1)}, u32[]{:S(2)}, u32[]{:S(2)}) %collective-permute-start.3) | collective-permute-done | bytes 278560 | tf_op jit(solution)/shard_map/ppermute | solution.py:28
  28.3 1.7 collective-permute-start.4
  33.9 6.2 %collective-permute-done.8 = bf16[2,32,2304]{2,1,0:T(8,128)(2,1)S(1)} collective-permute-done((bf16[2,32,2304]{2,1,0:T(8,128)(2,1)S(1)}, bf16[2,32,2304]{2,1,0:T(8,128)(2,1)S(1)}, u32[]{:S(2)}, u32[]{:S(2)}) %collective-permute-start.8) | collective-permute-done | bytes 294944 | tf_op jit(solution)/shard_map/ppermute | solution.py:28
  41.1 6.2 %collective-permute-done.5 = bf16[2,32,2176]{2,1,0:T(8,128)(2,1)S(1)} collective-permute-done((bf16[2,32,2176]{2,1,0:T(8,128)(2,1)S(1)}, bf16[2,32,2176]{2,1,0:T(8,128)(2,1)S(1)}, u32[]{:S(2)}, u32[]{:S(2)}) %collective-permute-start.5) | collective-permute-done | bytes 278560 | tf_op jit(solution)/shard_map/ppermute | solution.py:28
  47.3 2.8 collective-permute-done.7.refs_4_
  54.1 9.6 %collective-permute-done.9.refs_6_ = bf16[2,2,32,2176]{3,2,1,0:T(8,128)(2,1)S(1)} collective-permute-done((bf16[2,2,32,2176]{3,2,1,0:T(8,128)(2,1)S(1)}, bf16[2,2,32,2176]{3,2,1,0:T(8,128)(2,1)S(1)}, u32[]{:S(2)}, u32[]{:S(2)}) %collective-permute-start.9) | collective-permute-done | bytes 557088 | tf_op jit(solution)/shard_map/ppermute | solution.py:28
  63.8 6.7 %collective-permute-done.10.refs_3_ = bf16[2,2,32,2176]{3,2,1,0:T(8,128)(2,1)S(1)} collective-permute-done((bf16[2,2,32,2176]{3,2,1,0:T(8,128)(2,1)S(1)}, bf16[2,2,32,2176]{3,2,1,0:T(8,128)(2,1)S(1)}, u32[]{:S(2)}, u32[]{:S(2)}) %collective-permute-start.10) | collective-permute-done | bytes 557088 | tf_op jit(solution)/shard_map/ppermute | solution.py:28
  73.4 2.4 collective-permute-start.12
  78.7 9.7 %collective-permute-done.11.refs_5_ = bf16[2,2,32,2176]{3,2,1,0:T(8,128)(2,1)} collective-permute-done((bf16[2,2,32,2176]{3,2,1,0:T(8,128)(2,1)}, bf16[2,2,32,2176]{3,2,1,0:T(8,128)(2,1)}, u32[]{:S(2)}, u32[]{:S(2)}) %collective-permute-start.11) | collective-permute-done | bytes 557088 | tf_op jit(solution)/shard_map/ppermute | solution.py:28
  88.3 1.8 collective-permute-done.12.refs_7_
  90.1 3.5 shard_map.186
  94.7 1.9 collective-permute-start.17
  98.9 4.4 %collective-permute-start.16 = (f32[2,2,512]{2,1,0:T(2,128)S(1)}, f32[2,2,512]{2,1,0:T(2,128)S(1)}, u32[]{:S(2)}, u32[]{:S(2)}) collective-permute-start(f32[2,2,512]{2,1,0:T(2,128)S(1)} %reshape.229), channel_id=1, source_target_pairs={{0,1},{1,2},{2,3},{3,4},{4,5},{5,6},{6,7},{8,9},{9,10},{10,11},{11... | collective-permute-start | bytes 24584 | tf_op jit(solution)/shard_map/ppermute | solution.py:37
  106.9 10.3 %shard_map.187 = (bf16[1024,1024]{1,0:T(8,128)(2,1)}, f32[1024,1536]{1,0:T(8,128)}, f32[1024,512]{1,0:T(8,128)}, bf16[1024,512]{1,0:T(8,128)(2,1)}, f32[512,1024]{1,0:T(8,128)}, /*index=5*/bf16[512,1024]{1,0:T(8,128)(2,1)}) custom-call(bf16[1024,1024]{1,0:T(8,128)(2,1)} %pad_maximum_fusion.x_ref, f32[1,1024]{1,0:T(1,128)S(1)} %get-tuple-element.405.gain_ref.refs_6_, ...), custom_call_target="tpu_custom_call" | custom-call | bytes 65536 | tf_op jit(solution)/shard_map/pallas_call | solution.py:427
  119.0 2.6 collective-permute-done.18
  121.6 2.4 multiply_reduce_fusion
  124.5 2.5 collective-permute-done.19.refs_1_
  129.3 2.1 all-gather.3.cloned.1.call-done
  131.4 4.8 %copy.95 = bf16[1,4,8,32,2304]{4,3,2,1,0:T(8,128)(2,1)} copy(bf16[1,4,8,32,2304]{4,3,1,2,0:T(8,128)(2,1)} %bitcast.177) | data formatting | bytes 9437184 | tf_op jit(solution)/shard_map/transpose | solution.py:808
  136.3 11.3 %shard_map.188 = (bf16[1024,2304]{1,0:T(8,128)(2,1)}, bf16[1024,1152]{1,0:T(8,128)(2,1)}) custom-call(bf16[512,1024]{1,0:T(8,128)(2,1)} %copy-done.9, bf16[512,1024]{1,0:T(8,128)(2,1)} %copy-done.12, bf16[1024,2304]{1,0:T(8,128)(2,1)} %bitcast.168), custom_call_target="tpu_custom_call" | custom-call | bytes 65536 | tf_op jit(solution)/shard_map/pallas_call | solution.py:214
  147.6 6.7 %shard_map.189.refs_3_ = f32[1152,1024]{1,0:T(8,128)} custom-call(bf16[1024,1152]{1,0:T(8,128)(2,1)} %get-tuple-element.301.refs_0_.left_ref, bf16[512,1024]{1,0:T(8,128)(2,1)} %refs_6_, bf16[512,1024]{1,0:T(8,128)(2,1)} %collective-permute-done.14.refs_2_.refs_1_), custom_call_target="tpu_custom_call" | custom-call | bytes 65536 | tf_op jit(solution)/shard_map/pallas_call | solution.py:370
  154.8 2.4 collective-permute-done.21.refs_1_.refs_3_
  158.1 11.6 %shard_map.190 = (bf16[1024,2304]{1,0:T(8,128)(2,1)}, bf16[1024,1152]{1,0:T(8,128)(2,1)}) custom-call(bf16[512,1024]{1,0:T(8,128)(2,1)} %collective-permute-done.20.refs_0_.refs_2_, bf16[512,1024]{1,0:T(8,128)(2,1)} %copy-done.13, bf16[1024,2304]{1,0:T(8,128)(2,1)} %bitcast.169), custom_call_target="tpu_custom_call" | custom-call | bytes 65536 | tf_op jit(solution)/shard_map/pallas_call | solution.py:214
  170.7 7.1 %shard_map.191 = bf16[1152,1024]{1,0:T(8,128)(2,1)} custom-call(bf16[1024,1152]{1,0:T(8,128)(2,1)} %get-tuple-element.248.refs_0_.left_ref, bf16[512,1024]{1,0:T(8,128)(2,1)} %collective-permute-done.17.refs_1_.refs_0_, bf16[512,1024]{1,0:T(8,128)(2,1)} %copy-done.14, f32[1152,1024]{1,0:T(8,128)} %shard_map.189.refs_3_), custom_call_target="tpu_custom_call" | custom-call | bytes 65536 | tf_op jit(solution)/shard_map/pallas_call | solution.py:370
  177.8 3.0 dynamic-slice_bitcast_fusion
  182.2 2.5 all-gather.5.cloned.1.call-done.refs_3_.weight_ref
  184.6 14.8 %shard_map.192 = (bf16[1024,2304]{1,0:T(8,128)(2,1)S(1)}, f32[512,1024]{1,0:T(8,128)}, bf16[256,1024]{1,0:T(8,128)(2,1)}, bf16[256,1024]{1,0:T(8,128)(2,1)}) custom-call(bf16[512,1024]{1,0:T(8,128)(2,1)} %collective-permute-done.17.refs_1_.refs_0_, bf16[512,1024]{1,0:T(8,128)(2,1)} %copy-done.14, bf16[1024,2304]{1,0:T(8,128)(2,1)} %get-tuple-element.242.refs_2_, ...), custom_call_target="tpu_custom_call" | custom-call | bytes 65536 | tf_op jit(solution)/shard_map/pallas_call | solution.py:285
  200.0 8.8 %shard_map.193 = (f32[512,1024]{1,0:T(8,128)}, bf16[128,1024]{1,0:T(8,128)(2,1)S(1)}, bf16[128,1024]{1,0:T(8,128)(2,1)S(1)}, bf16[128,1024]{1,0:T(8,128)(2,1)S(1)}, bf16[128,1024]{1,0:T(8,128)(2,1)S(1)}) custom-call(bf16[1024,1152]{1,0:T(8,128)(2,1)} %get-tuple-element.248.refs_0_.left_ref, bf16[1152,1024]{1,0:T(8,128)(2,1)} %all-gather.5.cloned.1.call-done.refs_3_.weight_ref), custom_call_target="tpu_custom_call" | custom-call | bytes 65536 | tf_op jit(solution)/shard_map/pallas_call | solution.py:305
  213.9 2.6 collective-permute-start.28
  216.5 14.9 %shard_map.194 = (bf16[1024,2304]{1,0:T(8,128)(2,1)S(1)}, f32[512,1024]{1,0:T(8,128)}, bf16[256,1024]{1,0:T(8,128)(2,1)}, bf16[256,1024]{1,0:T(8,128)(2,1)}) custom-call(bf16[512,1024]{1,0:T(8,128)(2,1)} %refs_6_, bf16[512,1024]{1,0:T(8,128)(2,1)} %collective-permute-done.14.refs_2_.refs_1_, bf16[1024,2304]{1,0:T(8,128)(2,1)} %get-tuple-element.260.refs_2_, ...), custom_call_target="tpu_custom_call" | custom-call | bytes 65536 | tf_op jit(solution)/shard_map/pallas_call | solution.py:285
  231.4 13.2 %shard_map.195 = bf16[1,8,4,32,2304]{4,3,2,1,0:T(8,128)(2,1)} custom-call(bf16[512,1024]{1,0:T(8,128)(2,1)} %copy-done.9, bf16[512,1024]{1,0:T(8,128)(2,1)} %copy-done.12, bf16[512,1024]{1,0:T(8,128)(2,1)} %collective-permute-done.20.refs_0_.refs_2_, bf16[512,1024]{1,0:T(8,128)(2,1)} %copy-done.13, bf16[1024,2304]{1,0:T(8,128)(2,1)S(1)} %get-tuple-element.264.refs_4_, ...), custom_call_target="tpu_custom_call" | custom-call | bytes 65536 | tf_op jit(solution)/shard_map/pallas_call | solution.py:370
  250.7 5.4 %shard_map.196 = (f32[512,1024]{1,0:T(8,128)}, bf16[512,1024]{1,0:T(8,128)(2,1)}, f32[1,1024]{1,0:T(1,128)S(1)}) custom-call(f32[512,1024]{1,0:T(8,128)} %get-tuple-element.276.refs_0_, bf16[256,1024]{1,0:T(8,128)(2,1)} %copy-done.28, bf16[256,1024]{1,0:T(8,128)(2,1)} %copy-done.29, bf16[512,1024]{1,0:T(8,128)(2,1)} %collective-permute-done.26.refs_3_, ...), custom_call_target="tpu_custom_call" | custom-call | bytes 65536 | tf_op jit(solution)/shard_map/pallas_call | solution.py:646
  262.2 4.0 %collective-permute-done.38.refs_5_ = f32[2,2,512]{2,1,0:T(2,128)S(1)} collective-permute-done((f32[2,2,512]{2,1,0:T(2,128)S(1)}, f32[2,2,512]{2,1,0:T(2,128)S(1)}, u32[]{:S(2)}, u32[]{:S(2)}) %collective-permute-start.38) | collective-permute-done | bytes 8224 | tf_op jit(solution)/shard_map/ppermute | solution.py:37
  266.2 14.8 %shard_map.197 = (bf16[1024,1536]{1,0:T(8,128)(2,1)}, f32[8,512]{1,0:T(8,128)S(1)}, bf16[2,1,32,2048]{3,2,1,0:T(8,128)(2,1)S(1)}, bf16[2,1,32,2048]{3,2,1,0:T(8,...) custom-call(s32[4]{0:T(128)S(1)} %pad_add_fusion.2.here_ref, ...), custom_call_target="tpu_custom_call" | custom-call | bytes 65536 | tf_op jit(solution)/shard_map/pallas_call | solution.py:587
  281.0 2.4 collective-permute-done.39
  286.2 9.2 %shard_map.199 = (f32[512,1024]{1,0:T(8,128)}, bf16[128,1024]{1,0:T(8,128)(2,1)S(1)}, bf16[128,1024]{1,0:T(8,128)(2,1)S(1)}, bf16[128,1024]{1,0:T(8,128)(2,1)S(1...) custom-call(bf16[1024,1536]{1,0:T(8,128)(2,1)} %get-tuple-element.311.dp_ref, bf16[1024,1536]{1,0:T(8,128)(2,1)} %bitcast.161, ...), custom_call_target="tpu_custom_call" | custom-call | bytes 65536 | tf_op jit(solution)/shard_map/pallas_call | solution.py:335
  295.5 7.1 %shard_map.198 = (f32[512,1024]{1,0:T(8,128)}, bf16[128,1024]{1,0:T(8,128)(2,1)S(1)}, bf16[128,1024]{1,0:T(8,128)(2,1)S(1)}, bf16[128,1024]{1,0:T(8,128)(2,1)S(1)}, bf16[128,1024]{1,0:T(8,128)(2,1)S(1)}) custom-call(bf16[1024,1152]{1,0:T(8,128)(2,1)} %get-tuple-element.301.refs_0_.left_ref, bf16[1152,1024]{1,0:T(8,128)(2,1)} %all-gather.5.cloned.1.call-done.refs_3_.weight_ref), custom_call_target="tpu_custom_call" | custom-call | bytes 65536 | tf_op jit(solution)/shard_map/pallas_call | solution.py:305
  307.4 2.3 add_convert_fusion.5
  311.3 2.9 collective-permute-done.51
  318.5 4.8 %shard_map.200 = (bf16[512,1024]{1,0:T(8,128)(2,1)}, f32[1,1024]{1,0:T(1,128)}) custom-call(f32[512,1024]{1,0:T(8,128)} %get-tuple-element.332.refs_0_, bf16[128,1024]{1,0:T(8,128)(2,1)S(1)} %collective-permute-done.46.refs_1_, bf16[128,1024]{1,0:T(8,128)(2,1)S(1)} %collective-permute-done.47.refs_2_, bf16[128,1024]{1,0:T(8,128)(2,1)S(1)} %collective-permute-done.48.refs_3_, ...), custom_call_target="tpu_custom_call" | custom-call | bytes 65536 | tf_op jit(solution)/shard_map/pallas_call | solution.py:646
  323.4 9.7 %collective-permute-done.44 = bf16[2,3,32,2048]{3,2,1,0:T(8,128)(2,1)} collective-permute-done((bf16[2,3,32,2048]{3,2,1,0:T(8,128)(2,1)}, bf16[2,3,32,2048]{3,2,1,0:T(8,128)(2,1)}, u32[]{:S(2)}, u32[]{:S(2)}) %collective-permute-start.44) | collective-permute-done | bytes 786464 | tf_op jit(solution)/shard_map/ppermute | solution.py:28
  335.0 1.7 add_convert_fusion.4
  338.5 3.0 collective-permute-start.57
  342.6 16.4 %reduce-scatter.2.cloned.1.call-done = bf16[128,2304]{1,0:T(8,128)(2,1)} async-done(((bf16[1024,2304]{1,0:T(8,128)(2,1)}), bf16[128,2304]{1,0:T(8,128)(2,1)}) %reduce-scatter.2.cloned.1.call-update) | async-done | bytes 589840 | tf_op jit(solution)/shard_map/reduce_scatter | solution.py:841
  362.1 3.9 %add_convert_fusion.1 = bf16[512,1024]{1,0:T(8,128)(2,1)} fusion(f32[512,1024]{1,0:T(8,128)S(1)} %copy-done.8, bf16[512,1024]{1,0:T(8,128)(2,1)} %collective-permute-done.39, f32[512,1024]{1,0:T(8,128)} %get-tuple-element.302, bf16[128,1024]{1,0:T(8,128)(2,1)} %copy-done.39, bf16[128,1024]{1,0:T(8,128)(2,1)} %copy-done.38, bf16[128,1024]{1,0:T(8,128)(2,1)} %copy-done.37, ...), kind=kLoop, calls=%fused_computation.2 | loop fusion | flops 6815744 | bytes 7340032 | tf_op jit(solution)/shard_map/convert_element_type | solution.py:948
  366.0 6.4 %collective-permute-done.58 = bf16[2,32,2176]{2,1,0:T(8,128)(2,1)} collective-permute-done((bf16[2,32,2176]{2,1,0:T(8,128)(2,1)}, bf16[2,32,2176]{2,1,0:T(8,128)(2,1)}, u32[]{:S(2)}, u32[]{:S(2)}) %collective-permute-start.58) | collective-permute-done | bytes 278560 | tf_op jit(solution)/shard_map/ppermute | solution.py:28
  (320 shorter events, 84.4 us)
Async XLA Ops:
  7.2 124.2 %all-gather.3.cloned.1.call-start = ((), (), s32[]{:S(2)}) async-start(), calls=%async_computation.1 | async-start | bytes 5308416 | tf_op jit(solution)/shard_map/all_gather | solution.py:750
  16.3 12.0 %collective-permute-start.3 = (bf16[2,32,2176]{2,1,0:T(8,128)(2,1)S(1)}, bf16[2,32,2176]{2,1,0:T(8,128)(2,1)S(1)}, u32[]{:S(2)}, u32[]{:S(2)}) collective-permute-start(bf16[2,32,2176]{2,1,0:T(8,128)(2,1)S(1)} %pad_maximum_fusion.7), channel_id=1, source_target_pairs={{0,2},{2,4},{4,6},{6,0},{1,3},{3,5},{5,7},{7,1},{8,10},{10,12},{12... | collective-permute-start | bytes 835592 | tf_op jit(solution)/shard_map/ppermute | solution.py:28
  28.3 12.8 %collective-permute-start.4 = (bf16[2,32,2176]{2,1,0:T(8,128)(2,1)S(1)}, bf16[2,32,2176]{2,1,0:T(8,128)(2,1)S(1)}, u32[]{:S(2)}, u32[]{:S(2)}) collective-permute-start(bf16[2,32,2176]{2,1,0:T(8,128)(2,1)S(1)} %pad_maximum_fusion.7), channel_id=1, source_target_pairs={{0,6},{2,0},{4,2},{6,4},{1,7},{3,1},{5,3},{7,5},{8,14},{10,8},{12,... | collective-permute-start | bytes 835592 | tf_op jit(solution)/shard_map/ppermute | solution.py:28
  30.0 17.2 %collective-permute-start.5 = (bf16[2,32,2176]{2,1,0:T(8,128)(2,1)S(1)}, bf16[2,32,2176]{2,1,0:T(8,128)(2,1)S(1)}, u32[]{:S(2)}, u32[]{:S(2)}) collective-permute-start(bf16[2,32,2176]{2,1,0:T(8,128)(2,1)S(1)} %pad_maximum_fusion.7), channel_id=1, source_target_pairs={{0,4},{2,6},{4,0},{6,2},{1,5},{3,7},{5,1},{7,3},{8,12},{10,14},{12... | collective-permute-start | bytes 835592 | tf_op jit(solution)/shard_map/ppermute | solution.py:28
  30.1 10.0 %collective-permute-start.8 = (bf16[2,32,2304]{2,1,0:T(8,128)(2,1)S(1)}, bf16[2,32,2304]{2,1,0:T(8,128)(2,1)S(1)}, u32[]{:S(2)}, u32[]{:S(2)}) collective-permute-start(bf16[2,32,2304]{2,1,0:T(8,128)(2,1)S(1)} %fusion.1), channel_id=1, source_target_pairs={{0,16},{16,0},{1,17},{17,1},{2,18},{18,2},{3,19},{19,3},{4,20},{20... | collective-permute-start | bytes 884744 | tf_op jit(solution)/shard_map/ppermute | solution.py:28
  31.8 15.5 %collective-permute-start.6 = (bf16[2,2,32,2176]{3,2,1,0:T(8,128)(2,1)S(1)}, bf16[2,2,32,2176]{3,2,1,0:T(8,128)(2,1)S(1)}, u32[]{:S(2)}, u32[]{:S(2)}) collective-permute-start(bf16[2,2,32,2176]{3,2,1,0:T(8,128)(2,1)S(1)} %pad_maximum_fusion.3.refs_0_), channel_id=1, source_target_pairs={{0,1},{1,0},{2,3},{3,2},{4,5},{5,4},{6,7},{7,6},{8,9},{9,8},{10,11... | collective-permute-start | bytes 1671176 | tf_op jit(solution)/shard_map/ppermute | solution.py:28
  33.4 16.7 %collective-permute-start.7 = (bf16[2,2,32,2176]{3,2,1,0:T(8,128)(2,1)S(1)}, bf16[2,2,32,2176]{3,2,1,0:T(8,128)(2,1)S(1)}, u32[]{:S(2)}, u32[]{:S(2)}) collective-permute-start(bf16[2,2,32,2176]{3,2,1,0:T(8,128)(2,1)S(1)} %pad_maximum_fusion.3.refs_0_), channel_id=1, source_target_pairs={{0,16},{16,0},{1,17},{17,1},{2,18},{18,2},{3,19},{19,3},{4,20},{20... | collective-permute-start | bytes 1671176 | tf_op jit(solution)/shard_map/ppermute | solution.py:28
  50.9 133.7 %all-gather.5.cloned.1.call-start = ((), (), s32[]{:S(2)}) async-start(), calls=%async_computation.2 | async-start | bytes 2654208 | tf_op jit(solution)/shard_map/all_gather | solution.py:758
  51.1 12.7 %collective-permute-start.9 = (bf16[2,2,32,2176]{3,2,1,0:T(8,128)(2,1)S(1)}, bf16[2,2,32,2176]{3,2,1,0:T(8,128)(2,1)S(1)}, u32[]{:S(2)}, u32[]{:S(2)}) collective-permute-start(bf16[2,2,32,2176]{3,2,1,0:T(8,128)(2,1)S(1)} %pad_maximum_fusion.4.refs_2_), channel_id=1, source_target_pairs={{0,16},{16,0},{1,17},{17,1},{2,18},{18,2},{3,19},{19,3},{4,20},{20... | collective-permute-start | bytes 1671176 | tf_op jit(solution)/shard_map/ppermute | solution.py:28
  52.6 17.8 %collective-permute-start.10 = (bf16[2,2,32,2176]{3,2,1,0:T(8,128)(2,1)S(1)}, bf16[2,2,32,2176]{3,2,1,0:T(8,128)(2,1)S(1)}, u32[]{:S(2)}, u32[]{:S(2)}) collective-permute-start(bf16[2,2,32,2176]{3,2,1,0:T(8,128)(2,1)S(1)} %pad_maximum_fusion.4.refs_2_), channel_id=1, source_target_pairs={{0,1},{1,0},{2,3},{3,2},{4,5},{5,4},{6,7},{7,6},{8,9},{9,8},{10,11... | collective-permute-start | bytes 1671176 | tf_op jit(solution)/shard_map/ppermute | solution.py:28
  70.5 6.7 %collective-permute-start.13 = (bf16[512,1024]{1,0:T(8,128)(2,1)S(1)}, bf16[512,1024]{1,0:T(8,128)(2,1)S(1)}, u32[]{:S(2)}, u32[]{:S(2)}) collective-permute-start(bf16[512,1024]{1,0:T(8,128)(2,1)S(1)} %copy-done.11), channel_id=1, source_target_pairs={{0,8},{8,0},{1,9},{9,1},{2,10},{10,2},{3,11},{11,3},{4,12},{12,4},... | collective-permute-start | bytes 3145736 | tf_op jit(solution)/shard_map/ppermute | solution.py:28
  71.3 18.8 %collective-permute-start.14 = (bf16[512,1024]{1,0:T(8,128)(2,1)S(1)}, bf16[512,1024]{1,0:T(8,128)(2,1)}, u32[]{:S(2)}, u32[]{:S(2)}) collective-permute-start(bf16[512,1024]{1,0:T(8,128)(2,1)S(1)} %copy-done.10), channel_id=1, source_target_pairs={{0,8},{8,0},{1,9},{9,1},{2,10},{10,2},{3,11},{11,3},{4,12},{12,4},... | collective-permute-start | bytes 3145736 | tf_op jit(solution)/shard_map/ppermute | solution.py:28
  73.3 15.0 %collective-permute-start.11 = (bf16[2,2,32,2176]{3,2,1,0:T(8,128)(2,1)}, bf16[2,2,32,2176]{3,2,1,0:T(8,128)(2,1)}, u32[]{:S(2)}, u32[]{:S(2)}) collective-permute-start(bf16[2,2,32,2176]{3,2,1,0:T(8,128)(2,1)} %copy-done.24), channel_id=1, source_target_pairs={{0,16},{16,0},{1,17},{17,1},{2,18},{18,2},{3,19},{19,3},{4,20},{20... | collective-permute-start | bytes 1671176 | tf_op jit(solution)/shard_map/ppermute | solution.py:28
  73.4 16.7 %collective-permute-start.12 = (bf16[2,2,32,2176]{3,2,1,0:T(8,128)(2,1)}, bf16[2,2,32,2176]{3,2,1,0:T(8,128)(2,1)}, u32[]{:S(2)}, u32[]{:S(2)}) collective-permute-start(bf16[2,2,32,2176]{3,2,1,0:T(8,128)(2,1)} %copy-done.26), channel_id=1, source_target_pairs={{0,1},{1,0},{2,3},{3,2},{4,5},{5,4},{6,7},{7,6},{8,9},{9,8},{10,11... | collective-permute-start | bytes 1671176 | tf_op jit(solution)/shard_map/ppermute | solution.py:28
  94.7 24.0 %collective-permute-start.17 = (bf16[512,1024]{1,0:T(8,128)(2,1)}, bf16[512,1024]{1,0:T(8,128)(2,1)}, u32[]{:S(2)}, u32[]{:S(2)}) collective-permute-start(bf16[512,1024]{1,0:T(8,128)(2,1)} %refs_6_), channel_id=1, source_target_pairs={{0,16},{16,0},{1,17},{17,1},{2,18},{18,2},{3,19},{19,3},{4,20},{20... | collective-permute-start | bytes 3145736 | tf_op jit(solution)/shard_map/ppermute | solution.py:28
  98.9 5.8 %collective-permute-start.16 = (f32[2,2,512]{2,1,0:T(2,128)S(1)}, f32[2,2,512]{2,1,0:T(2,128)S(1)}, u32[]{:S(2)}, u32[]{:S(2)}) collective-permute-start(f32[2,2,512]{2,1,0:T(2,128)S(1)} %reshape.229), channel_id=1, source_target_pairs={{0,1},{1,2},{2,3},{3,4},{4,5},{5,6},{6,7},{8,9},{9,10},{10,11},{11... | collective-permute-start | bytes 24584 | tf_op jit(solution)/shard_map/ppermute | solution.py:37
  118.7 240.2 %reduce-scatter.2.cloned.1.call-start = ((), (), s32[]{:S(2)}) async-start(), calls=%async_computation.3 | async-start | bytes 5308416 | tf_op jit(solution)/shard_map/reduce_scatter | solution.py:841
  128.0 26.2 %collective-permute-start.20 = (bf16[512,1024]{1,0:T(8,128)(2,1)S(1)}, bf16[512,1024]{1,0:T(8,128)(2,1)}, u32[]{:S(2)}, u32[]{:S(2)}) collective-permute-start(bf16[512,1024]{1,0:T(8,128)(2,1)S(1)} %multiply_convert_fusion.refs_0_), channel_id=1, source_target_pairs={{0,16},{16,0},{1,17},{17,1},{2,18},{18,2},{3,19},{19,3},{4,20},{20... | collective-permute-start | bytes 3145736 | tf_op jit(solution)/shard_map/ppermute | solution.py:28
  154.3 15.5 %collective-permute-start.22 = (bf16[512,1024]{1,0:T(8,128)(2,1)}, bf16[512,1024]{1,0:T(8,128)(2,1)S(1)}, u32[]{:S(2)}, u32[]{:S(2)}) collective-permute-start(bf16[512,1024]{1,0:T(8,128)(2,1)} %collective-permute-done.17.refs_1_.refs_0_), channel_id=1, source_target_pairs={{0,8},{8,0},{1,9},{9,1},{2,10},{10,2},{3,11},{11,3},{4,12},{12,4},... | collective-permute-start | bytes 3145736 | tf_op jit(solution)/shard_map/ppermute | solution.py:28
  180.7 28.3 %collective-permute-start.23 = (bf16[1,4,144,1024]{3,2,1,0:T(8,128)(2,1)}, bf16[1,4,144,1024]{3,2,1,0:T(8,128)(2,1)S(1)}, u32[]{:S(2)}, u32[]{:S(2)}) collective-permute-start(bf16[1,4,144,1024]{3,2,1,0:T(8,128)(2,1)} %get-tuple-element.376), channel_id=1, source_target_pairs={{0,1},{1,0},{2,3},{3,2},{4,5},{5,4},{6,7},{7,6},{8,9},{9,8},{10,11... | collective-permute-start | bytes 3538952 | tf_op jit(solution)/shard_map/ppermute | solution.py:28
  199.5 9.3 %collective-permute-start.24 = (bf16[256,1024]{1,0:T(8,128)(2,1)}, bf16[256,1024]{1,0:T(8,128)(2,1)S(1)}, u32[]{:S(2)}, u32[]{:S(2)}) collective-permute-start(bf16[256,1024]{1,0:T(8,128)(2,1)} %get-tuple-element.246), channel_id=1, source_target_pairs={{0,8},{8,0},{1,9},{9,1},{2,10},{10,2},{3,11},{11,3},{4,12},{12,4},... | collective-permute-start | bytes 1572872 | tf_op jit(solution)/shard_map/ppermute | solution.py:28
  199.6 9.3 %collective-permute-start.25 = (bf16[256,1024]{1,0:T(8,128)(2,1)}, bf16[256,1024]{1,0:T(8,128)(2,1)S(1)}, u32[]{:S(2)}, u32[]{:S(2)}) collective-permute-start(bf16[256,1024]{1,0:T(8,128)(2,1)} %get-tuple-element.247), channel_id=1, source_target_pairs={{0,8},{8,0},{1,9},{9,1},{2,10},{10,2},{3,11},{11,3},{4,12},{12,4},... | collective-permute-start | bytes 1572872 | tf_op jit(solution)/shard_map/ppermute | solution.py:28
  210.4 34.2 %collective-permute-start.26 = (bf16[512,1024]{1,0:T(8,128)(2,1)}, bf16[512,1024]{1,0:T(8,128)(2,1)}, u32[]{:S(2)}, u32[]{:S(2)}) collective-permute-start(bf16[512,1024]{1,0:T(8,128)(2,1)} %add_convert_fusion.3), channel_id=1, source_target_pairs={{0,16},{16,0},{1,17},{17,1},{2,18},{18,2},{3,19},{19,3},{4,20},{20... | collective-permute-start | bytes 3145736 | tf_op jit(solution)/shard_map/ppermute | solution.py:28
  212.4 32.2 %collective-permute-start.27 = (bf16[1,144,1024]{2,1,0:T(8,128)(2,1)S(1)}, bf16[1,144,1024]{2,1,0:T(8,128)(2,1)S(1)}, u32[]{:S(2)}, u32[]{:S(2)}) collective-permute-start(bf16[1,144,1024]{2,1,0:T(8,128)(2,1)S(1)} %get-tuple-element.380), channel_id=1, source_target_pairs={{0,2},{2,4},{4,6},{6,0},{1,3},{3,5},{5,7},{7,1},{8,10},{10,12},{12... | collective-permute-start | bytes 884744 | tf_op jit(solution)/shard_map/ppermute | solution.py:28
  213.9 30.8 %collective-permute-start.28 = (bf16[1,144,1024]{2,1,0:T(8,128)(2,1)S(1)}, bf16[1,144,1024]{2,1,0:T(8,128)(2,1)S(1)}, u32[]{:S(2)}, u32[]{:S(2)}) collective-permute-start(bf16[1,144,1024]{2,1,0:T(8,128)(2,1)S(1)} %get-tuple-element.379), channel_id=1, source_target_pairs={{0,6},{2,0},{4,2},{6,4},{1,7},{3,1},{5,3},{7,5},{8,14},{10,8},{12,... | collective-permute-start | bytes 884744 | tf_op jit(solution)/shard_map/ppermute | solution.py:28
  216.5 28.2 %collective-permute-start.29 = (bf16[1,144,1024]{2,1,0:T(8,128)(2,1)S(1)}, bf16[1,144,1024]{2,1,0:T(8,128)(2,1)S(1)}, u32[]{:S(2)}, u32[]{:S(2)}) collective-permute-start(bf16[1,144,1024]{2,1,0:T(8,128)(2,1)S(1)} %get-tuple-element.378), channel_id=1, source_target_pairs={{0,4},{2,6},{4,0},{6,2},{1,5},{3,7},{5,1},{7,3},{8,12},{10,14},{12... | collective-permute-start | bytes 884744 | tf_op jit(solution)/shard_map/ppermute | solution.py:28
  245.5 4.2 %collective-permute-start.30 = (bf16[256,1024]{1,0:T(8,128)(2,1)}, bf16[256,1024]{1,0:T(8,128)(2,1)S(1)}, u32[]{:S(2)}, u32[]{:S(2)}) collective-permute-start(bf16[256,1024]{1,0:T(8,128)(2,1)} %get-tuple-element.268), channel_id=1, source_target_pairs={{0,8},{8,0},{1,9},{9,1},{2,10},{10,2},{3,11},{11,3},{4,12},{12,4},... | collective-permute-start | bytes 1572872 | tf_op jit(solution)/shard_map/ppermute | solution.py:28
  256.1 10.1 %collective-permute-start.36 = (bf16[512,1024]{1,0:T(8,128)(2,1)}, bf16[512,1024]{1,0:T(8,128)(2,1)}, u32[]{:S(2)}, u32[]{:S(2)}) collective-permute-start(bf16[512,1024]{1,0:T(8,128)(2,1)} %get-tuple-element.280.refs_0_), channel_id=1, source_target_pairs={{0,8},{8,0},{1,9},{9,1},{2,10},{10,2},{3,11},{11,3},{4,12},{12,4},... | collective-permute-start | bytes 3145736 | tf_op jit(solution)/shard_map/ppermute | solution.py:28
  257.7 25.7 %collective-permute-start.39 = (bf16[512,1024]{1,0:T(8,128)(2,1)}, bf16[512,1024]{1,0:T(8,128)(2,1)}, u32[]{:S(2)}, u32[]{:S(2)}) collective-permute-start(bf16[512,1024]{1,0:T(8,128)(2,1)} %add_convert_fusion.2), channel_id=1, source_target_pairs={{0,16},{16,0},{1,17},{17,1},{2,18},{18,2},{3,19},{19,3},{4,20},{20... | collective-permute-start | bytes 3145736 | tf_op jit(solution)/shard_map/ppermute | solution.py:28
  260.6 5.5 %collective-permute-start.38 = (f32[2,2,512]{2,1,0:T(2,128)S(1)}, f32[2,2,512]{2,1,0:T(2,128)S(1)}, u32[]{:S(2)}, u32[]{:S(2)}) collective-permute-start(f32[2,2,512]{2,1,0:T(2,128)S(1)} %reshape.240), channel_id=1, source_target_pairs={{1,0},{2,1},{3,2},{4,3},{5,4},{6,5},{7,6},{9,8},{10,9},{11,10},{12... | collective-permute-start | bytes 24584 | tf_op jit(solution)/shard_map/ppermute | solution.py:37
  283.4 20.3 %collective-permute-start.42 = (bf16[2,3,32,2048]{3,2,1,0:T(8,128)(2,1)}, bf16[2,3,32,2048]{3,2,1,0:T(8,128)(2,1)}, u32[]{:S(2)}, u32[]{:S(2)}) collective-permute-start(bf16[2,3,32,2048]{3,2,1,0:T(8,128)(2,1)} %get-tuple-element.305), channel_id=1, source_target_pairs={{0,16},{16,0},{1,17},{17,1},{2,18},{18,2},{3,19},{19,3},{4,20},{20... | collective-permute-start | bytes 2359304 | tf_op jit(solution)/shard_map/ppermute | solution.py:28
  284.2 18.5 %collective-permute-start.40 = (bf16[2,1,32,2048]{3,2,1,0:T(8,128)(2,1)S(1)}, bf16[2,1,32,2048]{3,2,1,0:T(8,128)(2,1)}, u32[]{:S(2)}, u32[]{:S(2)}) collective-permute-start(bf16[2,1,32,2048]{3,2,1,0:T(8,128)(2,1)S(1)} %get-tuple-element.303), channel_id=1, source_target_pairs={{0,1},{1,0},{2,3},{3,2},{4,5},{5,4},{6,7},{7,6},{8,9},{9,8},{10,11... | collective-permute-start | bytes 786440 | tf_op jit(solution)/shard_map/ppermute | solution.py:28
  285.6 18.1 %collective-permute-start.41 = (bf16[2,1,32,2048]{3,2,1,0:T(8,128)(2,1)S(1)}, bf16[2,1,32,2048]{3,2,1,0:T(8,128)(2,1)}, u32[]{:S(2)}, u32[]{:S(2)}) collective-permute-start(bf16[2,1,32,2048]{3,2,1,0:T(8,128)(2,1)S(1)} %get-tuple-element.304), channel_id=1, source_target_pairs={{0,1},{1,0},{2,3},{3,2},{4,5},{5,4},{6,7},{7,6},{8,9},{9,8},{10,11... | collective-permute-start | bytes 786440 | tf_op jit(solution)/shard_map/ppermute | solution.py:28
  304.8 10.8 %collective-permute-start.43 = (bf16[2,1,32,2048]{3,2,1,0:T(8,128)(2,1)S(1)}, bf16[2,1,32,2048]{3,2,1,0:T(8,128)(2,1)S(1)}, u32[]{:S(2)}, u32[]{:S(2)}) collective-permute-start(bf16[2,1,32,2048]{3,2,1,0:T(8,128)(2,1)S(1)} %add_convert_fusion.7), channel_id=1, source_target_pairs={{0,16},{16,0},{1,17},{17,1},{2,18},{18,2},{3,19},{19,3},{4,20},{20... | collective-permute-start | bytes 786440 | tf_op jit(solution)/shard_map/ppermute | solution.py:28
  306.2 9.4 %collective-permute-start.46 = (bf16[128,1024]{1,0:T(8,128)(2,1)S(1)}, bf16[128,1024]{1,0:T(8,128)(2,1)S(1)}, u32[]{:S(2)}, u32[]{:S(2)}) collective-permute-start(bf16[128,1024]{1,0:T(8,128)(2,1)S(1)} %get-tuple-element.333), channel_id=1, source_target_pairs={{0,8},{8,0},{1,9},{9,1},{2,10},{10,2},{3,11},{11,3},{4,12},{12,4},... | collective-permute-start | bytes 786440 | tf_op jit(solution)/shard_map/ppermute | solution.py:28
  306.4 9.7 %collective-permute-start.47 = (bf16[128,1024]{1,0:T(8,128)(2,1)S(1)}, bf16[128,1024]{1,0:T(8,128)(2,1)S(1)}, u32[]{:S(2)}, u32[]{:S(2)}) collective-permute-start(bf16[128,1024]{1,0:T(8,128)(2,1)S(1)} %get-tuple-element.334), channel_id=1, source_target_pairs={{0,8},{8,0},{1,9},{9,1},{2,10},{10,2},{3,11},{11,3},{4,12},{12,4},... | collective-permute-start | bytes 786440 | tf_op jit(solution)/shard_map/ppermute | solution.py:28
  306.7 7.6 %collective-permute-start.51 = (f32[5,1024]{1,0:T(8,128)S(1)}, f32[5,1024]{1,0:T(8,128)S(1)}, u32[]{:S(2)}, u32[]{:S(2)}) collective-permute-start(f32[5,1024]{1,0:T(8,128)S(1)} %add.240), channel_id=1, source_target_pairs={{0,16},{16,0},{1,17},{17,1},{2,18},{18,2},{3,19},{19,3},{4,20},{20... | collective-permute-start | bytes 61448 | tf_op jit(solution)/shard_map/ppermute | solution.py:28
  309.8 23.3 %collective-permute-start.44 = (bf16[2,3,32,2048]{3,2,1,0:T(8,128)(2,1)}, bf16[2,3,32,2048]{3,2,1,0:T(8,128)(2,1)}, u32[]{:S(2)}, u32[]{:S(2)}) collective-permute-start(bf16[2,3,32,2048]{3,2,1,0:T(8,128)(2,1)} %add_convert_fusion.5), channel_id=1, source_target_pairs={{0,1},{1,0},{2,3},{3,2},{4,5},{5,4},{6,7},{7,6},{8,9},{9,8},{10,11... | collective-permute-start | bytes 2359304 | tf_op jit(solution)/shard_map/ppermute | solution.py:28
  314.3 19.6 %collective-permute-start.45 = (bf16[2,3,32,2048]{3,2,1,0:T(8,128)(2,1)}, bf16[2,3,32,2048]{3,2,1,0:T(8,128)(2,1)}, u32[]{:S(2)}, u32[]{:S(2)}) collective-permute-start(bf16[2,3,32,2048]{3,2,1,0:T(8,128)(2,1)} %get-tuple-element.329), channel_id=1, source_target_pairs={{0,16},{16,0},{1,17},{17,1},{2,18},{18,2},{3,19},{19,3},{4,20},{20... | collective-permute-start | bytes 2359304 | tf_op jit(solution)/shard_map/ppermute | solution.py:28
  317.4 5.9 %collective-permute-start.53 = (bf16[128,1024]{1,0:T(8,128)(2,1)S(1)}, bf16[128,1024]{1,0:T(8,128)(2,1)S(1)}, u32[]{:S(2)}, u32[]{:S(2)}) collective-permute-start(bf16[128,1024]{1,0:T(8,128)(2,1)S(1)} %get-tuple-element.341), channel_id=1, source_target_pairs={{0,8},{8,0},{1,9},{9,1},{2,10},{10,2},{3,11},{11,3},{4,12},{12,4},... | collective-permute-start | bytes 786440 | tf_op jit(solution)/shard_map/ppermute | solution.py:28
  317.9 5.4 %collective-permute-start.54 = (bf16[128,1024]{1,0:T(8,128)(2,1)S(1)}, bf16[128,1024]{1,0:T(8,128)(2,1)S(1)}, u32[]{:S(2)}, u32[]{:S(2)}) collective-permute-start(bf16[128,1024]{1,0:T(8,128)(2,1)S(1)} %get-tuple-element.342), channel_id=1, source_target_pairs={{0,8},{8,0},{1,9},{9,1},{2,10},{10,2},{3,11},{11,3},{4,12},{12,4},... | collective-permute-start | bytes 786440 | tf_op jit(solution)/shard_map/ppermute | solution.py:28
  318.0 5.3 %collective-permute-start.55 = (bf16[128,1024]{1,0:T(8,128)(2,1)S(1)}, bf16[128,1024]{1,0:T(8,128)(2,1)S(1)}, u32[]{:S(2)}, u32[]{:S(2)}) collective-permute-start(bf16[128,1024]{1,0:T(8,128)(2,1)S(1)} %get-tuple-element.343), channel_id=1, source_target_pairs={{0,8},{8,0},{1,9},{9,1},{2,10},{10,2},{3,11},{11,3},{4,12},{12,4},... | collective-permute-start | bytes 786440 | tf_op jit(solution)/shard_map/ppermute | solution.py:28
  337.7 24.1 %collective-permute-start.56 = (bf16[2,32,2176]{2,1,0:T(8,128)(2,1)}, bf16[2,32,2176]{2,1,0:T(8,128)(2,1)S(1)}, u32[]{:S(2)}, u32[]{:S(2)}) collective-permute-start(bf16[2,32,2176]{2,1,0:T(8,128)(2,1)} %get-tuple-element.385), channel_id=1, source_target_pairs={{0,2},{2,4},{4,6},{6,0},{1,3},{3,5},{5,7},{7,1},{8,10},{10,12},{12... | collective-permute-start | bytes 835592 | tf_op jit(solution)/shard_map/ppermute | solution.py:28
  338.5 27.5 %collective-permute-start.57 = (bf16[2,32,2176]{2,1,0:T(8,128)(2,1)}, bf16[2,32,2176]{2,1,0:T(8,128)(2,1)S(1)}, u32[]{:S(2)}, u32[]{:S(2)}) collective-permute-start(bf16[2,32,2176]{2,1,0:T(8,128)(2,1)} %get-tuple-element.384), channel_id=1, source_target_pairs={{0,6},{2,0},{4,2},{6,4},{1,7},{3,1},{5,3},{7,5},{8,14},{10,8},{12,... | collective-permute-start | bytes 835592 | tf_op jit(solution)/shard_map/ppermute | solution.py:28
  341.5 30.9 %collective-permute-start.58 = (bf16[2,32,2176]{2,1,0:T(8,128)(2,1)}, bf16[2,32,2176]{2,1,0:T(8,128)(2,1)}, u32[]{:S(2)}, u32[]{:S(2)}) collective-permute-start(bf16[2,32,2176]{2,1,0:T(8,128)(2,1)} %get-tuple-element.383), channel_id=1, source_target_pairs={{0,4},{2,6},{4,0},{6,2},{1,5},{3,7},{5,1},{7,3},{8,12},{10,14},{12... | collective-permute-start | bytes 835592 | tf_op jit(solution)/shard_map/ppermute | solution.py:28
  360.1 12.3 %collective-permute-start.59 = (bf16[32,2304]{1,0:T(8,128)(2,1)S(1)}, bf16[32,2304]{1,0:T(8,128)(2,1)S(1)}, u32[]{:S(2)}, u32[]{:S(2)}) collective-permute-start(bf16[32,2304]{1,0:T(8,128)(2,1)S(1)} %get-tuple-element.390), channel_id=1, source_target_pairs={{0,8},{8,0},{16,24},{24,16},{1,9},{9,1},{17,25},{25,17},{2,10},{10... | collective-permute-start | bytes 442376 | tf_op jit(solution)/shard_map/ppermute | solution.py:923
  360.2 12.2 %collective-permute-start.60 = (bf16[32,2304]{1,0:T(8,128)(2,1)S(1)}, bf16[32,2304]{1,0:T(8,128)(2,1)S(1)}, u32[]{:S(2)}, u32[]{:S(2)}) collective-permute-start(bf16[32,2304]{1,0:T(8,128)(2,1)S(1)} %get-tuple-element.389), channel_id=1, source_target_pairs={{0,16},{8,24},{16,0},{24,8},{1,17},{9,25},{17,1},{25,9},{2,18},{10... | collective-permute-start | bytes 442376 | tf_op jit(solution)/shard_map/ppermute | solution.py:923
  361.8 10.6 %collective-permute-start.61 = (bf16[32,2304]{1,0:T(8,128)(2,1)S(1)}, bf16[32,2304]{1,0:T(8,128)(2,1)S(1)}, u32[]{:S(2)}, u32[]{:S(2)}) collective-permute-start(bf16[32,2304]{1,0:T(8,128)(2,1)S(1)} %get-tuple-element.388), channel_id=1, source_target_pairs={{0,24},{8,16},{16,8},{24,0},{1,25},{9,17},{17,9},{25,1},{2,26},{10... | collective-permute-start | bytes 442376 | tf_op jit(solution)/shard_map/ppermute | solution.py:923
  (66 other events, 500.1 us)
Sparse Core Ops, SparseCore 0:
  51.1 80.3 all-gather.2
  134.2 50.3 all-gather.4
  244.9 114.0 reduce-scatter.1
